TPU v7x, 128 devices: a whole 4x4x4 slice. The times are simulated.
128 devices in a mesh: rows: 4 (over y_hi, core), loop: 32 (over z, x, y_lo).
Axes of the slice: x: 4, y: 4 (y_hi: 2, y_lo: 2; y = y_hi * 2 + y_lo), z: 4, core: 2. Of those that a mesh axis runs over, the one named last changes fastest.
Arguments:
- delta_weight_matrix: float32 [98304, 4096], P('rows', 'loop'), may hold values from -18 to 18
- offsets: int32 [2, 4], replicated, may hold values from 0 to 63, as said below
Outputs:
- rotated: float32 [98304, 4096], P('rows', 'loop')
Inputs may be any that keep to these rules, and one draw needn't show every extreme that they name: The 4 offsets of each step are distinct.
All inputs are finite; a program needn't handle non-finite values.
Results may differ from a plain program's by a relative error of at most 0.0003.
Values sent between devices are 32-bit elements; how exact they have to be, the bound alone decides.
No kernel may reach another device: no remote copies, remote signals or barrier semaphores. Data moves between devices by JAX's collectives and lax.ppermute only.
A program may use at most 128 MiB of HBM per device.

v0:
```python
import jax
import jax.numpy as jnp
from jax import lax
from jax.sharding import PartitionSpec as P

INNER_ROUNDS = 4


PRECISION_HIGH = lax.Precision.HIGHEST


def passed_along(shard, axis, by):
    devices = lax.axis_size(axis)
    pairs = [(i, i + by) for i in range(devices) if 0 <= i + by < devices]
    return lax.ppermute(shard, axis, pairs)


def paired_gram_matrix(left, right):
    return lax.dot_general(
        left,
        right,
        (((0,), (0,)), ((), ())),
        precision=PRECISION_HIGH,
        preferred_element_type=jnp.float32,
    )


def jacobi_rotations(gram_matrix, circle_shifts):
    block_width = gram_matrix.shape[0]
    half = block_width // 2
    right_vectors = jnp.eye(block_width, dtype=gram_matrix.dtype)
    column = jnp.arange(half, dtype=jnp.int32)
    for which in range(INNER_ROUNDS):
        partner = half + (column + circle_shifts[which]) % half
        g_first = gram_matrix[column, column]
        g_second = gram_matrix[partner, partner]
        g_cross = gram_matrix[column, partner]
        spread = g_second - g_first
        sign_part = jnp.where(spread >= 0.0, 1.0, -1.0).astype(gram_matrix.dtype)
        tangent = (
            sign_part
            * 2.0
            * g_cross
            / (jnp.abs(spread) + jnp.sqrt(spread * spread + 4.0 * g_cross * g_cross))
        )
        cosine = 1.0 / jnp.sqrt(1.0 + tangent * tangent)
        sine = -tangent * cosine
        rotate_pair = jnp.zeros((block_width, block_width), gram_matrix.dtype)
        rotate_pair = rotate_pair.at[column, column].set(cosine).at[partner, partner].set(cosine)
        rotate_pair = rotate_pair.at[partner, column].set(sine).at[column, partner].set(-sine)
        gram_matrix = jnp.dot(
            rotate_pair.T,
            jnp.dot(gram_matrix, rotate_pair, precision=PRECISION_HIGH),
            precision=PRECISION_HIGH,
        )
        right_vectors = jnp.dot(right_vectors, rotate_pair, precision=PRECISION_HIGH)
    return (right_vectors, gram_matrix)


def reduced_gram_matrix(column_block):
    return lax.psum(paired_gram_matrix(column_block, column_block), "rows")


def body(delta_weight_matrix, offsets):
    half = delta_weight_matrix.shape[1] // 2
    place = lax.axis_index("loop")
    count = lax.axis_size("loop")
    first_place = place == 0
    last_place = place == count - 1
    right_vectors, rotated_blocks = jacobi_rotations(
        reduced_gram_matrix(delta_weight_matrix), offsets[0]
    )
    advanced_blocks = jnp.dot(
        delta_weight_matrix,
        right_vectors,
        precision=PRECISION_HIGH,
        preferred_element_type=jnp.float32,
    )
    first_half = advanced_blocks[:, :half]
    second_half = advanced_blocks[:, half:]
    arrived_up = passed_along(jnp.where(first_place, second_half, first_half), "loop", 1)
    arrived_down = passed_along(second_half, "loop", -1)
    new_first = jnp.where(first_place, first_half, arrived_up)
    new_second = jnp.where(last_place, first_half, arrived_down)
    shifted_blocks = jnp.concatenate([new_first, new_second], 1)
    updated_gram_matrix = reduced_gram_matrix(shifted_blocks)
    updated_right_vectors, discarded_value = jacobi_rotations(updated_gram_matrix, offsets[1])
    return jnp.dot(
        shifted_blocks,
        updated_right_vectors,
        precision=PRECISION_HIGH,
        preferred_element_type=jnp.float32,
    )


def solution(mesh):
    placed = (P("rows", "loop"), P())
    return jax.shard_map(
        body, mesh=mesh, in_specs=placed, out_specs=P("rows", "loop"), check_vma=False
    )
```

profile of v0, /device:TPU:0, one launch (start us, length us, event | category | flops | bytes accessed | tf_op | source)
XLA Modules:
  0.0 631.5 jit_solution(15431990333249425547)
XLA Ops:
  6.5 28.9 %fusion.116 = f32[128,128]{1,0:T(8,128)} fusion(f32[24576,128]{1,0:T(8,128)} %param.2), kind=kOutput, calls=%fused_computation.285 | convolution fusion | flops 4831838208 | bytes 12648448 | tf_op jit(solution)/shard_map/dot_general | solution.py:19
  43.9 33.9 %all-reduce.3.cloned.1.call-done = f32[128,128]{1,0:T(8,128)} async-done(((f32[128,128]{1,0:T(8,128)}), f32[128,128]{1,0:T(8,128)}) %all-reduce.3.cloned.1.call-update) | async-done | bytes 65552 | tf_op jit(solution)/shard_map/psum | solution.py:61
  79.5 1.7 gather_fusion
  81.2 1.7 gather_fusion.1
  83.0 4.0 scatter_fusion
  87.0 3.8 scatter_fusion.1
  90.8 3.8 scatter_fusion.2
  94.6 3.8 scatter_fusion.3
  102.3 3.8 scatter_fusion.4
  106.1 3.8 scatter_fusion.5
  109.9 3.8 scatter_fusion.6
  113.7 3.8 scatter_fusion.7
  120.4 3.8 scatter_fusion.8
  124.2 3.8 scatter_fusion.9
  128.0 3.8 scatter_fusion.10
  131.8 4.2 scatter_fusion.11
  139.3 3.8 scatter_fusion.12
  143.1 3.8 scatter_fusion.13
  146.9 3.8 scatter_fusion.14
  150.7 3.8 scatter_fusion.15
  154.7 17.3 %convolution_bitcast_fusion = f32[24576,128]{0,1:T(8,128)} fusion(f32[128,128]{1,0:T(8,128)S(1)} %fusion.125, f32[24576,128]{1,0:T(8,128)} %param.2), kind=kOutput, calls=%fused_computation.56 | convolution fusion | flops 4831838208 | bytes 25231360 | tf_op jit(solution)/shard_map/dot_general | solution.py:73
  171.9 10.4 %slice_select_fusion.2 = (f32[24576,64]{0,1:T(8,128)}, f32[24576,64]{0,1:T(8,128)}) fusion(f32[24576,128]{0,1:T(8,128)} %convolution_bitcast_fusion, pred[]{:T(512)S(6)} %eq.21), kind=kLoop, calls=%fused_computation.62 | loop fusion | flops 1572864 | bytes 25165824 | tf_op jit(solution)/shard_map/jit(_where)/select_n | solution.py:81
  182.3 5.2 collective-permute-start
  195.5 259.7 %collective-permute-done = f32[24576,64]{0,1:T(8,128)} collective-permute-done((f32[24576,64]{0,1:T(8,128)}, f32[24576,64]{0,1:T(8,128)}, u32[]{:S(2)}, u32[]{:S(2)}) %collective-permute-start) | collective-permute-done | bytes 6291488 | tf_op jit(solution)/shard_map/ppermute | solution.py:15
  455.2 5.0 collective-permute-done.1
  460.2 10.4 %slice_select_fusion.1 = (f32[24576,64]{0,1:T(8,128)}, f32[24576,64]{0,1:T(8,128)}) fusion(f32[24576,64]{0,1:T(8,128)} %collective-permute-done, f32[24576,128]{0,1:T(8,128)} %convolution_bitcast_fusion, pred[]{:T(512)S(6)} %eq.21, f32[24576,64]{0,1:T(8,128)} %collective-permute-done.1, pred[]{:T(512)S(6)} %eq.23), kind=kLoop, calls=%fused_computation.61 | loop fusion | flops 3145728 | bytes 31457282 | tf_op jit(solution)/shard_map/jit(_where)/select_n | solution.py:83
  470.6 14.8 %fusion.1 = f32[128,128]{1,0:T(8,128)} fusion(f32[24576,64]{0,1:T(8,128)} %get-tuple-element.30, f32[24576,64]{0,1:T(8,128)} %get-tuple-element.29), kind=kOutput, calls=%fused_computation.59 | convolution fusion | flops 4834983936 | bytes 12648448 | tf_op jit(solution)/shard_map/dot_general | solution.py:19
  486.0 37.7 %all-reduce.5.cloned.1.call-done = f32[128,128]{1,0:T(8,128)} async-done(((f32[128,128]{1,0:T(8,128)}), f32[128,128]{1,0:T(8,128)}) %all-reduce.5.cloned.1.call-update) | async-done | bytes 65552 | tf_op jit(solution)/shard_map/psum | solution.py:61
  523.7 1.7 gather_fusion.13
  525.4 1.7 gather_fusion.12
  527.1 1.7 gather_fusion.14
  528.8 3.8 scatter_fusion.16
  532.6 3.8 scatter_fusion.17
  536.4 3.8 scatter_fusion.18
  540.2 3.8 scatter_fusion.19
  548.0 3.8 scatter_fusion.20
  551.8 3.8 scatter_fusion.21
  555.5 3.8 scatter_fusion.22
  559.3 4.0 scatter_fusion.23
  566.2 3.8 scatter_fusion.24
  570.0 3.8 scatter_fusion.25
  573.8 3.8 scatter_fusion.26
  577.6 3.8 scatter_fusion.27
  584.8 3.8 scatter_fusion.28
  588.6 3.8 scatter_fusion.29
  592.3 3.8 scatter_fusion.30
  596.1 3.8 scatter_fusion.31
  600.1 24.1 %fusion = f32[24576,128]{1,0:T(8,128)} fusion(f32[128,128]{1,0:T(8,128)S(1)} %fusion.134, f32[24576,64]{0,1:T(8,128)} %get-tuple-element.30, f32[24576,64]{0,1:T(8,128)} %get-tuple-element.29), kind=kOutput, calls=%fused_computation.58 | convolution fusion | flops 4834983936 | bytes 25231360 | tf_op jit(solution)/shard_map/dot_general | solution.py:88
  (97 shorter events, 39.4 us)
Async XLA Ops:
  6.5 29.0 %copy-start = (s32[2,4]{1,0:T(2,128)S(1)}, s32[2,4]{1,0:T(2,128)}, u32[]{:S(2)}) copy-start(s32[2,4]{1,0:T(2,128)} %param.3) | copy-start | bytes 100
  6.5 71.3 %all-reduce.3.cloned.1.call-start = ((), (), s32[]{:S(2)}) async-start(), calls=%async_computation | async-start | bytes 131072 | tf_op jit(solution)/shard_map/psum | solution.py:61
  35.4 488.3 %all-reduce.5.cloned.1.call-start = ((), (), s32[]{:S(2)}) async-start(), calls=%async_computation.1 | async-start | bytes 131072 | tf_op jit(solution)/shard_map/psum | solution.py:61
  182.3 272.9 %collective-permute-start = (f32[24576,64]{0,1:T(8,128)}, f32[24576,64]{0,1:T(8,128)}, u32[]{:S(2)}, u32[]{:S(2)}) collective-permute-start(f32[24576,64]{0,1:T(8,128)} %get-tuple-element.31), channel_id=1, source_target_pairs={{0,1},{1,2},{2,3},{3,4},{4,5},{5,6},{6,7},{7,8},{8,9},{9,10},{10,1... | collective-permute-start | bytes 18874376 | tf_op jit(solution)/shard_map/ppermute | solution.py:15
  187.5 272.7 %collective-permute-start.1 = (f32[24576,64]{0,1:T(8,128)}, f32[24576,64]{0,1:T(8,128)}, u32[]{:S(2)}, u32[]{:S(2)}) collective-permute-start(f32[24576,64]{0,1:T(8,128)} %get-tuple-element.32), channel_id=1, source_target_pairs={{1,0},{2,1},{3,2},{4,3},{5,4},{6,5},{7,6},{8,7},{9,8},{10,9},{11,1... | collective-permute-start | bytes 18874376 | tf_op jit(solution)/shard_map/ppermute | solution.py:15
Sparse Core Ops, SparseCore 0:
  35.6 42.2 all-reduce.2
  485.5 38.1 all-reduce.4
where the time goes:
time: 642 us; the launch traced here: 632 us
  waiting for transfers between devices  336 us (52%)
  local copies, waits for them, and re-layouts  147 us (23%)
  matrix products  91.2 us (14%)
  other arithmetic  35.9 us (6%)
  between operations  14.5 us (2%)
  starting transfers between devices  6.48 us (1%)
    ppermute x2, waiting for transfers between devices, passed_along(): return lax.ppermute(shard, axis, pairs)  265 us
    psum x2, waiting for transfers between devices, reduced_gram_matrix(): return lax.psum(paired_gram_matrix(column_block, column_block), 'rows')  71.6 us
    scatter x16, local copies, waits for them, and re-layouts, jacobi_rotations(): rotate_pair.at[partner, column].set(sine).at[column, partner].set(-sine)  61.1 us
    scatter x16, local copies, waits for them, and re-layouts, jacobi_rotations(): rotate_pair.at[column, column].set(cosine).at[partner, partner].set(cosine)  60.7 us
    dot_general x2, matrix products, paired_gram_matrix(): lax.dot_general(left, right, (((0,), (0,)), ((), ())), precision=PRECISIO...  43.7 us
    dot_general x1, matrix products, body(): jnp.dot(shifted_blocks, updated_right_vectors, precision=PRECISION_HIGH,...  24.1 us
    dot_general x1, matrix products, body(): jnp.dot(delta_weight_matrix, right_vectors, precision=PRECISION_HIGH, pre...  17.3 us
  transfers between devices with their start and end apart: 4, of which 4 were waited for; matrix products, arithmetic and copies ran while one was open for 2% of the time, Pallas kernels for 0%

commit v1 on v0

v1 whole, which is shorter than its diff:
```python
import functools

import jax
import jax.numpy as jnp
from jax import lax
from jax.experimental import pallas as pl
from jax.experimental.pallas import tpu as pltpu
from jax.sharding import PartitionSpec as P

ROUNDS = 4
MIB = 1024 * 1024
F32 = jnp.float32
BF16 = jnp.bfloat16


def params(mib=58):
    return pltpu.CompilerParams(vmem_limit_bytes=mib * MIB)


def parts(x):
    high = x.astype(BF16)
    low = (x - high.astype(F32)).astype(BF16)
    return high, low


def gram_terms(x):
    high, low = parts(x)
    return lax.dot_general(
        high,
        jnp.concatenate([high, low], axis=1),
        (((0,), (0,)), ((), ())),
        preferred_element_type=F32,
    )


def gram_of_terms(terms):
    width = terms.shape[0]
    cross = terms[:, width:]
    return terms[:, :width] + cross + cross.T


def swapped(x, axis):
    return pltpu.roll(x, x.shape[axis] // 2, axis)


def times(x, weights):
    width = x.shape[1]
    both = jnp.dot(
        jnp.concatenate(parts(x), axis=1), weights, preferred_element_type=F32
    )
    return both[:, :width] + both[:, width:]


def left_lanes(shape):
    return lax.broadcasted_iota(jnp.int32, shape, 1) < shape[1] // 2


def gram_kernel(x_ref, gram_ref, terms_ref):
    step = pl.program_id(0)

    @pl.when(step == 0)
    def _():
        terms_ref[...] = jnp.zeros_like(terms_ref)

    terms_ref[...] += gram_terms(x_ref[...])

    @pl.when(step == pl.num_programs(0) - 1)
    def _():
        gram_ref[...] = gram_of_terms(terms_ref[...])


def local_gram(x, block):
    rows, width = x.shape
    return pl.pallas_call(
        gram_kernel,
        grid=(rows // block,),
        in_specs=[pl.BlockSpec((block, width), lambda i: (i, 0))],
        out_specs=pl.BlockSpec((width, width), lambda i: (0, 0)),
        out_shape=jax.ShapeDtypeStruct((width, width), F32),
        scratch_shapes=[pltpu.VMEM((width, 2 * width), F32)],
        compiler_params=params(),
    )(x)


def rotation_kernel(which, flags_ref, offsets_ref, one_ref, two_ref, a_ref, b_ref):
    gram = one_ref[...] + two_ref[...]
    width = gram.shape[0]
    half = width // 2
    row = lax.broadcasted_iota(jnp.int32, (width, width), 0)
    lane = lax.broadcasted_iota(jnp.int32, (width, width), 1)
    eye = row == lane
    is_first = lax.broadcasted_iota(jnp.int32, (1, width), 1) < half
    vectors = jnp.where(eye, 1.0, 0.0).astype(F32)
    dot = functools.partial(
        jnp.dot, precision=lax.Precision.HIGHEST, preferred_element_type=F32
    )
    for turn in range(ROUNDS):
        offset = offsets_ref[which, turn]
        above = lane + offset
        above = half + jnp.where(above >= half, above - half, above)
        below = lane - half - offset
        below = jnp.where(below < 0, below + half, below)
        pair = row == jnp.where(lane < half, above, below)
        own = jnp.sum(jnp.where(eye, gram, 0.0), axis=0, keepdims=True)
        own_col = jnp.sum(jnp.where(eye, gram, 0.0), axis=1, keepdims=True)
        other = jnp.sum(jnp.where(pair, own_col, 0.0), axis=0, keepdims=True)
        cross = jnp.sum(jnp.where(pair, gram, 0.0), axis=0, keepdims=True)
        spread = jnp.where(is_first, other - own, own - other)
        sign = jnp.where(spread >= 0.0, 1.0, -1.0)
        tangent = (
            sign
            * 2.0
            * cross
            / (jnp.abs(spread) + jnp.sqrt(spread * spread + 4.0 * cross * cross))
        )
        cosine = 1.0 / jnp.sqrt(1.0 + tangent * tangent)
        sine = tangent * cosine
        signed = jnp.where(is_first, -sine, sine)
        on_diagonal = jnp.where(eye, cosine, 0.0)
        off_diagonal = jnp.where(pair, signed, 0.0)
        turned = on_diagonal + off_diagonal
        vectors = dot(vectors, turned)
        if turn < ROUNDS - 1:
            gram = dot(on_diagonal - off_diagonal, dot(gram, turned))
    if which == 0:
        vectors = jnp.where(flags_ref[0] == 1, swapped(vectors, 1), vectors)
        other_vectors = swapped(vectors, 1)
    else:
        other_vectors = swapped(vectors, 0)
    for out_ref, v in ((a_ref, vectors), (b_ref, other_vectors)):
        both = jnp.concatenate(parts(v), axis=1)
        out_ref[...] = jnp.concatenate([both, both], axis=0)


def rotations(which, flags, offsets, one, two):
    width = one.shape[0]
    smem = pl.BlockSpec(memory_space=pltpu.SMEM)
    vmem = pl.BlockSpec(memory_space=pltpu.VMEM)
    return pl.pallas_call(
        functools.partial(rotation_kernel, which),
        in_specs=[smem, smem, vmem, vmem],
        out_specs=[vmem, vmem],
        out_shape=[jax.ShapeDtypeStruct((2 * width, 2 * width), BF16)] * 2,
        compiler_params=params(8),
    )(flags, offsets, one, two)


def first_product_kernel(
    early, flags_ref, x_ref, a_ref, b_ref, u1_ref, w1_ref, u2_ref, w2_ref, sent_ref
):
    ya = times(x_ref[0], a_ref[...])
    yb = times(x_ref[1], b_ref[...])
    left = left_lanes(ya.shape)
    up = jnp.where(left, ya, yb)
    down = jnp.where(left, yb, ya)
    sent_ref[...] = jnp.where(flags_ref[2] == 1, down, up)
    step = pl.program_id(0)

    @pl.when(step < early)
    def _():
        u1_ref[...] = up
        w1_ref[...] = down

    @pl.when(step >= early)
    def _():
        u2_ref[...] = up
        w2_ref[...] = down


def first_product(flags, x, a, b, block, early):
    _, rows, width = x.shape
    steps = rows // block
    whole = pl.BlockSpec(a.shape, lambda i, f: (0, 0))
    one = pl.BlockSpec((block, width), lambda i, f: (jnp.minimum(i, early - 1), 0))
    two = pl.BlockSpec((block, width), lambda i, f: (jnp.maximum(i - early, 0), 0))
    shape_one = jax.ShapeDtypeStruct((early * block, width), F32)
    shape_two = jax.ShapeDtypeStruct((rows - early * block, width), F32)
    return pl.pallas_call(
        functools.partial(first_product_kernel, early),
        grid_spec=pltpu.PrefetchScalarGridSpec(
            num_scalar_prefetch=1,
            grid=(steps,),
            in_specs=[
                pl.BlockSpec((2, block, width), lambda i, f: (0, i, 0)),
                whole,
                whole,
            ],
            out_specs=[one, one, two, two, pl.BlockSpec((block, width), lambda i, f: (i, 0))],
        ),
        out_shape=[
            shape_one,
            shape_one,
            shape_two,
            shape_two,
            jax.ShapeDtypeStruct((rows, width), F32),
        ],
        compiler_params=params(),
    )(flags, x, a, b)


def pair_gram_kernel(
    early, flags_ref, got_ref, u1_ref, w1_ref, u2_ref, w2_ref, gram_ref, a_ref, b_ref
):
    step = pl.program_id(0)

    @pl.when(step == 0)
    def _():
        a_ref[...] = jnp.zeros_like(a_ref)
        b_ref[...] = jnp.zeros_like(b_ref)

    def add(u_ref, w_ref):
        own = jnp.where(flags_ref[2] == 1, u_ref[...], w_ref[...])
        at_end = flags_ref[0] + flags_ref[1]
        own = jnp.where(at_end == 1, swapped(own, 1), own)
        got = got_ref[...]
        first = jnp.where(flags_ref[3] == 1, own, got)
        second = jnp.where(flags_ref[3] == 1, got, own)
        left = left_lanes(got.shape)
        a_ref[...] += gram_terms(jnp.where(left, first, second))
        b_ref[...] += gram_terms(jnp.where(left, second, first))

    @pl.when(step < early)
    def _():
        add(u1_ref, w1_ref)

    @pl.when(step >= early)
    def _():
        add(u2_ref, w2_ref)

    @pl.when(step == pl.num_programs(0) - 1)
    def _():
        other = gram_of_terms(b_ref[...])
        gram_ref[...] = gram_of_terms(a_ref[...]) + swapped(swapped(other, 0), 1)


def pair_gram(flags, got, u1, w1, u2, w2, block):
    rows, width = got.shape
    early = u1.shape[0] // block
    one = pl.BlockSpec((block, width), lambda i, f: (jnp.minimum(i, early - 1), 0))
    two = pl.BlockSpec((block, width), lambda i, f: (jnp.maximum(i - early, 0), 0))
    return pl.pallas_call(
        functools.partial(pair_gram_kernel, early),
        grid_spec=pltpu.PrefetchScalarGridSpec(
            num_scalar_prefetch=1,
            grid=(rows // block,),
            in_specs=[
                pl.BlockSpec((block, width), lambda i, f: (i, 0)),
                one,
                one,
                two,
                two,
            ],
            out_specs=pl.BlockSpec((width, width), lambda i, f: (0, 0)),
            scratch_shapes=[pltpu.VMEM((width, 2 * width), F32)] * 2,
        ),
        out_shape=jax.ShapeDtypeStruct((width, width), F32),
        compiler_params=params(),
    )(flags, got, u1, w1, u2, w2)


def second_product_kernel(
    flags_ref, up_ref, down_ref, got_ref, u_ref, w_ref, a_ref, b_ref, *rest
):
    out_ref = rest[-1]
    bottom = flags_ref[0] == 1
    top = flags_ref[1] == 1

    def finish(first, second):
        left = left_lanes(first.shape)
        out_ref[0] = times(jnp.where(left, first, second), a_ref[...])
        out_ref[1] = times(jnp.where(left, second, first), b_ref[...])

    @pl.when(jnp.logical_not(jnp.logical_or(bottom, top)))
    def _():
        finish(up_ref[...], down_ref[...])

    @pl.when(bottom)
    def _():
        finish(swapped(w_ref[...], 1), got_ref[...])

    @pl.when(top)
    def _():
        finish(got_ref[...], swapped(u_ref[...], 1))


def second_product(flags, up, down, got, u, w, a, b, out, start, total, block):
    rows, width = up.shape
    first = start // block
    rows_spec = pl.BlockSpec((block, width), lambda i, f: (i, 0))
    kept = pl.BlockSpec((block, width), lambda i, f: (i * (f[0] + f[1]), 0))
    got_spec = pl.BlockSpec((block, width), lambda i, f: ((i + first) * (f[0] + f[1]), 0))
    whole = pl.BlockSpec(a.shape, lambda i, f: (0, 0))
    operands = [flags, up, down, got, u, w, a, b]
    in_specs = [rows_spec, rows_spec, got_spec, kept, kept, whole, whole]
    aliases = {}
    if out is not None:
        aliases = {len(operands): 0}
        operands.append(out)
        in_specs.append(pl.BlockSpec(memory_space=pl.ANY))
    return pl.pallas_call(
        second_product_kernel,
        grid_spec=pltpu.PrefetchScalarGridSpec(
            num_scalar_prefetch=1,
            grid=(rows // block,),
            in_specs=in_specs,
            out_specs=pl.BlockSpec((2, block, width), lambda i, f: (0, i + first, 0)),
        ),
        out_shape=jax.ShapeDtypeStruct((2, total, width), F32),
        input_output_aliases=aliases,
        compiler_params=params(),
    )(*operands)


def row_partner(x, bit):
    size = lax.axis_size("rows")
    return lax.ppermute(x, "rows", [(i, i ^ bit) for i in range(size)])


def body(block, x, offsets):
    rows, width = x.shape
    half_rows = rows // 2
    steps = half_rows // block
    early = steps - 1
    place = lax.axis_index("loop")
    count = lax.axis_size("loop")
    last = count - 1
    odd = place % 2
    flags = jnp.stack(
        [
            (place == 0).astype(jnp.int32),
            (place == last).astype(jnp.int32),
            odd.astype(jnp.int32),
            ((place == 0) | ((odd == 1) & (place != last))).astype(jnp.int32),
        ]
    )
    halves = x.reshape(2, half_rows, width)

    gram = local_gram(x, 2 * block)
    gram = gram + row_partner(gram, 1)
    a, b = rotations(0, flags, offsets, gram, row_partner(gram, 2))
    u1, w1, u2, w2, sent = first_product(flags, halves, a, b, block, early)

    ups = [(i, i + 1) for i in range(last - 1)]
    downs = [(i, i - 1) for i in range(2, count)]
    skips = (
        [(i, i + 2) for i in range(0, last - 1, 2)]
        + [(i, i - 2) for i in range(3, count, 2)]
        + [(1, 0), (last - 1, last)]
    )
    homes = (
        [(i, i - 1) for i in range(2, count, 2)]
        + [(i, i + 1) for i in range(1, last, 2)]
        + [(0, 0), (last, last)]
    )
    up1 = lax.ppermute(u1, "loop", ups)
    down1 = lax.ppermute(w1, "loop", downs)
    got = lax.ppermute(sent, "loop", skips)
    up2 = lax.ppermute(u2, "loop", ups)
    down2 = lax.ppermute(w2, "loop", downs)

    gram = pair_gram(flags, got, u1, w1, u2, w2, block)
    gram = lax.ppermute(gram, "loop", homes)
    gram = gram + row_partner(gram, 1)
    a, b = rotations(1, flags, offsets, gram, row_partner(gram, 2))

    out = second_product(flags, up1, down1, got, u1, w1, a, b, None, 0, half_rows, block)
    out = second_product(
        flags, up2, down2, got, u2, w2, a, b, out, early * block, half_rows, block
    )
    return out.reshape(rows, width)


def solution(mesh, block=1024):
    placed = (P("rows", "loop"), P())
    return jax.shard_map(
        functools.partial(body, block),
        mesh=mesh,
        in_specs=placed,
        out_specs=P("rows", "loop"),
        check_vma=False,
    )
```

time: 642 us -> 366 us (0.57)
  the two profiles are of different devices: /device:TPU:0 before, /device:TPU:32 now
where the time goes in v1:
time: 366 us; the launch traced here: 364 us
  waiting for transfers between devices  262 us (72%)
  Pallas kernels  68.4 us (19%)
  starting transfers between devices  27.5 us (8%)
  local copies, waits for them, and re-layouts  5.06 us (1%)
    ppermute x1, waiting for transfers between devices, body(): got = lax.ppermute(sent, 'loop', skips)  247 us
    pallas_call x2, Pallas kernels, second_product(): pl.pallas_call(second_product_kernel, grid_spec=pltpu.PrefetchScalarGridS...  20 us
    pallas_call x1, Pallas kernels, first_product(): pl.pallas_call(functools.partial(first_product_kernel, early), grid_spec=...  17.6 us
    pallas_call x1, Pallas kernels, pair_gram(): pl.pallas_call(functools.partial(pair_gram_kernel, early), grid_spec=pltp...  14.2 us
    pallas_call x1, Pallas kernels, local_gram(): pl.pallas_call(gram_kernel, grid=(rows // block,), in_specs=[pl.BlockSpec...  11 us
    ppermute x4, waiting for transfers between devices, row_partner(): return lax.ppermute(x, 'rows', [(i, i ^ bit) for i in range(size)])  7.87 us
    ppermute x1, waiting for transfers between devices, body(): gram = lax.ppermute(gram, 'loop', homes)  7.49 us
  transfers between devices with their start and end apart: 10, of which 6 were waited for; matrix products, arithmetic and copies ran while one was open for 0% of the time, Pallas kernels for 9%

profile of v1, /device:TPU:32, one launch (start us, length us, event | category | flops | bytes accessed | tf_op | source)
XLA Modules:
  0.0 364.4 jit_solution(956280989527677551)
XLA Ops:
  0.0 0.0 copy-start.6
  0.0 11.0 %shard_map.28 = f32[128,128]{1,0:T(8,128)} custom-call(f32[24576,128]{1,0:T(8,128)} %x_ref.1), custom_call_target="tpu_custom_call" | custom-call | tf_op jit(solution)/shard_map/pallas_call | solution.py:74
  11.0 0.0 collective-permute-start
  11.0 1.5 collective-permute-done
  12.5 0.9 add.11.one_ref
  13.3 3.2 collective-permute-start.1
  16.5 0.1 pad_add_fusion.flags_ref
  16.6 0.0 copy-start.4
  16.6 2.5 collective-permute-done.1.two_ref
  19.1 0.0 copy-done.6
  19.1 2.9 shard_map.29
  22.0 0.0 copy-start.2
  22.0 0.6 copy-done.2
  22.7 0.0 copy-start.3
  22.7 0.7 copy-done.3
  23.3 0.0 copy-done.4
  23.3 17.6 %shard_map.30 = (f32[11264,128]{1,0:T(8,128)}, f32[11264,128]{1,0:T(8,128)}, f32[1024,128]{1,0:T(8,128)}, f32[1024,128]{1,0:T(8,128)}, f32[12288,128]{1,0:T(8,128)}) custom-call(s32[4]{0:T(128)} %copy-done.4, f32[2,12288,128]{2,1,0:T(8,128)} %bitcast.6, bf16[256,256]{1,0:T(8,128)(2,1)} %copy-done.2, bf16[256,256]{1,0:T(8,128)(2,1)} %copy-done.3), custom_call_target="tpu_custom_call" | custom-call | tf_op jit(solution)/shard_map/pallas_call | solution.py:178
  40.9 1.5 collective-permute-start.4
  42.4 4.3 %collective-permute-start.8 = (f32[11264,128]{1,0:T(8,128)}, f32[11264,128]{1,0:T(8,128)S(1)}, u32[]{:S(2)}, u32[]{:S(2)}) collective-permute-start(f32[11264,128]{1,0:T(8,128)} %get-tuple-element.19.u1_ref.u_ref), channel_id=1, source_target_pairs={{0,1},{1,2},{2,3},{3,4},{4,5},{5,6},{6,7},{7,8},{8,9},{9,10},{10,1... | collective-permute-start | bytes 17301512 | tf_op jit(solution)/shard_map/ppermute | solution.py:355
  46.7 4.6 %collective-permute-start.9 = (f32[11264,128]{1,0:T(8,128)}, f32[11264,128]{1,0:T(8,128)}, u32[]{:S(2)}, u32[]{:S(2)}) collective-permute-start(f32[11264,128]{1,0:T(8,128)} %get-tuple-element.20.w1_ref.w_ref), channel_id=1, source_target_pairs={{2,1},{3,2},{4,3},{5,4},{6,5},{7,6},{8,7},{9,8},{10,9},{11,10},{12... | collective-permute-start | bytes 17301512 | tf_op jit(solution)/shard_map/ppermute | solution.py:356
  51.2 1.9 collective-permute-start.2
  53.2 0.0 copy-start.5
  53.2 6.9 %collective-permute-start.3 = (f32[1024,128]{1,0:T(8,128)}, f32[1024,128]{1,0:T(8,128)}, u32[]{:S(2)}, u32[]{:S(2)}) collective-permute-start(f32[1024,128]{1,0:T(8,128)} %get-tuple-element.17.w2_ref.w_ref), channel_id=1, source_target_pairs={{2,1},{3,2},{4,3},{5,4},{6,5},{7,6},{8,7},{9,8},{10,9},{11,10},{12... | collective-permute-start | bytes 1572872 | tf_op jit(solution)/shard_map/ppermute | solution.py:359
  60.1 246.9 %collective-permute-done.4.got_ref = f32[12288,128]{1,0:T(8,128)} collective-permute-done((f32[12288,128]{1,0:T(8,128)}, f32[12288,128]{1,0:T(8,128)}, u32[]{:S(2)}, u32[]{:S(2)}) %collective-permute-start.4) | collective-permute-done | bytes 6291488 | tf_op jit(solution)/shard_map/ppermute | solution.py:357
  307.1 14.2 %shard_map.31 = f32[128,128]{1,0:T(8,128)} custom-call(s32[4]{0:T(128)} %copy-done.4, f32[12288,128]{1,0:T(8,128)} %collective-permute-done.4.got_ref, f32[11264,128]{1,0:T(8,128)} %get-tuple-element.19.u1_ref.u_ref, f32[11264,128]{1,0:T(8,128)} %get-tuple-element.20.w1_ref.w_ref, f32[1024,128]{1,0:T(8,128)} %get-tuple-element.16.u2_ref.u_ref, ...), custom_call_target="tpu_custom_call" | custom-call | tf_op jit(solution)/shard_map/pallas_call | solution.py:241
  321.3 2.0 collective-permute-start.5
  323.2 7.5 %collective-permute-done.5 = f32[128,128]{1,0:T(8,128)S(1)} collective-permute-done((f32[128,128]{1,0:T(8,128)}, f32[128,128]{1,0:T(8,128)S(1)}, u32[]{:S(2)}, u32[]{:S(2)}) %collective-permute-start.5) | collective-permute-done | bytes 65568 | tf_op jit(solution)/shard_map/ppermute | solution.py:362
  330.7 0.0 collective-permute-start.6
  330.7 1.3 collective-permute-done.6
  332.0 3.2 collective-permute-start.7
  335.2 2.7 collective-permute-done.7.two_ref
  337.8 0.0 copy-done.5
  337.8 2.7 shard_map.32
  340.6 0.0 copy-start
  340.6 0.7 copy-done
  341.3 0.0 copy-start.1
  341.3 0.6 copy-done.1
  341.9 0.0 collective-permute-done.8.up_ref
  341.9 0.0 copy-start.7
  341.9 0.0 collective-permute-done.9.down_ref
  341.9 2.4 copy-done.7
  344.3 16.2 %shard_map.33.rest_0_ = f32[2,12288,128]{2,1,0:T(8,128)} custom-call(s32[4]{0:T(128)} %copy-done.4, f32[11264,128]{1,0:T(8,128)} %copy-done.7, f32[11264,128]{1,0:T(8,128)} %collective-permute-done.9.down_ref, f32[12288,128]{1,0:T(8,128)} %collective-permute-done.4.got_ref, f32[11264,128]{1,0:T(8,128)} %get-tuple-element.19.u1_ref.u_ref, ...), custom_call_target="tpu_custom_call" | custom-call | tf_op jit(solution)/shard_map/pallas_call | solution.py:300
  360.5 0.0 collective-permute-done.2.up_ref
  360.5 0.0 collective-permute-done.3.down_ref
  360.5 3.8 %shard_map.34 = f32[2,12288,128]{2,1,0:T(8,128)} custom-call(s32[4]{0:T(128)} %copy-done.4, f32[1024,128]{1,0:T(8,128)} %collective-permute-done.2.up_ref, f32[1024,128]{1,0:T(8,128)} %collective-permute-done.3.down_ref, f32[12288,128]{1,0:T(8,128)} %collective-permute-done.4.got_ref, ...), custom_call_target="tpu_custom_call", output_to_operand_aliasing={{}: (8, {})} | custom-call | tf_op jit(solution)/shard_map/pallas_call | solution.py:300
  (1 shorter events, 0.0 us)
Async XLA Ops:
  0.0 19.1 %copy-start.6 = (s32[2,4]{1,0:T(2,128)S(1)}, s32[2,4]{1,0:T(2,128)}, u32[]{:S(2)}) copy-start(s32[2,4]{1,0:T(2,128)} %offsets_ref.3) | copy-start | bytes 100
  11.0 1.5 collective-permute-start
  13.3 5.8 %collective-permute-start.1 = (f32[128,128]{1,0:T(8,128)S(1)}, f32[128,128]{1,0:T(8,128)S(1)}, u32[]{:S(2)}, u32[]{:S(2)}) collective-permute-start(f32[128,128]{1,0:T(8,128)S(1)} %add.11.one_ref), channel_id=1, source_target_pairs={{0,64},{32,96},{64,0},{96,32},{1,65},{33,97},{65,1},{97,33},{2,66}... | collective-permute-start | bytes 196616 | tf_op jit(solution)/shard_map/ppermute | solution.py:316
  16.6 6.7 %copy-start.4 = (s32[4]{0:T(128)}, s32[4]{0:T(128)S(1)}, u32[]{:S(2)}) copy-start(s32[4]{0:T(128)S(1)} %pad_add_fusion.flags_ref) | copy-start | bytes 52
  22.0 0.6 copy-start.2
  22.7 0.7 copy-start.3
  40.9 266.2 %collective-permute-start.4 = (f32[12288,128]{1,0:T(8,128)}, f32[12288,128]{1,0:T(8,128)}, u32[]{:S(2)}, u32[]{:S(2)}) collective-permute-start(f32[12288,128]{1,0:T(8,128)} %get-tuple-element.18), channel_id=1, source_target_pairs={{0,2},{2,4},{4,6},{6,8},{8,10},{10,12},{12,14},{14,16},{16,18},{18... | collective-permute-start | bytes 18874376 | tf_op jit(solution)/shard_map/ppermute | solution.py:357
  42.4 299.5 %collective-permute-start.8 = (f32[11264,128]{1,0:T(8,128)}, f32[11264,128]{1,0:T(8,128)S(1)}, u32[]{:S(2)}, u32[]{:S(2)}) collective-permute-start(f32[11264,128]{1,0:T(8,128)} %get-tuple-element.19.u1_ref.u_ref), channel_id=1, source_target_pairs={{0,1},{1,2},{2,3},{3,4},{4,5},{5,6},{6,7},{7,8},{8,9},{9,10},{10,1... | collective-permute-start | bytes 17301512 | tf_op jit(solution)/shard_map/ppermute | solution.py:355
  46.7 295.2 %collective-permute-start.9 = (f32[11264,128]{1,0:T(8,128)}, f32[11264,128]{1,0:T(8,128)}, u32[]{:S(2)}, u32[]{:S(2)}) collective-permute-start(f32[11264,128]{1,0:T(8,128)} %get-tuple-element.20.w1_ref.w_ref), channel_id=1, source_target_pairs={{2,1},{3,2},{4,3},{5,4},{6,5},{7,6},{8,7},{9,8},{10,9},{11,10},{12... | collective-permute-start | bytes 17301512 | tf_op jit(solution)/shard_map/ppermute | solution.py:356
  51.2 309.3 %collective-permute-start.2 = (f32[1024,128]{1,0:T(8,128)}, f32[1024,128]{1,0:T(8,128)}, u32[]{:S(2)}, u32[]{:S(2)}) collective-permute-start(f32[1024,128]{1,0:T(8,128)} %get-tuple-element.16.u2_ref.u_ref), channel_id=1, source_target_pairs={{0,1},{1,2},{2,3},{3,4},{4,5},{5,6},{6,7},{7,8},{8,9},{9,10},{10,1... | collective-permute-start | bytes 1572872 | tf_op jit(solution)/shard_map/ppermute | solution.py:358
  53.2 284.7 %copy-start.5 = (s32[4]{0:T(128)S(1)}, s32[4]{0:T(128)}, u32[]{:S(2)}) copy-start(s32[4]{0:T(128)} %copy-done.4) | copy-start | bytes 52
  53.2 307.3 %collective-permute-start.3 = (f32[1024,128]{1,0:T(8,128)}, f32[1024,128]{1,0:T(8,128)}, u32[]{:S(2)}, u32[]{:S(2)}) collective-permute-start(f32[1024,128]{1,0:T(8,128)} %get-tuple-element.17.w2_ref.w_ref), channel_id=1, source_target_pairs={{2,1},{3,2},{4,3},{5,4},{6,5},{7,6},{8,7},{9,8},{10,9},{11,10},{12... | collective-permute-start | bytes 1572872 | tf_op jit(solution)/shard_map/ppermute | solution.py:359
  321.3 9.5 %collective-permute-start.5 = (f32[128,128]{1,0:T(8,128)}, f32[128,128]{1,0:T(8,128)S(1)}, u32[]{:S(2)}, u32[]{:S(2)}) collective-permute-start(f32[128,128]{1,0:T(8,128)} %shard_map.31), channel_id=1, source_target_pairs={{2,1},{4,3},{6,5},{8,7},{10,9},{12,11},{14,13},{16,15},{18,17},{20... | collective-permute-start | bytes 196616 | tf_op jit(solution)/shard_map/ppermute | solution.py:362
  330.7 1.3 collective-permute-start.6
  332.0 5.8 %collective-permute-start.7 = (f32[128,128]{1,0:T(8,128)S(1)}, f32[128,128]{1,0:T(8,128)S(1)}, u32[]{:S(2)}, u32[]{:S(2)}) collective-permute-start(f32[128,128]{1,0:T(8,128)S(1)} %add.12.one_ref), channel_id=1, source_target_pairs={{0,64},{32,96},{64,0},{96,32},{1,65},{33,97},{65,1},{97,33},{2,66}... | collective-permute-start | bytes 196616 | tf_op jit(solution)/shard_map/ppermute | solution.py:316
  340.6 0.7 copy-start
  341.3 0.6 copy-start.1
  341.9 2.4 copy-start.7

commit v2 on v1

--- a/solution.py
+++ b/solution.py
@@ -145,38 +145,43 @@
     )(flags, offsets, one, two)
 
 
-def first_product_kernel(
-    early, flags_ref, x_ref, a_ref, b_ref, u1_ref, w1_ref, u2_ref, w2_ref, sent_ref
-):
+def run_spec(low, count, block, width):
+    return pl.BlockSpec(
+        (block, width), lambda i, f: (jnp.clip(i - low, 0, count - 1), 0)
+    )
+
+
+def first_product_kernel(runs, flags_ref, x_ref, a_ref, b_ref, *out_refs):
     ya = times(x_ref[0], a_ref[...])
     yb = times(x_ref[1], b_ref[...])
     left = left_lanes(ya.shape)
     up = jnp.where(left, ya, yb)
     down = jnp.where(left, yb, ya)
-    sent_ref[...] = jnp.where(flags_ref[2] == 1, down, up)
     step = pl.program_id(0)
-
-    @pl.when(step < early)
-    def _():
-        u1_ref[...] = up
-        w1_ref[...] = down
-
-    @pl.when(step >= early)
-    def _():
-        u2_ref[...] = up
-        w2_ref[...] = down
-
-
-def first_product(flags, x, a, b, block, early):
+    for which, (low, count) in enumerate(runs):
+
+        @pl.when((step >= low) & (step < low + count))
+        def _():
+            out_refs[2 * which][...] = up
+            out_refs[2 * which + 1][...] = down
+
+    @pl.when(step >= runs[0][1])
+    def _():
+        out_refs[-1][...] = jnp.where(flags_ref[2] == 1, down, up)
+
+
+def first_product(flags, x, a, b, block, runs):
     _, rows, width = x.shape
     steps = rows // block
+    first_run = runs[0][1]
     whole = pl.BlockSpec(a.shape, lambda i, f: (0, 0))
-    one = pl.BlockSpec((block, width), lambda i, f: (jnp.minimum(i, early - 1), 0))
-    two = pl.BlockSpec((block, width), lambda i, f: (jnp.maximum(i - early, 0), 0))
-    shape_one = jax.ShapeDtypeStruct((early * block, width), F32)
-    shape_two = jax.ShapeDtypeStruct((rows - early * block, width), F32)
+    out_specs, out_shape = [], []
+    for low, count in runs + [(first_run, steps - first_run)]:
+        for _ in range(2 if len(out_specs) < 2 * len(runs) else 1):
+            out_specs.append(run_spec(low, count, block, width))
+            out_shape.append(jax.ShapeDtypeStruct((count * block, width), F32))
     return pl.pallas_call(
-        functools.partial(first_product_kernel, early),
+        functools.partial(first_product_kernel, runs),
         grid_spec=pltpu.PrefetchScalarGridSpec(
             num_scalar_prefetch=1,
             grid=(steps,),
@@ -185,22 +190,15 @@
                 whole,
                 whole,
             ],
-            out_specs=[one, one, two, two, pl.BlockSpec((block, width), lambda i, f: (i, 0))],
+            out_specs=out_specs,
         ),
-        out_shape=[
-            shape_one,
-            shape_one,
-            shape_two,
-            shape_two,
-            jax.ShapeDtypeStruct((rows, width), F32),
-        ],
+        out_shape=out_shape,
         compiler_params=params(),
     )(flags, x, a, b)
 
 
-def pair_gram_kernel(
-    early, flags_ref, got_ref, u1_ref, w1_ref, u2_ref, w2_ref, gram_ref, a_ref, b_ref
-):
+def packed_gram_kernel(halves, flags_ref, *refs):
+    *in_refs, gram_ref, a_ref, b_ref = refs
     step = pl.program_id(0)
 
     @pl.when(step == 0)
@@ -208,97 +206,154 @@
         a_ref[...] = jnp.zeros_like(a_ref)
         b_ref[...] = jnp.zeros_like(b_ref)
 
-    def add(u_ref, w_ref):
+    def add(first, second):
+        left = left_lanes(first.shape)
+        a_ref[...] += gram_terms(jnp.where(left, first, second))
+        b_ref[...] += gram_terms(jnp.where(left, second, first))
+
+    halves(step, flags_ref, add, *in_refs)
+
+    @pl.when(step == pl.num_programs(0) - 1)
+    def _():
+        other = gram_of_terms(b_ref[...])
+        gram_ref[...] = gram_of_terms(a_ref[...]) + swapped(swapped(other, 0), 1)
+
+
+def neighbour_halves(early, step, flags_ref, add, got_ref, *own_refs):
+    def with_own(u_ref, w_ref):
         own = jnp.where(flags_ref[2] == 1, u_ref[...], w_ref[...])
         at_end = flags_ref[0] + flags_ref[1]
         own = jnp.where(at_end == 1, swapped(own, 1), own)
         got = got_ref[...]
-        first = jnp.where(flags_ref[3] == 1, own, got)
-        second = jnp.where(flags_ref[3] == 1, got, own)
-        left = left_lanes(got.shape)
-        a_ref[...] += gram_terms(jnp.where(left, first, second))
-        b_ref[...] += gram_terms(jnp.where(left, second, first))
+        own_first = flags_ref[3] == 1
+        add(jnp.where(own_first, own, got), jnp.where(own_first, got, own))
 
     @pl.when(step < early)
     def _():
-        add(u1_ref, w1_ref)
+        with_own(*own_refs[:2])
 
     @pl.when(step >= early)
     def _():
-        add(u2_ref, w2_ref)
-
-    @pl.when(step == pl.num_programs(0) - 1)
-    def _():
-        other = gram_of_terms(b_ref[...])
-        gram_ref[...] = gram_of_terms(a_ref[...]) + swapped(swapped(other, 0), 1)
-
-
-def pair_gram(flags, got, u1, w1, u2, w2, block):
-    rows, width = got.shape
-    early = u1.shape[0] // block
-    one = pl.BlockSpec((block, width), lambda i, f: (jnp.minimum(i, early - 1), 0))
-    two = pl.BlockSpec((block, width), lambda i, f: (jnp.maximum(i - early, 0), 0))
+        with_own(*own_refs[2:])
+
+
+def arrived_halves(step, flags_ref, add, up_ref, down_ref, u_ref, w_ref):
+    bottom = flags_ref[0] == 1
+    top = flags_ref[1] == 1
+
+    @pl.when(jnp.logical_not(jnp.logical_or(bottom, top)))
+    def _():
+        add(up_ref[...], down_ref[...])
+
+    @pl.when(bottom)
+    def _():
+        add(swapped(w_ref[...], 1), down_ref[...])
+
+    @pl.when(top)
+    def _():
+        add(up_ref[...], swapped(u_ref[...], 1))
+
+
+def skipped_halves(step, flags_ref, add, up_ref, down_ref, u_ref, w_ref, got_ref):
+    bottom = flags_ref[0] == 1
+    top = flags_ref[1] == 1
+
+    @pl.when(jnp.logical_not(jnp.logical_or(bottom, top)))
+    def _():
+        add(up_ref[...], down_ref[...])
+
+    @pl.when(bottom)
+    def _():
+        add(swapped(w_ref[...], 1), got_ref[...])
+
+    @pl.when(top)
+    def _():
+        add(got_ref[...], swapped(u_ref[...], 1))
+
+
+def gram_call(halves, flags, operands, specs, steps):
+    width = operands[0].shape[1]
     return pl.pallas_call(
-        functools.partial(pair_gram_kernel, early),
+        functools.partial(packed_gram_kernel, halves),
         grid_spec=pltpu.PrefetchScalarGridSpec(
             num_scalar_prefetch=1,
-            grid=(rows // block,),
-            in_specs=[
-                pl.BlockSpec((block, width), lambda i, f: (i, 0)),
-                one,
-                one,
-                two,
-                two,
-            ],
+            grid=(steps,),
+            in_specs=specs,
             out_specs=pl.BlockSpec((width, width), lambda i, f: (0, 0)),
             scratch_shapes=[pltpu.VMEM((width, 2 * width), F32)] * 2,
         ),
         out_shape=jax.ShapeDtypeStruct((width, width), F32),
         compiler_params=params(),
-    )(flags, got, u1, w1, u2, w2)
-
-
-def second_product_kernel(
-    flags_ref, up_ref, down_ref, got_ref, u_ref, w_ref, a_ref, b_ref, *rest
-):
-    out_ref = rest[-1]
-    bottom = flags_ref[0] == 1
-    top = flags_ref[1] == 1
+    )(flags, *operands)
+
+
+def neighbour_gram(flags, got, u2, w2, u3, w3, block):
+    rows, width = got.shape
+    early = u2.shape[0] // block
+    late = u3.shape[0] // block
+    one = run_spec(0, early, block, width)
+    two = run_spec(early, late, block, width)
+    every = run_spec(0, early + late, block, width)
+    return gram_call(
+        functools.partial(neighbour_halves, early),
+        flags,
+        [got, u2, w2, u3, w3],
+        [every, one, one, two, two],
+        early + late,
+    )
+
+
+def kept_spec(block, width):
+    return pl.BlockSpec((block, width), lambda i, f: (i * (f[0] + f[1]), 0))
+
+
+def arrived_gram(flags, up, down, u, w, block):
+    rows, width = up.shape
+    steps = rows // block
+    every = run_spec(0, steps, block, width)
+    kept = kept_spec(block, width)
+    return gram_call(
+        arrived_halves, flags, [up, down, u, w], [every, every, kept, kept], steps
+    )
+
+
+def second_product_kernel(halves, count, flags_ref, a_ref, b_ref, *refs):
+    out_ref = refs[-1]
 
     def finish(first, second):
         left = left_lanes(first.shape)
         out_ref[0] = times(jnp.where(left, first, second), a_ref[...])
         out_ref[1] = times(jnp.where(left, second, first), b_ref[...])
 
-    @pl.when(jnp.logical_not(jnp.logical_or(bottom, top)))
-    def _():
-        finish(up_ref[...], down_ref[...])
-
-    @pl.when(bottom)
-    def _():
-        finish(swapped(w_ref[...], 1), got_ref[...])
-
-    @pl.when(top)
-    def _():
-        finish(got_ref[...], swapped(u_ref[...], 1))
-
-
-def second_product(flags, up, down, got, u, w, a, b, out, start, total, block):
-    rows, width = up.shape
+    halves(pl.program_id(0), flags_ref, finish, *refs[:count])
+
+
+def second_product(flags, a, b, operands, got, got_start, out, start, total, block):
+    rows, width = operands[0].shape
     first = start // block
-    rows_spec = pl.BlockSpec((block, width), lambda i, f: (i, 0))
-    kept = pl.BlockSpec((block, width), lambda i, f: (i * (f[0] + f[1]), 0))
-    got_spec = pl.BlockSpec((block, width), lambda i, f: ((i + first) * (f[0] + f[1]), 0))
+    got_first = got_start // block
+    every = run_spec(0, rows // block, block, width)
+    kept = kept_spec(block, width)
     whole = pl.BlockSpec(a.shape, lambda i, f: (0, 0))
-    operands = [flags, up, down, got, u, w, a, b]
-    in_specs = [rows_spec, rows_spec, got_spec, kept, kept, whole, whole]
+    in_specs = [whole, whole, every, every, kept, kept]
+    operands = list(operands)
+    halves = arrived_halves
+    if got is not None:
+        halves = skipped_halves
+        operands.append(got)
+        in_specs.append(
+            pl.BlockSpec(
+                (block, width), lambda i, f: ((i + got_first) * (f[0] + f[1]), 0)
+            )
+        )
+    count = len(operands)
     aliases = {}
     if out is not None:
-        aliases = {len(operands): 0}
+        aliases = {3 + count: 0}
         operands.append(out)
         in_specs.append(pl.BlockSpec(memory_space=pl.ANY))
     return pl.pallas_call(
-        second_product_kernel,
+        functools.partial(second_product_kernel, halves, count),
         grid_spec=pltpu.PrefetchScalarGridSpec(
             num_scalar_prefetch=1,
             grid=(rows // block,),
@@ -308,7 +363,7 @@
         out_shape=jax.ShapeDtypeStruct((2, total, width), F32),
         input_output_aliases=aliases,
         compiler_params=params(),
-    )(*operands)
+    )(flags, a, b, *operands)
 
 
 def row_partner(x, bit):
@@ -320,7 +375,13 @@
     rows, width = x.shape
     half_rows = rows // 2
     steps = half_rows // block
-    early = steps - 1
+    late = max(1, steps // 12)
+    middle = max(1, steps // 4)
+    runs = [
+        (0, steps - middle - late),
+        (steps - middle - late, middle),
+        (steps - late, late),
+    ]
     place = lax.axis_index("loop")
     count = lax.axis_size("loop")
     last = count - 1
@@ -338,10 +399,10 @@
     gram = local_gram(x, 2 * block)
     gram = gram + row_partner(gram, 1)
     a, b = rotations(0, flags, offsets, gram, row_partner(gram, 2))
-    u1, w1, u2, w2, sent = first_product(flags, halves, a, b, block, early)
-
-    ups = [(i, i + 1) for i in range(last - 1)]
-    downs = [(i, i - 1) for i in range(2, count)]
+    u1, w1, u2, w2, u3, w3, sent = first_product(flags, halves, a, b, block, runs)
+
+    ups = [(i, i + 1) for i in range(last)]
+    downs = [(i, i - 1) for i in range(1, count)]
     skips = (
         [(i, i + 2) for i in range(0, last - 1, 2)]
         + [(i, i - 2) for i in range(3, count, 2)]
@@ -355,18 +416,35 @@
     up1 = lax.ppermute(u1, "loop", ups)
     down1 = lax.ppermute(w1, "loop", downs)
     got = lax.ppermute(sent, "loop", skips)
-    up2 = lax.ppermute(u2, "loop", ups)
-    down2 = lax.ppermute(w2, "loop", downs)
-
-    gram = pair_gram(flags, got, u1, w1, u2, w2, block)
+    up2 = lax.ppermute(u2, "loop", ups[:-1])
+    down2 = lax.ppermute(w2, "loop", downs[1:])
+    up3 = lax.ppermute(u3, "loop", ups[:-1])
+    down3 = lax.ppermute(w3, "loop", downs[1:])
+
+    gram = neighbour_gram(flags, got, u2, w2, u3, w3, block)
     gram = lax.ppermute(gram, "loop", homes)
+    gram = gram + arrived_gram(flags, up1, down1, u1, w1, block)
     gram = gram + row_partner(gram, 1)
     a, b = rotations(1, flags, offsets, gram, row_partner(gram, 2))
 
-    out = second_product(flags, up1, down1, got, u1, w1, a, b, None, 0, half_rows, block)
-    out = second_product(
-        flags, up2, down2, got, u2, w2, a, b, out, early * block, half_rows, block
-    )
+    out = None
+    for (low, _), arrays, got_start, size in (
+        (runs[0], (up1, down1, u1, w1), None, block),
+        (runs[1], (up2, down2, u2, w2), 0, block),
+        (runs[2], (up3, down3, u3, w3), runs[1][1] * block, max(16, block // 4)),
+    ):
+        out = second_product(
+            flags,
+            a,
+            b,
+            arrays,
+            None if got_start is None else got,
+            got_start or 0,
+            out,
+            low * block,
+            half_rows,
+            size,
+        )
     return out.reshape(rows, width)
 
 

time: 366 us -> 383 us (1.046)
  the two profiles are of different devices: /device:TPU:32 before, /device:TPU:0 now
where the time goes in v2:
time: 383 us; the launch traced here: 382 us
  waiting for transfers between devices  275 us (72%)
  Pallas kernels  75.9 us (20%)
  starting transfers between devices  23.4 us (6%)
  local copies, waits for them, and re-layouts  5.68 us (1%)
    ppermute x1, waiting for transfers between devices, body(): got = lax.ppermute(sent, 'loop', skips)  266 us
    pallas_call x3, Pallas kernels, second_product(): pl.pallas_call(functools.partial(second_product_kernel, halves, count), g...  25.3 us
    pallas_call x2, Pallas kernels, gram_call(): pl.pallas_call(functools.partial(packed_gram_kernel, halves), grid_spec=p...  17 us
    pallas_call x1, Pallas kernels, first_product(): pl.pallas_call(functools.partial(first_product_kernel, runs), grid_spec=p...  17 us
    pallas_call x1, Pallas kernels, local_gram(): pl.pallas_call(gram_kernel, grid=(rows // block,), in_specs=[pl.BlockSpec...  11 us
    ppermute x4, waiting for transfers between devices, row_partner(): return lax.ppermute(x, 'rows', [(i, i ^ bit) for i in range(size)])  8.92 us
  transfers between devices with their start and end apart: 12, of which 5 were waited for; matrix products, arithmetic and copies ran while one was open for 0% of the time, Pallas kernels for 10%

profile of v2, /device:TPU:0, one launch (start us, length us, event | category | flops | bytes accessed | tf_op | source)
XLA Modules:
  0.0 381.9 jit_solution(9499013108646349883)
XLA Ops:
  0.0 11.0 %shard_map.28 = f32[128,128]{1,0:T(8,128)} custom-call(f32[24576,128]{1,0:T(8,128)} %x_ref.1), custom_call_target="tpu_custom_call" | custom-call | tf_op jit(solution)/shard_map/pallas_call | solution.py:74
  11.0 0.0 collective-permute-start
  11.0 1.5 collective-permute-done
  12.5 0.9 add.14.one_ref
  13.4 3.3 collective-permute-start.1
  16.6 0.1 pad_add_fusion.flags_ref
  16.7 2.4 collective-permute-done.1.two_ref
  19.1 0.0 copy-done.6
  19.1 2.9 shard_map.29
  22.0 0.0 copy-start.2
  22.0 0.6 copy-done.2
  22.7 0.6 copy-done.3
  23.3 0.0 copy-done.4
  23.3 17.0 %shard_map.30 = (f32[8192,128]{1,0:T(8,128)}, f32[8192,128]{1,0:T(8,128)}, f32[3072,128]{1,0:T(8,128)}, f32[3072,128]{1,0:T(8,128)}, f32[1024,128]{1,0:T(8,128)}...) custom-call(s32[4]{0:T(128)} %copy-done.4, f32[2,12288,128]{2,1,0:T(8,128)} %bitcast.6, bf16[256,256]{1,0:T(8,128)(2,1)} %copy-done.2, ...), custom_call_target="tpu_custom_call" | custom-call | tf_op jit(solution)/shard_map/pallas_call | solution.py:183
  40.3 5.5 %collective-permute-start.4 = (f32[8192,128]{1,0:T(8,128)}, f32[8192,128]{1,0:T(8,128)}, u32[]{:S(2)}, u32[]{:S(2)}) collective-permute-start(f32[8192,128]{1,0:T(8,128)} %get-tuple-element.23.refs_2_), channel_id=1, source_target_pairs={{0,1},{1,2},{2,3},{3,4},{4,5},{5,6},{6,7},{7,8},{8,9},{9,10},{10,1... | collective-permute-start | bytes 12582920 | tf_op jit(solution)/shard_map/ppermute | solution.py:416
  45.8 1.3 collective-permute-start.5
  47.1 1.5 collective-permute-start.2
  48.6 3.2 collective-permute-start.10
  51.8 0.8 collective-permute-start.11
  52.6 266.0 %collective-permute-done.2.refs_0_.refs_4_ = f32[4096,128]{1,0:T(8,128)S(1)} collective-permute-done((f32[4096,128]{1,0:T(8,128)}, f32[4096,128]{1,0:T(8,128)S(1)}, u32[]{:S(2)}, u32[]{:S(2)}) %collective-permute-start.2) | collective-permute-done | bytes 2097184 | tf_op jit(solution)/shard_map/ppermute | solution.py:418
  318.6 1.6 collective-permute-start.8
  320.2 0.0 collective-permute-done.4.refs_0_
  320.2 1.5 collective-permute-start.9
  321.7 0.0 copy-done.7
  321.7 6.2 %shard_map.31 = f32[128,128]{1,0:T(8,128)} custom-call(s32[4]{0:T(128)} %copy-done.4, f32[4096,128]{1,0:T(8,128)} %copy-done.7, f32[3072,128]{1,0:T(8,128)} %get-tuple-element.19.refs_1_.refs_2_, f32[3072,128]{1,0:T(8,128)} %get-tuple-element.20.refs_2_.refs_3_, f32[1024,128]{1,0:T(8,128)} %get-tuple-element.21.refs_3_.refs_2_, ...), custom_call_target="tpu_custom_call" | custom-call | tf_op jit(solution)/shard_map/pallas_call | solution.py:276
  327.9 0.0 collective-permute-done.5.refs_1_
  327.9 1.5 collective-permute-start.3
  329.4 10.8 %shard_map.32 = f32[128,128]{1,0:T(8,128)} custom-call(s32[4]{0:T(128)} %copy-done.4, f32[8192,128]{1,0:T(8,128)} %collective-permute-done.4.refs_0_, f32[8192,128]{1,0:T(8,128)} %collective-permute-done.5.refs_1_, f32[8192,128]{1,0:T(8,128)} %get-tuple-element.23.refs_2_, f32[8192,128]{1,0:T(8,128)} %get-tuple-element.24.refs_3_), custom_call_target="tpu_custom_call" | custom-call | tf_op jit(solution)/shard_map/pallas_call | solution.py:276
  340.2 0.0 collective-permute-done.3
  340.2 0.9 add.15
  341.1 0.0 collective-permute-start.6
  341.1 1.2 collective-permute-done.6
  342.4 3.3 collective-permute-start.7
  345.6 3.8 collective-permute-done.7.two_ref
  349.4 2.7 shard_map.33
  352.2 0.0 copy-start
  352.2 0.6 copy-done
  352.8 0.6 copy-done.1
  353.5 13.0 %shard_map.34.refs_5_ = f32[2,12288,128]{2,1,0:T(8,128)} custom-call(s32[4]{0:T(128)} %copy-done.4, bf16[256,256]{1,0:T(8,128)(2,1)} %copy-done, bf16[256,256]{1,0:T(8,128)(2,1)} %copy-done.1, f32[8192,128]{1,0:T(8,128)} %collective-permute-done.4.refs_0_, f32[8192,128]{1,0:T(8,128)} %collective-permute-done.5.refs_1_, ...), custom_call_target="tpu_custom_call" | custom-call | tf_op jit(solution)/shard_map/pallas_call | solution.py:355
  366.5 0.0 collective-permute-done.10.refs_0_
  366.5 0.0 collective-permute-done.11.refs_1_
  366.5 1.2 copy-done.8
  367.6 1.1 copy-done.9
  368.8 7.2 %shard_map.35.refs_5_ = f32[2,12288,128]{2,1,0:T(8,128)} custom-call(s32[4]{0:T(128)} %copy-done.4, bf16[256,256]{1,0:T(8,128)(2,1)} %copy-done, bf16[256,256]{1,0:T(8,128)(2,1)} %copy-done.1, f32[3072,128]{1,0:T(8,128)} %copy-done.8, f32[3072,128]{1,0:T(8,128)} %copy-done.9, ...), custom_call_target="tpu_custom_call", output_to_operand_aliasing={{}: (8, {})} | custom-call | tf_op jit(solution)/shard_map/pallas_call | solution.py:355
  375.9 0.0 collective-permute-done.8.refs_0_
  376.0 0.0 collective-permute-done.9.refs_1_
  376.0 0.8 copy-done.10
  376.7 5.2 %shard_map.36 = f32[2,12288,128]{2,1,0:T(8,128)} custom-call(s32[4]{0:T(128)} %copy-done.4, bf16[256,256]{1,0:T(8,128)(2,1)} %copy-done, bf16[256,256]{1,0:T(8,128)(2,1)} %copy-done.1, f32[1024,128]{1,0:T(8,128)} %copy-done.10, f32[1024,128]{1,0:T(8,128)} %collective-permute-done.9.refs_1_, ...), custom_call_target="tpu_custom_call", output_to_operand_aliasing={{}: (8, {})} | custom-call | tf_op jit(solution)/shard_map/pallas_call | solution.py:355
  (11 shorter events, 0.0 us)
Async XLA Ops:
  0.0 19.1 %copy-start.6 = (s32[2,4]{1,0:T(2,128)S(1)}, s32[2,4]{1,0:T(2,128)}, u32[]{:S(2)}) copy-start(s32[2,4]{1,0:T(2,128)} %offsets_ref.3) | copy-start | bytes 100
  11.0 1.5 collective-permute-start
  13.4 5.8 %collective-permute-start.1 = (f32[128,128]{1,0:T(8,128)S(1)}, f32[128,128]{1,0:T(8,128)S(1)}, u32[]{:S(2)}, u32[]{:S(2)}) collective-permute-start(f32[128,128]{1,0:T(8,128)S(1)} %add.14.one_ref), channel_id=1, source_target_pairs={{0,64},{32,96},{64,0},{96,32},{1,65},{33,97},{65,1},{97,33},{2,66}... | collective-permute-start | bytes 196616 | tf_op jit(solution)/shard_map/ppermute | solution.py:371
  16.7 6.6 %copy-start.4 = (s32[4]{0:T(128)}, s32[4]{0:T(128)S(1)}, u32[]{:S(2)}) copy-start(s32[4]{0:T(128)S(1)} %pad_add_fusion.flags_ref) | copy-start | bytes 52
  22.0 0.6 copy-start.2
  22.7 0.6 copy-start.3
  40.3 279.9 %collective-permute-start.4 = (f32[8192,128]{1,0:T(8,128)}, f32[8192,128]{1,0:T(8,128)}, u32[]{:S(2)}, u32[]{:S(2)}) collective-permute-start(f32[8192,128]{1,0:T(8,128)} %get-tuple-element.23.refs_2_), channel_id=1, source_target_pairs={{0,1},{1,2},{2,3},{3,4},{4,5},{5,6},{6,7},{7,8},{8,9},{9,10},{10,1... | collective-permute-start | bytes 12582920 | tf_op jit(solution)/shard_map/ppermute | solution.py:416
  45.8 282.1 %collective-permute-start.5 = (f32[8192,128]{1,0:T(8,128)}, f32[8192,128]{1,0:T(8,128)}, u32[]{:S(2)}, u32[]{:S(2)}) collective-permute-start(f32[8192,128]{1,0:T(8,128)} %get-tuple-element.24.refs_3_), channel_id=1, source_target_pairs={{1,0},{2,1},{3,2},{4,3},{5,4},{6,5},{7,6},{8,7},{9,8},{10,9},{11,1... | collective-permute-start | bytes 12582920 | tf_op jit(solution)/shard_map/ppermute | solution.py:417
  47.1 271.5 %collective-permute-start.2 = (f32[4096,128]{1,0:T(8,128)}, f32[4096,128]{1,0:T(8,128)S(1)}, u32[]{:S(2)}, u32[]{:S(2)}) collective-permute-start(f32[4096,128]{1,0:T(8,128)} %get-tuple-element.18), channel_id=1, source_target_pairs={{0,2},{2,4},{4,6},{6,8},{8,10},{10,12},{12,14},{14,16},{16,18},{18... | collective-permute-start | bytes 6291464 | tf_op jit(solution)/shard_map/ppermute | solution.py:418
  48.6 317.8 %collective-permute-start.10 = (f32[3072,128]{1,0:T(8,128)}, f32[3072,128]{1,0:T(8,128)S(1)}, u32[]{:S(2)}, u32[]{:S(2)}) collective-permute-start(f32[3072,128]{1,0:T(8,128)} %get-tuple-element.19.refs_1_.refs_2_), channel_id=1, source_target_pairs={{0,1},{1,2},{2,3},{3,4},{4,5},{5,6},{6,7},{7,8},{8,9},{9,10},{10,1... | collective-permute-start | bytes 4718600 | tf_op jit(solution)/shard_map/ppermute | solution.py:419
  51.8 314.6 %collective-permute-start.11 = (f32[3072,128]{1,0:T(8,128)}, f32[3072,128]{1,0:T(8,128)S(1)}, u32[]{:S(2)}, u32[]{:S(2)}) collective-permute-start(f32[3072,128]{1,0:T(8,128)} %get-tuple-element.20.refs_2_.refs_3_), channel_id=1, source_target_pairs={{2,1},{3,2},{4,3},{5,4},{6,5},{7,6},{8,7},{9,8},{10,9},{11,10},{12... | collective-permute-start | bytes 4718600 | tf_op jit(solution)/shard_map/ppermute | solution.py:420
  318.6 3.1 copy-start.7
  318.6 57.3 %collective-permute-start.8 = (f32[1024,128]{1,0:T(8,128)}, f32[1024,128]{1,0:T(8,128)S(1)}, u32[]{:S(2)}, u32[]{:S(2)}) collective-permute-start(f32[1024,128]{1,0:T(8,128)} %get-tuple-element.21.refs_3_.refs_2_), channel_id=1, source_target_pairs={{0,1},{1,2},{2,3},{3,4},{4,5},{5,6},{6,7},{7,8},{8,9},{9,10},{10,1... | collective-permute-start | bytes 1572872 | tf_op jit(solution)/shard_map/ppermute | solution.py:421
  320.2 55.8 %collective-permute-start.9 = (f32[1024,128]{1,0:T(8,128)}, f32[1024,128]{1,0:T(8,128)}, u32[]{:S(2)}, u32[]{:S(2)}) collective-permute-start(f32[1024,128]{1,0:T(8,128)} %get-tuple-element.22.refs_4_.refs_3_), channel_id=1, source_target_pairs={{2,1},{3,2},{4,3},{5,4},{6,5},{7,6},{8,7},{9,8},{10,9},{11,10},{12... | collective-permute-start | bytes 1572872 | tf_op jit(solution)/shard_map/ppermute | solution.py:422
  327.9 21.5 %copy-start.5 = (s32[4]{0:T(128)S(1)}, s32[4]{0:T(128)}, u32[]{:S(2)}) copy-start(s32[4]{0:T(128)} %copy-done.4) | copy-start | bytes 52
  327.9 12.3 %collective-permute-start.3 = (f32[128,128]{1,0:T(8,128)}, f32[128,128]{1,0:T(8,128)S(1)}, u32[]{:S(2)}, u32[]{:S(2)}) collective-permute-start(f32[128,128]{1,0:T(8,128)} %shard_map.31), channel_id=1, source_target_pairs={{2,1},{4,3},{6,5},{8,7},{10,9},{12,11},{14,13},{16,15},{18,17},{20... | collective-permute-start | bytes 196616 | tf_op jit(solution)/shard_map/ppermute | solution.py:425
  341.1 1.3 collective-permute-start.6
  342.4 7.1 %collective-permute-start.7 = (f32[128,128]{1,0:T(8,128)S(1)}, f32[128,128]{1,0:T(8,128)S(1)}, u32[]{:S(2)}, u32[]{:S(2)}) collective-permute-start(f32[128,128]{1,0:T(8,128)S(1)} %add.16.one_ref), channel_id=1, source_target_pairs={{0,64},{32,96},{64,0},{96,32},{1,65},{33,97},{65,1},{97,33},{2,66}... | collective-permute-start | bytes 196616 | tf_op jit(solution)/shard_map/ppermute | solution.py:371
  352.2 0.7 copy-start
  352.8 0.6 copy-start.1
  366.5 1.2 copy-start.8
  367.6 1.1 copy-start.9
  375.9 0.8 copy-start.10

commit v3 on v2

--- a/solution.py
+++ b/solution.py
@@ -11,6 +11,7 @@
 MIB = 1024 * 1024
 F32 = jnp.float32
 BF16 = jnp.bfloat16
+HINT = pl.CostEstimate(flops=1000, bytes_accessed=1000, transcendentals=0)
 
 
 def params(mib=58):
@@ -51,6 +52,11 @@
     return both[:, :width] + both[:, width:]
 
 
+def weights_of(v):
+    both = jnp.concatenate(parts(v), axis=1)
+    return jnp.concatenate([both, both], axis=0)
+
+
 def left_lanes(shape):
     return lax.broadcasted_iota(jnp.int32, shape, 1) < shape[1] // 2
 
@@ -78,11 +84,12 @@
         out_specs=pl.BlockSpec((width, width), lambda i: (0, 0)),
         out_shape=jax.ShapeDtypeStruct((width, width), F32),
         scratch_shapes=[pltpu.VMEM((width, 2 * width), F32)],
+        cost_estimate=HINT,
         compiler_params=params(),
     )(x)
 
 
-def rotation_kernel(which, flags_ref, offsets_ref, one_ref, two_ref, a_ref, b_ref):
+def rotation_kernel(which, flags_ref, offsets_ref, one_ref, two_ref, a_ref, b_ref, v_ref):
     gram = one_ref[...] + two_ref[...]
     width = gram.shape[0]
     half = width // 2
@@ -127,9 +134,9 @@
         other_vectors = swapped(vectors, 1)
     else:
         other_vectors = swapped(vectors, 0)
-    for out_ref, v in ((a_ref, vectors), (b_ref, other_vectors)):
-        both = jnp.concatenate(parts(v), axis=1)
-        out_ref[...] = jnp.concatenate([both, both], axis=0)
+    v_ref[...] = vectors
+    a_ref[...] = weights_of(vectors)
+    b_ref[...] = weights_of(other_vectors)
 
 
 def rotations(which, flags, offsets, one, two):
@@ -139,8 +146,10 @@
     return pl.pallas_call(
         functools.partial(rotation_kernel, which),
         in_specs=[smem, smem, vmem, vmem],
-        out_specs=[vmem, vmem],
-        out_shape=[jax.ShapeDtypeStruct((2 * width, 2 * width), BF16)] * 2,
+        out_specs=[vmem, vmem, vmem],
+        out_shape=[jax.ShapeDtypeStruct((2 * width, 2 * width), BF16)] * 2
+        + [jax.ShapeDtypeStruct((width, width), F32)],
+        cost_estimate=HINT,
         compiler_params=params(8),
     )(flags, offsets, one, two)
 
@@ -151,7 +160,7 @@
     )
 
 
-def first_product_kernel(runs, flags_ref, x_ref, a_ref, b_ref, *out_refs):
+def first_product_kernel(runs, skip, flags_ref, x_ref, a_ref, b_ref, *out_refs):
     ya = times(x_ref[0], a_ref[...])
     yb = times(x_ref[1], b_ref[...])
     left = left_lanes(ya.shape)
@@ -165,36 +174,141 @@
             out_refs[2 * which][...] = up
             out_refs[2 * which + 1][...] = down
 
-    @pl.when(step >= runs[0][1])
-    def _():
-        out_refs[-1][...] = jnp.where(flags_ref[2] == 1, down, up)
-
-
-def first_product(flags, x, a, b, block, runs):
-    _, rows, width = x.shape
-    steps = rows // block
-    first_run = runs[0][1]
+    if skip:
+        out_refs[2 * len(runs)][...] = jnp.where(flags_ref[2] == 1, down, up)
+
+
+def first_product(flags, x, a, b, start, block, runs, skip):
+    width = x.shape[2]
+    steps = sum(count for _, count in runs)
+    first = start // block
     whole = pl.BlockSpec(a.shape, lambda i, f: (0, 0))
     out_specs, out_shape = [], []
-    for low, count in runs + [(first_run, steps - first_run)]:
-        for _ in range(2 if len(out_specs) < 2 * len(runs) else 1):
-            out_specs.append(run_spec(low, count, block, width))
-            out_shape.append(jax.ShapeDtypeStruct((count * block, width), F32))
-    return pl.pallas_call(
-        functools.partial(first_product_kernel, runs),
+    for low, count in [run for run in runs for _ in range(2)] + [(0, steps)] * skip:
+        out_specs.append(run_spec(low, count, block, width))
+        out_shape.append(jax.ShapeDtypeStruct((count * block, width), F32))
+    return pl.pallas_call(
+        functools.partial(first_product_kernel, runs, skip),
         grid_spec=pltpu.PrefetchScalarGridSpec(
             num_scalar_prefetch=1,
             grid=(steps,),
             in_specs=[
-                pl.BlockSpec((2, block, width), lambda i, f: (0, i, 0)),
+                pl.BlockSpec((2, block, width), lambda i, f: (0, i + first, 0)),
                 whole,
                 whole,
             ],
             out_specs=out_specs,
         ),
         out_shape=out_shape,
+        cost_estimate=HINT,
         compiler_params=params(),
     )(flags, x, a, b)
+
+
+def gated_kernel(count, *refs):
+    refs[count][...] = refs[0][...]
+
+
+def gate(v, arrived, passed):
+    anywhere = pl.BlockSpec(memory_space=pl.ANY)
+    vmem = pl.BlockSpec(memory_space=pltpu.VMEM)
+    low = 1 + len(arrived)
+    return pl.pallas_call(
+        functools.partial(gated_kernel, low + len(passed)),
+        in_specs=[vmem] + [anywhere] * (len(arrived) + len(passed)),
+        out_specs=[vmem] + [anywhere] * len(passed),
+        out_shape=[jax.ShapeDtypeStruct(p.shape, p.dtype) for p in (v, *passed)],
+        input_output_aliases={low + k: 1 + k for k in range(len(passed))},
+        cost_estimate=HINT,
+        compiler_params=params(),
+    )(v, *arrived, *passed)
+
+
+def raw_pair_kernel(
+    flags_ref,
+    up_ref,
+    down_ref,
+    x_ref,
+    v_up_ref,
+    v_down_ref,
+    v_ref,
+    out_ref,
+    gram_ref,
+    terms_ref,
+):
+    step = pl.program_id(0)
+    bottom = flags_ref[0] == 1
+    top = flags_ref[1] == 1
+
+    @pl.when(step == 0)
+    def _():
+        terms_ref[...] = jnp.zeros_like(terms_ref)
+
+    own = swapped(v_ref[...], 1)
+    left = left_lanes(own.shape)
+    v_up = jnp.where(bottom, own, v_up_ref[...])
+    v_down = jnp.where(top, own, v_down_ref[...])
+    a = weights_of(jnp.where(left, v_up, 0.0))
+    b = weights_of(jnp.where(left, 0.0, v_down))
+    for side in range(2):
+        x = x_ref[side]
+        moved = times(jnp.where(bottom, x, up_ref[side]), a) + times(
+            jnp.where(top, x, down_ref[side]), b
+        )
+        out_ref[side] = moved
+        terms_ref[...] += gram_terms(moved)
+
+    @pl.when(step == pl.num_programs(0) - 1)
+    def _():
+        gram_ref[...] = gram_of_terms(terms_ref[...])
+
+
+def raw_pair(flags, up, down, x, start, v_up, v_down, v, block):
+    _, rows, width = up.shape
+    first = start // block
+    every = pl.BlockSpec((2, block, width), lambda i, f: (0, i, 0))
+    kept = pl.BlockSpec(
+        (2, block, width), lambda i, f: (0, first + i * (f[0] + f[1]), 0)
+    )
+    square = pl.BlockSpec((width, width), lambda i, f: (0, 0))
+    return pl.pallas_call(
+        raw_pair_kernel,
+        grid_spec=pltpu.PrefetchScalarGridSpec(
+            num_scalar_prefetch=1,
+            grid=(rows // block,),
+            in_specs=[every, every, kept, square, square, square],
+            out_specs=[every, square],
+            scratch_shapes=[pltpu.VMEM((width, 2 * width), F32)],
+        ),
+        out_shape=[
+            jax.ShapeDtypeStruct((2, rows, width), F32),
+            jax.ShapeDtypeStruct((width, width), F32),
+        ],
+        cost_estimate=HINT,
+        compiler_params=params(),
+    )(flags, up, down, x, v_up, v_down, v)
+
+
+def raw_product_kernel(x_ref, a_ref, out_ref):
+    for side in range(2):
+        out_ref[side] = times(x_ref[side], a_ref[...])
+
+
+def raw_product(x, a, start, total, block):
+    _, rows, width = x.shape
+    first = start // block
+    return pl.pallas_call(
+        raw_product_kernel,
+        grid=(rows // block,),
+        in_specs=[
+            pl.BlockSpec((2, block, width), lambda i: (0, i, 0)),
+            pl.BlockSpec(a.shape, lambda i: (0, 0)),
+        ],
+        out_specs=pl.BlockSpec((2, block, width), lambda i: (0, i + first, 0)),
+        out_shape=jax.ShapeDtypeStruct((2, total, width), F32),
+        cost_estimate=HINT,
+        compiler_params=params(),
+    )(x, a)
 
 
 def packed_gram_kernel(halves, flags_ref, *refs):
@@ -283,6 +397,7 @@
             scratch_shapes=[pltpu.VMEM((width, 2 * width), F32)] * 2,
         ),
         out_shape=jax.ShapeDtypeStruct((width, width), F32),
+        cost_estimate=HINT,
         compiler_params=params(),
     )(flags, *operands)
 
@@ -362,6 +477,7 @@
         ),
         out_shape=jax.ShapeDtypeStruct((2, total, width), F32),
         input_output_aliases=aliases,
+        cost_estimate=HINT,
         compiler_params=params(),
     )(flags, a, b, *operands)
 
@@ -371,17 +487,12 @@
     return lax.ppermute(x, "rows", [(i, i ^ bit) for i in range(size)])
 
 
-def body(block, x, offsets):
+def body(x, offsets):
     rows, width = x.shape
     half_rows = rows // 2
-    steps = half_rows // block
-    late = max(1, steps // 12)
-    middle = max(1, steps // 4)
-    runs = [
-        (0, steps - middle - late),
-        (steps - middle - late, middle),
-        (steps - late, late),
-    ]
+    unit = half_rows // 24
+    first, middle, final, raw = 7 * unit, 14 * unit, 21 * unit, 22 * unit
+    block = 7 * unit // 2
     place = lax.axis_index("loop")
     count = lax.axis_size("loop")
     last = count - 1
@@ -396,11 +507,6 @@
     )
     halves = x.reshape(2, half_rows, width)
 
-    gram = local_gram(x, 2 * block)
-    gram = gram + row_partner(gram, 1)
-    a, b = rotations(0, flags, offsets, gram, row_partner(gram, 2))
-    u1, w1, u2, w2, u3, w3, sent = first_product(flags, halves, a, b, block, runs)
-
     ups = [(i, i + 1) for i in range(last)]
     downs = [(i, i - 1) for i in range(1, count)]
     skips = (
@@ -413,45 +519,61 @@
         + [(i, i + 1) for i in range(1, last, 2)]
         + [(0, 0), (last, last)]
     )
+
+    bare = halves[:, raw:]
+    raw_up = lax.ppermute(bare, "loop", ups)
+    raw_down = lax.ppermute(bare, "loop", downs)
+
+    gram = local_gram(x, rows // 3)
+    gram = gram + row_partner(gram, 1)
+    a, b, v = rotations(0, flags, offsets, gram, row_partner(gram, 2))
+
+    *late, sent = first_product(
+        flags, halves, a, b, middle, unit, [(0, 7), (7, 1)], True
+    )
+    early = first_product(flags, halves, a, b, 0, block, [(0, 2), (2, 2)], False)
+    late_v, *sends = gate(v, [raw_up, raw_down], [*early, *late])
+    u0, w0, u1, w1, u2, w2, u3, w3 = sends
+    got = lax.ppermute(sent, "loop", skips)
+    up0 = lax.ppermute(u0, "loop", ups)
+    down0 = lax.ppermute(w0, "loop", downs)
     up1 = lax.ppermute(u1, "loop", ups)
     down1 = lax.ppermute(w1, "loop", downs)
-    got = lax.ppermute(sent, "loop", skips)
+    v_up = lax.ppermute(late_v, "loop", ups)
+    v_down = lax.ppermute(late_v, "loop", downs)
     up2 = lax.ppermute(u2, "loop", ups[:-1])
     down2 = lax.ppermute(w2, "loop", downs[1:])
     up3 = lax.ppermute(u3, "loop", ups[:-1])
     down3 = lax.ppermute(w3, "loop", downs[1:])
 
-    gram = neighbour_gram(flags, got, u2, w2, u3, w3, block)
+    gram = neighbour_gram(flags, got, u2, w2, u3, w3, unit)
     gram = lax.ppermute(gram, "loop", homes)
+    moved, raw_gram = raw_pair(
+        flags, raw_up, raw_down, halves, raw, v_up, v_down, v, unit
+    )
+    gram = gram + raw_gram + arrived_gram(flags, up0, down0, u0, w0, block)
     gram = gram + arrived_gram(flags, up1, down1, u1, w1, block)
     gram = gram + row_partner(gram, 1)
-    a, b = rotations(1, flags, offsets, gram, row_partner(gram, 2))
-
-    out = None
-    for (low, _), arrays, got_start, size in (
-        (runs[0], (up1, down1, u1, w1), None, block),
-        (runs[1], (up2, down2, u2, w2), 0, block),
-        (runs[2], (up3, down3, u3, w3), runs[1][1] * block, max(16, block // 4)),
+    a, b, _ = rotations(1, flags, offsets, gram, row_partner(gram, 2))
+
+    out = raw_product(moved, a, raw, half_rows, unit)
+    for arrays, got_start, start, size in (
+        ((up0, down0, u0, w0), None, 0, block),
+        ((up1, down1, u1, w1), None, first, block),
+        ((up2, down2, u2, w2), 0, middle, block),
+        ((up3, down3, u3, w3), final - middle, final, unit),
     ):
+        skipped = None if got_start is None else got
         out = second_product(
-            flags,
-            a,
-            b,
-            arrays,
-            None if got_start is None else got,
-            got_start or 0,
-            out,
-            low * block,
-            half_rows,
-            size,
+            flags, a, b, arrays, skipped, got_start or 0, out, start, half_rows, size
         )
     return out.reshape(rows, width)
 
 
-def solution(mesh, block=1024):
+def solution(mesh):
     placed = (P("rows", "loop"), P())
     return jax.shard_map(
-        functools.partial(body, block),
+        body,
         mesh=mesh,
         in_specs=placed,
         out_specs=P("rows", "loop"),

time: 383 us -> 485 us (1.27)
  the two profiles are of different devices: /device:TPU:0 before, /device:TPU:127 now
where the time goes in v3:
time: 485 us; the launch traced here: 484 us
  waiting for transfers between devices  352 us (73%)
  Pallas kernels  80 us (16%)
  starting transfers between devices  41.7 us (9%)
  local copies, waits for them, and re-layouts  8.3 us (2%)
    ppermute x1, waiting for transfers between devices, body(): v_up = lax.ppermute(late_v, 'loop', ups)  184 us
    ppermute x1, waiting for transfers between devices, body(): down1 = lax.ppermute(w1, 'loop', downs)  79.2 us
    ppermute x4, waiting for transfers between devices, row_partner(): return lax.ppermute(x, 'rows', [(i, i ^ bit) for i in range(size)])  71.8 us
    pallas_call x4, Pallas kernels, second_product(): pl.pallas_call(functools.partial(second_product_kernel, halves, count), g...  21.5 us
    pallas_call x3, Pallas kernels, gram_call(): pl.pallas_call(functools.partial(packed_gram_kernel, halves), grid_spec=p...  19 us
    pallas_call x2, Pallas kernels, first_product(): pl.pallas_call(functools.partial(first_product_kernel, runs, skip), grid_...  17.5 us
    ppermute x1, waiting for transfers between devices, body(): up1 = lax.ppermute(u1, 'loop', ups)  16.8 us
  transfers between devices with their start and end apart: 18, of which 7 were waited for; matrix products, arithmetic and copies ran while one was open for 0% of the time, Pallas kernels for 16%

profile of v3, /device:TPU:127, one launch (start us, length us, event | category | flops | bytes accessed | tf_op | source)
XLA Modules:
  0.0 483.5 jit_solution(1903166342785632634)
XLA Ops:
  0.0 2.3 slice.4
  2.3 1.4 collective-permute-start.3
  3.7 4.1 collective-permute-start.4
  7.8 6.8 %shard_map.28 = f32[128,128]{1,0:T(8,128)} custom-call(f32[24576,128]{1,0:T(8,128)} %x_ref.1), custom_call_target="tpu_custom_call" | custom-call | flops 1000 | bytes 1000 | tf_op jit(solution)/shard_map/pallas_call | solution.py:80
  14.5 1.2 collective-permute-start
  15.8 1.1 collective-permute-done
  16.9 0.9 add.20.one_ref
  17.7 1.0 collective-permute-start.1
  18.8 35.2 %collective-permute-done.1.two_ref = f32[128,128]{1,0:T(8,128)S(1)} collective-permute-done((f32[128,128]{1,0:T(8,128)S(1)}, f32[128,128]{1,0:T(8,128)S(1)}, u32[]{:S(2)}, u32[]{:S(2)}) %collective-permute-start.1) | collective-permute-done | bytes 65568 | tf_op jit(solution)/shard_map/ppermute | solution.py:487
  54.0 2.9 shard_map.29
  57.6 0.6 copy-done.3
  58.8 8.9 %shard_map.30 = (f32[3584,128]{1,0:T(8,128)}, f32[3584,128]{1,0:T(8,128)}, f32[512,128]{1,0:T(8,128)}, f32[512,128]{1,0:T(8,128)}, f32[4096,128]{1,0:T(8,128)}) custom-call(s32[4]{0:T(128)} %copy-done.5, f32[2,12288,128]{2,1,0:T(8,128)} %bitcast.7, bf16[256,256]{1,0:T(8,128)(2,1)} %copy-done.2, bf16[256,256]{1,0:T(8,128)(2,1)} %copy-done.3), custom_call_target="tpu_custom_call" | custom-call | flops 1000 | bytes 1000 | tf_op jit(solution)/shard_map/pallas_call | solution.py:190
  68.3 8.6 %shard_map.31 = (f32[3584,128]{1,0:T(8,128)}, f32[3584,128]{1,0:T(8,128)}, f32[3584,128]{1,0:T(8,128)}, f32[3584,128]{1,0:T(8,128)}) custom-call(s32[4]{0:T(128)} %copy-done.5, f32[2,12288,128]{2,1,0:T(8,128)} %bitcast.8, bf16[256,256]{1,0:T(8,128)(2,1)} %copy-done.2, bf16[256,256]{1,0:T(8,128)(2,1)} %copy-done.3), custom_call_target="tpu_custom_call" | custom-call | flops 1000 | bytes 1000 | tf_op jit(solution)/shard_map/pallas_call | solution.py:190
  76.9 1.0 copy-done.10
  78.3 1.5 shard_map.32
  79.7 1.3 collective-permute-start.8
  81.0 1.3 collective-permute-start.6
  82.3 4.6 collective-permute-start.7
  86.9 5.6 %collective-permute-start.9 = (f32[3584,128]{1,0:T(8,128)}, f32[3584,128]{1,0:T(8,128)}, u32[]{:S(2)}, u32[]{:S(2)}) collective-permute-start(f32[3584,128]{1,0:T(8,128)} %get-tuple-element.49.refs_3_), channel_id=1, source_target_pairs={{1,0},{2,1},{3,2},{4,3},{5,4},{6,5},{7,6},{8,7},{9,8},{10,9},{11,1... | collective-permute-start | bytes 5505032 | tf_op jit(solution)/shard_map/ppermute | solution.py:539
  92.5 183.7 %collective-permute-done.6.v_up_ref = f32[128,128]{1,0:T(8,128)S(1)} collective-permute-done((f32[128,128]{1,0:T(8,128)}, f32[128,128]{1,0:T(8,128)S(1)}, u32[]{:S(2)}, u32[]{:S(2)}) %collective-permute-start.6) | collective-permute-done | bytes 65568 | tf_op jit(solution)/shard_map/ppermute | solution.py:542
  276.2 1.3 collective-permute-start.10
  277.5 5.3 %collective-permute-start.11 = (f32[3584,128]{1,0:T(8,128)}, f32[3584,128]{1,0:T(8,128)}, u32[]{:S(2)}, u32[]{:S(2)}) collective-permute-start(f32[3584,128]{1,0:T(8,128)} %get-tuple-element.51.refs_3_), channel_id=1, source_target_pairs={{1,0},{2,1},{3,2},{4,3},{5,4},{6,5},{7,6},{8,7},{9,8},{10,9},{11,1... | collective-permute-start | bytes 5505032 | tf_op jit(solution)/shard_map/ppermute | solution.py:541
  282.8 1.9 collective-permute-start.16
  284.7 2.5 collective-permute-start.17
  287.2 8.2 %shard_map.33 = f32[128,128]{1,0:T(8,128)} custom-call(s32[4]{0:T(128)} %copy-done.5, f32[4096,128]{1,0:T(8,128)} %copy-done.8, f32[3584,128]{1,0:T(8,128)} %get-tuple-element.42.refs_1_.refs_2_, f32[3584,128]{1,0:T(8,128)} %get-tuple-element.43.refs_2_.refs_3_, f32[512,128]{1,0:T(8,128)} %get-tuple-element.44.refs_3_.refs_2_, ...), custom_call_target="tpu_custom_call" | custom-call | flops 1000 | bytes 1000 | tf_op jit(solution)/shard_map/pallas_call | solution.py:390
  295.4 1.5 collective-permute-start.5
  296.9 5.0 %shard_map.34 = (f32[2,1024,128]{2,1,0:T(8,128)}, f32[128,128]{1,0:T(8,128)}) custom-call(s32[4]{0:T(128)} %copy-done.5, f32[2,1024,128]{2,1,0:T(8,128)} %copy-done.10, f32[2,1024,128]{2,1,0:T(8,128)} %copy-done.11, f32[2,12288,128]{2,1,0:T(8,128)} %bitcast.9, f32[128,128]{1,0:T(8,128)} %copy-done.17, f32[128,128]{1,0:T(8,128)} %copy-done.18, ...), custom_call_target="tpu_custom_call" | custom-call | flops 1000 | bytes 1000 | tf_op jit(solution)/shard_map/pallas_call | solution.py:274
  301.9 5.5 %shard_map.35 = f32[128,128]{1,0:T(8,128)} custom-call(s32[4]{0:T(128)} %copy-done.5, f32[3584,128]{1,0:T(8,128)} %copy-done.9, f32[3584,128]{1,0:T(8,128)} %collective-permute-done.9.refs_1_, f32[3584,128]{1,0:T(8,128)} %get-tuple-element.48.refs_2_, f32[3584,128]{1,0:T(8,128)} %get-tuple-element.49.refs_3_), custom_call_target="tpu_custom_call" | custom-call | flops 1000 | bytes 1000 | tf_op jit(solution)/shard_map/pallas_call | solution.py:390
  307.3 16.8 %collective-permute-done.10.refs_0_ = f32[3584,128]{1,0:T(8,128)} collective-permute-done((f32[3584,128]{1,0:T(8,128)}, f32[3584,128]{1,0:T(8,128)}, u32[]{:S(2)}, u32[]{:S(2)}) %collective-permute-start.10) | collective-permute-done | bytes 1835040 | tf_op jit(solution)/shard_map/ppermute | solution.py:540
  324.2 0.7 collective-permute-start.14
  324.8 79.2 %collective-permute-done.11.refs_1_ = f32[3584,128]{1,0:T(8,128)} collective-permute-done((f32[3584,128]{1,0:T(8,128)}, f32[3584,128]{1,0:T(8,128)}, u32[]{:S(2)}, u32[]{:S(2)}) %collective-permute-start.11) | collective-permute-done | bytes 1835040 | tf_op jit(solution)/shard_map/ppermute | solution.py:541
  404.1 4.1 collective-permute-start.15
  408.2 5.3 %shard_map.36 = f32[128,128]{1,0:T(8,128)} custom-call(s32[4]{0:T(128)} %copy-done.5, f32[3584,128]{1,0:T(8,128)} %collective-permute-done.10.refs_0_, f32[3584,128]{1,0:T(8,128)} %collective-permute-done.11.refs_1_, f32[3584,128]{1,0:T(8,128)} %get-tuple-element.50.refs_2_, f32[3584,128]{1,0:T(8,128)} %get-tuple-element.51.refs_3_), custom_call_target="tpu_custom_call" | custom-call | flops 1000 | bytes 1000 | tf_op jit(solution)/shard_map/pallas_call | solution.py:390
  413.5 0.9 add_add_fusion
  414.4 0.9 collective-permute-start.12
  415.4 0.9 collective-permute-done.12
  416.3 2.6 collective-permute-start.13
  418.9 34.5 %collective-permute-done.13.two_ref = f32[128,128]{1,0:T(8,128)S(1)} collective-permute-done((f32[128,128]{1,0:T(8,128)S(1)}, f32[128,128]{1,0:T(8,128)S(1)}, u32[]{:S(2)}, u32[]{:S(2)}) %collective-permute-start.13) | collective-permute-done | bytes 65568 | tf_op jit(solution)/shard_map/ppermute | solution.py:487
  453.4 3.4 shard_map.37
  456.7 0.7 copy-done
  457.4 0.7 copy-done.1
  458.0 2.5 shard_map.38.refs_4_
  460.5 6.0 %shard_map.39.refs_4_ = f32[2,12288,128]{2,1,0:T(8,128)} custom-call(s32[4]{0:T(128)} %copy-done.5, bf16[256,256]{1,0:T(8,128)(2,1)} %copy-done, bf16[256,256]{1,0:T(8,128)(2,1)} %copy-done.1, f32[3584,128]{1,0:T(8,128)} %copy-done.9, f32[3584,128]{1,0:T(8,128)} %collective-permute-done.9.refs_1_, ...), custom_call_target="tpu_custom_call", output_to_operand_aliasing={{}: (7, {})} | custom-call | flops 1000 | bytes 1000 | tf_op jit(solution)/shard_map/pallas_call | solution.py:470
  466.5 6.0 %shard_map.40.refs_5_ = f32[2,12288,128]{2,1,0:T(8,128)} custom-call(s32[4]{0:T(128)} %copy-done.5, bf16[256,256]{1,0:T(8,128)(2,1)} %copy-done, bf16[256,256]{1,0:T(8,128)(2,1)} %copy-done.1, f32[3584,128]{1,0:T(8,128)} %collective-permute-done.10.refs_0_, f32[3584,128]{1,0:T(8,128)} %collective-permute-done.11.refs_1_, ...), custom_call_target="tpu_custom_call", output_to_operand_aliasing={{}: (7, {})} | custom-call | flops 1000 | bytes 1000 | tf_op jit(solution)/shard_map/pallas_call | solution.py:470
  472.5 6.4 %shard_map.41.refs_5_ = f32[2,12288,128]{2,1,0:T(8,128)} custom-call(s32[4]{0:T(128)} %copy-done.5, bf16[256,256]{1,0:T(8,128)(2,1)} %copy-done, bf16[256,256]{1,0:T(8,128)(2,1)} %copy-done.1, f32[3584,128]{1,0:T(8,128)} %collective-permute-done.16.refs_0_, f32[3584,128]{1,0:T(8,128)} %collective-permute-done.17.refs_1_, ...), custom_call_target="tpu_custom_call", output_to_operand_aliasing={{}: (8, {})} | custom-call | flops 1000 | bytes 1000 | tf_op jit(solution)/shard_map/pallas_call | solution.py:470
  478.9 0.7 copy-done.14
  479.6 0.7 copy-done.15
  480.3 3.2 shard_map.42
  (48 shorter events, 2.3 us)
Async XLA Ops:
  2.3 51.7 %copy-start.7 = (s32[2,4]{1,0:T(2,128)S(1)}, s32[2,4]{1,0:T(2,128)}, u32[]{:S(2)}) copy-start(s32[2,4]{1,0:T(2,128)} %offsets_ref.3) | copy-start | bytes 100
  2.3 74.6 %collective-permute-start.3 = (f32[2,1024,128]{2,1,0:T(8,128)}, f32[2,1024,128]{2,1,0:T(8,128)S(1)}, u32[]{:S(2)}, u32[]{:S(2)}) collective-permute-start(f32[2,1024,128]{2,1,0:T(8,128)} %slice.4), channel_id=1, source_target_pairs={{0,1},{1,2},{2,3},{3,4},{4,5},{5,6},{6,7},{7,8},{8,9},{9,10},{10,1... | collective-permute-start | bytes 3145736 | tf_op jit(solution)/shard_map/ppermute | solution.py:524
  3.7 73.2 %collective-permute-start.4 = (f32[2,1024,128]{2,1,0:T(8,128)}, f32[2,1024,128]{2,1,0:T(8,128)S(1)}, u32[]{:S(2)}, u32[]{:S(2)}) collective-permute-start(f32[2,1024,128]{2,1,0:T(8,128)} %slice.4), channel_id=1, source_target_pairs={{1,0},{2,1},{3,2},{4,3},{5,4},{6,5},{7,6},{8,7},{9,8},{10,9},{11,1... | collective-permute-start | bytes 3145736 | tf_op jit(solution)/shard_map/ppermute | solution.py:525
  14.5 2.3 collective-permute-start
  17.7 36.3 %collective-permute-start.1 = (f32[128,128]{1,0:T(8,128)S(1)}, f32[128,128]{1,0:T(8,128)S(1)}, u32[]{:S(2)}, u32[]{:S(2)}) collective-permute-start(f32[128,128]{1,0:T(8,128)S(1)} %add.20.one_ref), channel_id=1, source_target_pairs={{0,64},{32,96},{64,0},{96,32},{1,65},{33,97},{65,1},{97,33},{2,66}... | collective-permute-start | bytes 196616 | tf_op jit(solution)/shard_map/ppermute | solution.py:487
  18.8 40.1 %copy-start.5 = (s32[4]{0:T(128)}, s32[4]{0:T(128)S(1)}, u32[]{:S(2)}) copy-start(s32[4]{0:T(128)S(1)} %pad_add_fusion.flags_ref) | copy-start | bytes 52
  56.9 0.7 copy-start.2
  57.6 0.6 copy-start.3
  58.2 0.6 copy-start.4
  67.8 215.0 %collective-permute-start.2 = (f32[4096,128]{1,0:T(8,128)}, f32[4096,128]{1,0:T(8,128)S(1)}, u32[]{:S(2)}, u32[]{:S(2)}) collective-permute-start(f32[4096,128]{1,0:T(8,128)} %get-tuple-element.32), channel_id=1, source_target_pairs={{0,2},{2,4},{4,6},{6,8},{8,10},{10,12},{12,14},{14,16},{16,18},{18... | collective-permute-start | bytes 6291464 | tf_op jit(solution)/shard_map/ppermute | solution.py:537
  76.9 1.1 copy-start.10
  76.9 1.4 copy-start.11
  79.7 205.0 %collective-permute-start.8 = (f32[3584,128]{1,0:T(8,128)}, f32[3584,128]{1,0:T(8,128)S(1)}, u32[]{:S(2)}, u32[]{:S(2)}) collective-permute-start(f32[3584,128]{1,0:T(8,128)} %get-tuple-element.48.refs_2_), channel_id=1, source_target_pairs={{0,1},{1,2},{2,3},{3,4},{4,5},{5,6},{6,7},{7,8},{8,9},{9,10},{10,1... | collective-permute-start | bytes 5505032 | tf_op jit(solution)/shard_map/ppermute | solution.py:538
  81.0 195.2 %collective-permute-start.6 = (f32[128,128]{1,0:T(8,128)}, f32[128,128]{1,0:T(8,128)S(1)}, u32[]{:S(2)}, u32[]{:S(2)}) collective-permute-start(f32[128,128]{1,0:T(8,128)} %get-tuple-element.46), channel_id=1, source_target_pairs={{0,1},{1,2},{2,3},{3,4},{4,5},{5,6},{6,7},{7,8},{8,9},{9,10},{10,1... | collective-permute-start | bytes 196616 | tf_op jit(solution)/shard_map/ppermute | solution.py:542
  82.3 195.2 %collective-permute-start.7 = (f32[128,128]{1,0:T(8,128)}, f32[128,128]{1,0:T(8,128)S(1)}, u32[]{:S(2)}, u32[]{:S(2)}) collective-permute-start(f32[128,128]{1,0:T(8,128)} %get-tuple-element.46), channel_id=1, source_target_pairs={{1,0},{2,1},{3,2},{4,3},{5,4},{6,5},{7,6},{8,7},{9,8},{10,9},{11,1... | collective-permute-start | bytes 196616 | tf_op jit(solution)/shard_map/ppermute | solution.py:543
  86.9 208.4 %collective-permute-start.9 = (f32[3584,128]{1,0:T(8,128)}, f32[3584,128]{1,0:T(8,128)}, u32[]{:S(2)}, u32[]{:S(2)}) collective-permute-start(f32[3584,128]{1,0:T(8,128)} %get-tuple-element.49.refs_3_), channel_id=1, source_target_pairs={{1,0},{2,1},{3,2},{4,3},{5,4},{6,5},{7,6},{8,7},{9,8},{10,9},{11,1... | collective-permute-start | bytes 5505032 | tf_op jit(solution)/shard_map/ppermute | solution.py:539
  276.2 20.7 %copy-start.17 = (f32[128,128]{1,0:T(8,128)}, f32[128,128]{1,0:T(8,128)S(1)}, u32[]{:S(2)}) copy-start(f32[128,128]{1,0:T(8,128)S(1)} %collective-permute-done.6.v_up_ref) | copy-start | bytes 196612
  276.2 48.0 %collective-permute-start.10 = (f32[3584,128]{1,0:T(8,128)}, f32[3584,128]{1,0:T(8,128)}, u32[]{:S(2)}, u32[]{:S(2)}) collective-permute-start(f32[3584,128]{1,0:T(8,128)} %get-tuple-element.50.refs_2_), channel_id=1, source_target_pairs={{0,1},{1,2},{2,3},{3,4},{4,5},{5,6},{6,7},{7,8},{8,9},{9,10},{10,1... | collective-permute-start | bytes 5505032 | tf_op jit(solution)/shard_map/ppermute | solution.py:540
  277.5 19.4 %copy-start.18 = (f32[128,128]{1,0:T(8,128)}, f32[128,128]{1,0:T(8,128)S(1)}, u32[]{:S(2)}) copy-start(f32[128,128]{1,0:T(8,128)S(1)} %collective-permute-done.7.v_down_ref) | copy-start | bytes 196612
  277.5 126.6 %collective-permute-start.11 = (f32[3584,128]{1,0:T(8,128)}, f32[3584,128]{1,0:T(8,128)}, u32[]{:S(2)}, u32[]{:S(2)}) collective-permute-start(f32[3584,128]{1,0:T(8,128)} %get-tuple-element.51.refs_3_), channel_id=1, source_target_pairs={{1,0},{2,1},{3,2},{4,3},{5,4},{6,5},{7,6},{8,7},{9,8},{10,9},{11,1... | collective-permute-start | bytes 5505032 | tf_op jit(solution)/shard_map/ppermute | solution.py:541
  282.8 4.4 copy-start.8
  282.8 189.8 %collective-permute-start.16 = (f32[3584,128]{1,0:T(8,128)}, f32[3584,128]{1,0:T(8,128)}, u32[]{:S(2)}, u32[]{:S(2)}) collective-permute-start(f32[3584,128]{1,0:T(8,128)} %get-tuple-element.42.refs_1_.refs_2_), channel_id=1, source_target_pairs={{0,1},{1,2},{2,3},{3,4},{4,5},{5,6},{6,7},{7,8},{8,9},{9,10},{10,1... | collective-permute-start | bytes 5505032 | tf_op jit(solution)/shard_map/ppermute | solution.py:544
  284.7 10.7 %copy-start.9 = (f32[3584,128]{1,0:T(8,128)}, f32[3584,128]{1,0:T(8,128)S(1)}, u32[]{:S(2)}) copy-start(f32[3584,128]{1,0:T(8,128)S(1)} %collective-permute-done.8.refs_0_) | copy-start | bytes 5505028
  284.7 187.8 %collective-permute-start.17 = (f32[3584,128]{1,0:T(8,128)}, f32[3584,128]{1,0:T(8,128)}, u32[]{:S(2)}, u32[]{:S(2)}) collective-permute-start(f32[3584,128]{1,0:T(8,128)} %get-tuple-element.43.refs_2_.refs_3_), channel_id=1, source_target_pairs={{2,1},{3,2},{4,3},{5,4},{6,5},{7,6},{8,7},{9,8},{10,9},{11,10},{12... | collective-permute-start | bytes 5505032 | tf_op jit(solution)/shard_map/ppermute | solution.py:545
  295.4 118.2 %collective-permute-start.5 = (f32[128,128]{1,0:T(8,128)}, f32[128,128]{1,0:T(8,128)S(1)}, u32[]{:S(2)}, u32[]{:S(2)}) collective-permute-start(f32[128,128]{1,0:T(8,128)} %shard_map.33), channel_id=1, source_target_pairs={{2,1},{4,3},{6,5},{8,7},{10,9},{12,11},{14,13},{16,15},{18,17},{20... | collective-permute-start | bytes 196616 | tf_op jit(solution)/shard_map/ppermute | solution.py:550
  301.9 22.3 %copy-start.12 = (f32[512,128]{1,0:T(8,128)S(1)}, f32[512,128]{1,0:T(8,128)}, u32[]{:S(2)}) copy-start(f32[512,128]{1,0:T(8,128)} %get-tuple-element.44.refs_3_.refs_2_) | copy-start | bytes 786436
  301.9 102.2 %copy-start.13 = (f32[512,128]{1,0:T(8,128)S(1)}, f32[512,128]{1,0:T(8,128)}, u32[]{:S(2)}) copy-start(f32[512,128]{1,0:T(8,128)} %get-tuple-element.45.refs_4_.refs_3_) | copy-start | bytes 786436
  307.3 106.2 %copy-start.16 = (f32[128,128]{1,0:T(8,128)S(1)}, f32[128,128]{1,0:T(8,128)}, u32[]{:S(2)}) copy-start(f32[128,128]{1,0:T(8,128)} %shard_map.35) | copy-start | bytes 196612
  307.3 106.2 %copy-start.19 = (f32[128,128]{1,0:T(8,128)S(1)}, f32[128,128]{1,0:T(8,128)}, u32[]{:S(2)}) copy-start(f32[128,128]{1,0:T(8,128)} %get-tuple-element.47) | copy-start | bytes 196612
  307.3 146.0 %copy-start.6 = (s32[4]{0:T(128)S(1)}, s32[4]{0:T(128)}, u32[]{:S(2)}) copy-start(s32[4]{0:T(128)} %copy-done.5) | copy-start | bytes 52
  324.2 154.7 %collective-permute-start.14 = (f32[512,128]{1,0:T(8,128)S(1)}, f32[512,128]{1,0:T(8,128)S(1)}, u32[]{:S(2)}, u32[]{:S(2)}) collective-permute-start(f32[512,128]{1,0:T(8,128)S(1)} %copy-done.12), channel_id=1, source_target_pairs={{0,1},{1,2},{2,3},{3,4},{4,5},{5,6},{6,7},{7,8},{8,9},{9,10},{10,1... | collective-permute-start | bytes 786440 | tf_op jit(solution)/shard_map/ppermute | solution.py:546
  404.1 74.8 %collective-permute-start.15 = (f32[512,128]{1,0:T(8,128)S(1)}, f32[512,128]{1,0:T(8,128)S(1)}, u32[]{:S(2)}, u32[]{:S(2)}) collective-permute-start(f32[512,128]{1,0:T(8,128)S(1)} %copy-done.13), channel_id=1, source_target_pairs={{2,1},{3,2},{4,3},{5,4},{6,5},{7,6},{8,7},{9,8},{10,9},{11,10},{12... | collective-permute-start | bytes 786440 | tf_op jit(solution)/shard_map/ppermute | solution.py:547
  414.4 1.8 collective-permute-start.12
  416.3 37.1 %collective-permute-start.13 = (f32[128,128]{1,0:T(8,128)S(1)}, f32[128,128]{1,0:T(8,128)S(1)}, u32[]{:S(2)}, u32[]{:S(2)}) collective-permute-start(f32[128,128]{1,0:T(8,128)S(1)} %add.24.one_ref), channel_id=1, source_target_pairs={{0,64},{32,96},{64,0},{96,32},{1,65},{33,97},{65,1},{97,33},{2,66}... | collective-permute-start | bytes 196616 | tf_op jit(solution)/shard_map/ppermute | solution.py:487
  456.7 0.7 copy-start
  457.4 0.7 copy-start.1
  478.9 0.7 copy-start.14
  479.6 0.7 copy-start.15

commit v4 on v2

--- a/solution.py
+++ b/solution.py
@@ -11,6 +11,7 @@
 MIB = 1024 * 1024
 F32 = jnp.float32
 BF16 = jnp.bfloat16
+HINT = pl.CostEstimate(flops=1000, bytes_accessed=1000, transcendentals=0)
 
 
 def params(mib=58):
@@ -49,6 +50,11 @@
         jnp.concatenate(parts(x), axis=1), weights, preferred_element_type=F32
     )
     return both[:, :width] + both[:, width:]
+
+
+def weights_of(v):
+    both = jnp.concatenate(parts(v), axis=1)
+    return jnp.concatenate([both, both], axis=0)
 
 
 def left_lanes(shape):
@@ -78,6 +84,7 @@
         out_specs=pl.BlockSpec((width, width), lambda i: (0, 0)),
         out_shape=jax.ShapeDtypeStruct((width, width), F32),
         scratch_shapes=[pltpu.VMEM((width, 2 * width), F32)],
+        cost_estimate=HINT,
         compiler_params=params(),
     )(x)
 
@@ -127,9 +134,8 @@
         other_vectors = swapped(vectors, 1)
     else:
         other_vectors = swapped(vectors, 0)
-    for out_ref, v in ((a_ref, vectors), (b_ref, other_vectors)):
-        both = jnp.concatenate(parts(v), axis=1)
-        out_ref[...] = jnp.concatenate([both, both], axis=0)
+    a_ref[...] = weights_of(vectors)
+    b_ref[...] = weights_of(other_vectors)
 
 
 def rotations(which, flags, offsets, one, two):
@@ -141,6 +147,7 @@
         in_specs=[smem, smem, vmem, vmem],
         out_specs=[vmem, vmem],
         out_shape=[jax.ShapeDtypeStruct((2 * width, 2 * width), BF16)] * 2,
+        cost_estimate=HINT,
         compiler_params=params(8),
     )(flags, offsets, one, two)
 
@@ -151,7 +158,7 @@
     )
 
 
-def first_product_kernel(runs, flags_ref, x_ref, a_ref, b_ref, *out_refs):
+def first_product_kernel(runs, skip, flags_ref, x_ref, a_ref, b_ref, _, *out_refs):
     ya = times(x_ref[0], a_ref[...])
     yb = times(x_ref[1], b_ref[...])
     left = left_lanes(ya.shape)
@@ -165,36 +172,36 @@
             out_refs[2 * which][...] = up
             out_refs[2 * which + 1][...] = down
 
-    @pl.when(step >= runs[0][1])
-    def _():
-        out_refs[-1][...] = jnp.where(flags_ref[2] == 1, down, up)
-
-
-def first_product(flags, x, a, b, block, runs):
-    _, rows, width = x.shape
-    steps = rows // block
-    first_run = runs[0][1]
+    if skip:
+        out_refs[2 * len(runs)][...] = jnp.where(flags_ref[2] == 1, down, up)
+
+
+def first_product(flags, x, a, b, earlier, start, block, runs, skip):
+    width = x.shape[2]
+    steps = sum(count for _, count in runs)
+    first = start // block
     whole = pl.BlockSpec(a.shape, lambda i, f: (0, 0))
     out_specs, out_shape = [], []
-    for low, count in runs + [(first_run, steps - first_run)]:
-        for _ in range(2 if len(out_specs) < 2 * len(runs) else 1):
-            out_specs.append(run_spec(low, count, block, width))
-            out_shape.append(jax.ShapeDtypeStruct((count * block, width), F32))
+    for low, count in [run for run in runs for _ in range(2)] + [(0, steps)] * skip:
+        out_specs.append(run_spec(low, count, block, width))
+        out_shape.append(jax.ShapeDtypeStruct((count * block, width), F32))
     return pl.pallas_call(
-        functools.partial(first_product_kernel, runs),
+        functools.partial(first_product_kernel, runs, skip),
         grid_spec=pltpu.PrefetchScalarGridSpec(
             num_scalar_prefetch=1,
             grid=(steps,),
             in_specs=[
-                pl.BlockSpec((2, block, width), lambda i, f: (0, i, 0)),
+                pl.BlockSpec((2, block, width), lambda i, f: (0, i + first, 0)),
                 whole,
                 whole,
+                pl.BlockSpec(memory_space=pl.ANY),
             ],
             out_specs=out_specs,
         ),
         out_shape=out_shape,
+        cost_estimate=HINT,
         compiler_params=params(),
-    )(flags, x, a, b)
+    )(flags, x, a, b, earlier)
 
 
 def packed_gram_kernel(halves, flags_ref, *refs):
@@ -283,6 +290,7 @@
             scratch_shapes=[pltpu.VMEM((width, 2 * width), F32)] * 2,
         ),
         out_shape=jax.ShapeDtypeStruct((width, width), F32),
+        cost_estimate=HINT,
         compiler_params=params(),
     )(flags, *operands)
 
@@ -362,6 +370,7 @@
         ),
         out_shape=jax.ShapeDtypeStruct((2, total, width), F32),
         input_output_aliases=aliases,
+        cost_estimate=HINT,
         compiler_params=params(),
     )(flags, a, b, *operands)
 
@@ -371,17 +380,49 @@
     return lax.ppermute(x, "rows", [(i, i ^ bit) for i in range(size)])
 
 
-def body(block, x, offsets):
+def everywhere(x, target):
+    rows, places = lax.axis_size("rows"), lax.axis_size("loop")
+    pairs = []
+    for row in range(rows):
+        for place in range(places):
+            where = target(row, place)
+            pairs.append((row * places + place, where[0] * places + where[1]))
+    return lax.ppermute(x, ("rows", "loop"), pairs)
+
+
+def home(x, last):
+    def onward(row, place):
+        if place == 1:
+            return row ^ 2, 0
+        if place == last - 1:
+            return row ^ 2, last
+        return row, place - 2 if place % 2 else place + 2
+
+    x = everywhere(x, lambda row, place: (row ^ 2, place ^ 1))
+    return everywhere(x, onward)
+
+
+def far_partner(x, count):
+    ring = min(4, count // 2)
+
+    def along(place):
+        pair, odd = divmod(place, 2)
+        group, at = divmod(pair, ring)
+        at = (at - 1) % ring if odd else (at + 1) % ring
+        return 2 * (group * ring + at) + odd
+
+    x = everywhere(x, lambda row, place: (row ^ 2, along(place)))
+    for _ in range(ring - 1):
+        x = everywhere(x, lambda row, place: (row, along(place)))
+    return x
+
+
+def body(x, offsets):
     rows, width = x.shape
     half_rows = rows // 2
-    steps = half_rows // block
-    late = max(1, steps // 12)
-    middle = max(1, steps // 4)
-    runs = [
-        (0, steps - middle - late),
-        (steps - middle - late, middle),
-        (steps - late, late),
-    ]
+    small = half_rows // 12
+    large = 5 * small // 2
+    middle, late, final = 2 * large, 9 * small, 11 * small
     place = lax.axis_index("loop")
     count = lax.axis_size("loop")
     last = count - 1
@@ -396,11 +437,6 @@
     )
     halves = x.reshape(2, half_rows, width)
 
-    gram = local_gram(x, 2 * block)
-    gram = gram + row_partner(gram, 1)
-    a, b = rotations(0, flags, offsets, gram, row_partner(gram, 2))
-    u1, w1, u2, w2, u3, w3, sent = first_product(flags, halves, a, b, block, runs)
-
     ups = [(i, i + 1) for i in range(last)]
     downs = [(i, i - 1) for i in range(1, count)]
     skips = (
@@ -408,50 +444,50 @@
         + [(i, i - 2) for i in range(3, count, 2)]
         + [(1, 0), (last - 1, last)]
     )
-    homes = (
-        [(i, i - 1) for i in range(2, count, 2)]
-        + [(i, i + 1) for i in range(1, last, 2)]
-        + [(0, 0), (last, last)]
-    )
+
+    gram = local_gram(x, rows // 3)
+    gram = gram + row_partner(gram, 1)
+    a, b = rotations(0, flags, offsets, gram, row_partner(gram, 2))
+
+    u2, w2, u3, w3, sent = first_product(
+        flags, halves, a, b, halves, late, small, [(0, 2), (2, 1)], True
+    )
+    got = lax.ppermute(sent, "loop", skips)
+    u0, w0 = first_product(flags, halves, a, b, sent, 0, large, [(0, 2)], False)
+    up0 = lax.ppermute(u0, "loop", ups)
+    down0 = lax.ppermute(w0, "loop", downs)
+    u1, w1 = first_product(flags, halves, a, b, got, middle, small, [(0, 4)], False)
     up1 = lax.ppermute(u1, "loop", ups)
     down1 = lax.ppermute(w1, "loop", downs)
-    got = lax.ppermute(sent, "loop", skips)
     up2 = lax.ppermute(u2, "loop", ups[:-1])
     down2 = lax.ppermute(w2, "loop", downs[1:])
     up3 = lax.ppermute(u3, "loop", ups[:-1])
     down3 = lax.ppermute(w3, "loop", downs[1:])
 
-    gram = neighbour_gram(flags, got, u2, w2, u3, w3, block)
-    gram = lax.ppermute(gram, "loop", homes)
-    gram = gram + arrived_gram(flags, up1, down1, u1, w1, block)
+    gram = home(neighbour_gram(flags, got, u2, w2, u3, w3, small), last)
+    gram = gram + arrived_gram(flags, up0, down0, u0, w0, large)
+    gram = gram + arrived_gram(flags, up1, down1, u1, w1, small)
     gram = gram + row_partner(gram, 1)
-    a, b = rotations(1, flags, offsets, gram, row_partner(gram, 2))
+    a, b = rotations(1, flags, offsets, gram, far_partner(gram, count))
 
     out = None
-    for (low, _), arrays, got_start, size in (
-        (runs[0], (up1, down1, u1, w1), None, block),
-        (runs[1], (up2, down2, u2, w2), 0, block),
-        (runs[2], (up3, down3, u3, w3), runs[1][1] * block, max(16, block // 4)),
+    for arrays, got_start, low, size in (
+        ((up0, down0, u0, w0), None, 0, large),
+        ((up1, down1, u1, w1), None, middle, small),
+        ((up2, down2, u2, w2), 0, late, small),
+        ((up3, down3, u3, w3), final - late, final, small),
     ):
+        skipped = None if got_start is None else got
         out = second_product(
-            flags,
-            a,
-            b,
-            arrays,
-            None if got_start is None else got,
-            got_start or 0,
-            out,
-            low * block,
-            half_rows,
-            size,
+            flags, a, b, arrays, skipped, got_start or 0, out, low, half_rows, size
         )
     return out.reshape(rows, width)
 
 
-def solution(mesh, block=1024):
+def solution(mesh):
     placed = (P("rows", "loop"), P())
     return jax.shard_map(
-        functools.partial(body, block),
+        body,
         mesh=mesh,
         in_specs=placed,
         out_specs=P("rows", "loop"),

time: 383 us -> 364 us (0.950)
  waiting for transfers between devices: 275 us -> 249 us
  starting transfers between devices: 23.4 us -> 30.3 us
    ppermute x1, waiting for transfers between devices: 266 us -> 49.2 us  [body(): got = lax.ppermute(sent, 'loop', skips)]
    ppermute x1 -> x8, waiting for transfers between devices: 0.01 us -> 152 us  [the longest x1 82.2 us: body(): up0 = lax.ppermute(u0, 'loop', ups)]
    ppermute x1, waiting for transfers between devices: 0.01 us -> 31.1 us  [body(): down1 = lax.ppermute(w1, 'loop', downs)]
    ppermute x1, waiting for transfers between devices: 0.01 us -> 12.3 us  [body(): up1 = lax.ppermute(u1, 'loop', ups)]
    ppermute x1 -> x8, starting transfers between devices: 1.5 us -> 12.6 us  [the longest x6 8.83 us: everywhere(): return lax.ppermute(x, ('rows', 'loop'), pairs)]
    pallas_call x1, Pallas kernels: 11 us -> 6.78 us  [local_gram(): pl.pallas_call(gram_kernel, grid=(rows // block,), in_specs=[pl.BlockSpec...]
    ppermute x1, starting transfers between devices: 5.55 us -> 1.54 us  [body(): up1 = lax.ppermute(u1, 'loop', ups)]
    ppermute x4 -> x3, waiting for transfers between devices: 8.92 us -> 5.12 us  [row_partner(): return lax.ppermute(x, 'rows', [(i, i ^ bit) for i in range(size)])]
  transfers between devices with their start and end apart: 12 -> 18, of which waited for: 5 -> 13; matrix products, arithmetic and copies ran while one was open for 0% -> 0% of each run, Pallas kernels for 10% -> 15%
where the time goes in v4:
time: 364 us; the launch traced here: 360 us
  waiting for transfers between devices  249 us (68%)
  Pallas kernels  73.3 us (20%)
  starting transfers between devices  30.3 us (8%)
  local copies, waits for them, and re-layouts  5.38 us (1%)
    ppermute x1, waiting for transfers between devices, body(): up0 = lax.ppermute(u0, 'loop', ups)  82.2 us
    ppermute x1, waiting for transfers between devices, body(): got = lax.ppermute(sent, 'loop', skips)  49.2 us
    ppermute x1, waiting for transfers between devices, body(): down0 = lax.ppermute(w0, 'loop', downs)  46.8 us
    ppermute x1, waiting for transfers between devices, body(): down1 = lax.ppermute(w1, 'loop', downs)  31.1 us
    pallas_call x4, Pallas kernels, second_product(): pl.pallas_call(functools.partial(second_product_kernel, halves, count), g...  23.6 us
    ppermute x6, waiting for transfers between devices, everywhere(): return lax.ppermute(x, ('rows', 'loop'), pairs)  22.7 us
    pallas_call x3, Pallas kernels, first_product(): pl.pallas_call(functools.partial(first_product_kernel, runs, skip), grid_...  19.1 us
    pallas_call x3, Pallas kernels, gram_call(): pl.pallas_call(functools.partial(packed_gram_kernel, halves), grid_spec=p...  18.2 us
  transfers between devices with their start and end apart: 18, of which 13 were waited for; matrix products, arithmetic and copies ran while one was open for 0% of the time, Pallas kernels for 15%

profile of v4, /device:TPU:0, one launch (start us, length us, event | category | flops | bytes accessed | tf_op | source)
XLA Modules:
  0.0 360.3 jit_solution(15331286222747066275)
XLA Ops:
  0.0 6.8 %shard_map.28 = f32[128,128]{1,0:T(8,128)} custom-call(f32[24576,128]{1,0:T(8,128)} %x_ref.1), custom_call_target="tpu_custom_call" | custom-call | flops 1000 | bytes 1000 | tf_op jit(solution)/shard_map/pallas_call | solution.py:80
  6.8 1.5 collective-permute-done
  8.2 0.9 add.17.one_ref
  9.1 3.3 collective-permute-start.1
  12.5 2.4 collective-permute-done.1.two_ref
  14.9 2.9 shard_map.29
  17.8 0.6 copy-done.2
  18.4 0.7 copy-done.3
  19.1 6.4 %shard_map.30 = (f32[2048,128]{1,0:T(8,128)}, f32[2048,128]{1,0:T(8,128)}, f32[1024,128]{1,0:T(8,128)}, f32[1024,128]{1,0:T(8,128)}, f32[3072,128]{1,0:T(8,128)}) custom-call(s32[4]{0:T(128)} %copy-done.4, f32[2,12288,128]{2,1,0:T(8,128)} %bitcast.6, bf16[256,256]{1,0:T(8,128)(2,1)} %copy-done.2, bf16[256,256]{1,0:T(8,128)(2,1)} %copy-done.3, ...), custom_call_target="tpu_custom_call" | custom-call | flops 1000 | bytes 1000 | tf_op jit(solution)/shard_map/pallas_call | solution.py:188
  25.5 1.6 collective-permute-start.2
  27.1 6.1 %shard_map.32 = (f32[5120,128]{1,0:T(8,128)}, f32[5120,128]{1,0:T(8,128)}) custom-call(s32[4]{0:T(128)} %copy-done.4, f32[2,12288,128]{2,1,0:T(8,128)} %bitcast.8, bf16[256,256]{1,0:T(8,128)(2,1)} %copy-done.2, bf16[256,256]{1,0:T(8,128)(2,1)} %copy-done.3, f32[3072,128]{1,0:T(8,128)} %get-tuple-element.20._), custom_call_target="tpu_custom_call" | custom-call | flops 1000 | bytes 1000 | tf_op jit(solution)/shard_map/pallas_call | solution.py:188
  33.2 2.5 collective-permute-start.5
  35.8 1.3 collective-permute-start.6
  37.1 49.2 %collective-permute-done.2.refs_0_._.refs_4_ = f32[3072,128]{1,0:T(8,128)S(1)} collective-permute-done((f32[3072,128]{1,0:T(8,128)}, f32[3072,128]{1,0:T(8,128)S(1)}, u32[]{:S(2)}, u32[]{:S(2)}) %collective-permute-start.2) | collective-permute-done | bytes 1572896 | tf_op jit(solution)/shard_map/ppermute | solution.py:455
  86.2 1.1 copy-done.7
  87.4 6.5 %shard_map.34 = (f32[4096,128]{1,0:T(8,128)}, f32[4096,128]{1,0:T(8,128)}) custom-call(s32[4]{0:T(128)} %copy-done.4, f32[2,12288,128]{2,1,0:T(8,128)} %bitcast.9, bf16[256,256]{1,0:T(8,128)(2,1)} %copy-done.2, bf16[256,256]{1,0:T(8,128)(2,1)} %copy-done.3, f32[3072,128]{1,0:T(8,128)} %copy-done.7), custom_call_target="tpu_custom_call" | custom-call | flops 1000 | bytes 1000 | tf_op jit(solution)/shard_map/pallas_call | solution.py:188
  93.9 1.5 collective-permute-start.7
  95.4 1.3 collective-permute-start.8
  96.7 5.3 %shard_map.31 = f32[128,128]{1,0:T(8,128)} custom-call(s32[4]{0:T(128)} %copy-done.4, f32[3072,128]{1,0:T(8,128)} %copy-done.7, f32[2048,128]{1,0:T(8,128)} %get-tuple-element.21.refs_1_.refs_2_, f32[2048,128]{1,0:T(8,128)} %get-tuple-element.22.refs_2_.refs_3_, f32[1024,128]{1,0:T(8,128)} %get-tuple-element.23.refs_3_.refs_2_, ...), custom_call_target="tpu_custom_call" | custom-call | flops 1000 | bytes 1000 | tf_op jit(solution)/shard_map/pallas_call | solution.py:283
  102.1 4.5 %collective-permute-start.3 = (f32[128,128]{1,0:T(8,128)}, f32[128,128]{1,0:T(8,128)S(1)}, u32[]{:S(2)}, u32[]{:S(2)}) collective-permute-start(f32[128,128]{1,0:T(8,128)} %shard_map.31), channel_id=1, source_target_pairs={{0,65},{1,64},{2,67},{3,66},{4,69},{5,68},{6,71},{7,70},{8,73},{9,... | collective-permute-start | bytes 196616 | tf_op jit(solution)/shard_map/ppermute | solution.py:390
  106.6 2.5 collective-permute-done.3
  109.0 3.1 collective-permute-start.16
  112.1 82.2 %collective-permute-done.5.refs_0_ = f32[5120,128]{1,0:T(8,128)S(1)} collective-permute-done((f32[5120,128]{1,0:T(8,128)}, f32[5120,128]{1,0:T(8,128)S(1)}, u32[]{:S(2)}, u32[]{:S(2)}) %collective-permute-start.5) | collective-permute-done | bytes 2621472 | tf_op jit(solution)/shard_map/ppermute | solution.py:457
  194.3 1.8 collective-permute-start.17
  196.2 46.8 %collective-permute-done.6.refs_1_ = f32[5120,128]{1,0:T(8,128)} collective-permute-done((f32[5120,128]{1,0:T(8,128)}, f32[5120,128]{1,0:T(8,128)}, u32[]{:S(2)}, u32[]{:S(2)}) %collective-permute-start.6) | collective-permute-done | bytes 2621472 | tf_op jit(solution)/shard_map/ppermute | solution.py:458
  242.9 6.5 %shard_map.33 = f32[128,128]{1,0:T(8,128)} custom-call(s32[4]{0:T(128)} %copy-done.4, f32[5120,128]{1,0:T(8,128)} %copy-done.8, f32[5120,128]{1,0:T(8,128)} %collective-permute-done.6.refs_1_, f32[5120,128]{1,0:T(8,128)} %get-tuple-element.25.refs_2_, f32[5120,128]{1,0:T(8,128)} %get-tuple-element.26.refs_3_), custom_call_target="tpu_custom_call" | custom-call | flops 1000 | bytes 1000 | tf_op jit(solution)/shard_map/pallas_call | solution.py:283
  249.4 12.3 %collective-permute-done.7.refs_0_ = f32[4096,128]{1,0:T(8,128)S(1)} collective-permute-done((f32[4096,128]{1,0:T(8,128)}, f32[4096,128]{1,0:T(8,128)S(1)}, u32[]{:S(2)}, u32[]{:S(2)}) %collective-permute-start.7) | collective-permute-done | bytes 2097184 | tf_op jit(solution)/shard_map/ppermute | solution.py:460
  261.7 4.3 %collective-permute-start.14 = (f32[1024,128]{1,0:T(8,128)}, f32[1024,128]{1,0:T(8,128)S(1)}, u32[]{:S(2)}, u32[]{:S(2)}) collective-permute-start(f32[1024,128]{1,0:T(8,128)} %get-tuple-element.23.refs_3_.refs_2_), channel_id=1, source_target_pairs={{0,1},{1,2},{2,3},{3,4},{4,5},{5,6},{6,7},{7,8},{8,9},{9,10},{10,1... | collective-permute-start | bytes 1572872 | tf_op jit(solution)/shard_map/ppermute | solution.py:464
  266.1 31.1 %collective-permute-done.8.refs_1_ = f32[4096,128]{1,0:T(8,128)} collective-permute-done((f32[4096,128]{1,0:T(8,128)}, f32[4096,128]{1,0:T(8,128)}, u32[]{:S(2)}, u32[]{:S(2)}) %collective-permute-start.8) | collective-permute-done | bytes 2097184 | tf_op jit(solution)/shard_map/ppermute | solution.py:461
  297.1 0.7 collective-permute-start.15
  297.8 6.4 %shard_map.35 = f32[128,128]{1,0:T(8,128)} custom-call(s32[4]{0:T(128)} %copy-done.4, f32[4096,128]{1,0:T(8,128)} %copy-done.9, f32[4096,128]{1,0:T(8,128)} %collective-permute-done.8.refs_1_, f32[4096,128]{1,0:T(8,128)} %get-tuple-element.27.refs_2_, f32[4096,128]{1,0:T(8,128)} %get-tuple-element.28.refs_3_), custom_call_target="tpu_custom_call" | custom-call | flops 1000 | bytes 1000 | tf_op jit(solution)/shard_map/pallas_call | solution.py:283
  304.2 0.9 add_add_fusion
  305.2 1.2 collective-permute-done.9
  306.4 4.2 %collective-permute-start.10 = (f32[128,128]{1,0:T(8,128)S(1)}, f32[128,128]{1,0:T(8,128)S(1)}, u32[]{:S(2)}, u32[]{:S(2)}) collective-permute-start(f32[128,128]{1,0:T(8,128)S(1)} %add.20.one_ref), channel_id=1, source_target_pairs={{0,66},{1,71},{2,68},{3,65},{4,70},{5,67},{6,64},{7,69},{8,74},{9,... | collective-permute-start | bytes 196616 | tf_op jit(solution)/shard_map/ppermute | solution.py:390
  310.7 3.9 %collective-permute-done.10 = f32[128,128]{1,0:T(8,128)S(1)} collective-permute-done((f32[128,128]{1,0:T(8,128)S(1)}, f32[128,128]{1,0:T(8,128)S(1)}, u32[]{:S(2)}, u32[]{:S(2)}) %collective-permute-start.10) | collective-permute-done | bytes 65568 | tf_op jit(solution)/shard_map/ppermute | solution.py:390
  314.6 0.1 collective-permute-start.11
  314.7 5.4 %collective-permute-done.11 = f32[128,128]{1,0:T(8,128)S(1)} collective-permute-done((f32[128,128]{1,0:T(8,128)S(1)}, f32[128,128]{1,0:T(8,128)S(1)}, u32[]{:S(2)}, u32[]{:S(2)}) %collective-permute-start.11) | collective-permute-done | bytes 65568 | tf_op jit(solution)/shard_map/ppermute | solution.py:390
  320.0 5.5 %collective-permute-done.12 = f32[128,128]{1,0:T(8,128)S(1)} collective-permute-done((f32[128,128]{1,0:T(8,128)S(1)}, f32[128,128]{1,0:T(8,128)S(1)}, u32[]{:S(2)}, u32[]{:S(2)}) %collective-permute-start.12) | collective-permute-done | bytes 65568 | tf_op jit(solution)/shard_map/ppermute | solution.py:390
  325.5 5.5 %collective-permute-done.13.two_ref = f32[128,128]{1,0:T(8,128)S(1)} collective-permute-done((f32[128,128]{1,0:T(8,128)S(1)}, f32[128,128]{1,0:T(8,128)S(1)}, u32[]{:S(2)}, u32[]{:S(2)}) %collective-permute-start.13) | collective-permute-done | bytes 65568 | tf_op jit(solution)/shard_map/ppermute | solution.py:390
  331.0 2.7 shard_map.36
  333.7 0.6 copy-done
  334.4 0.7 copy-done.1
  335.0 7.3 %shard_map.37.refs_4_ = f32[2,12288,128]{2,1,0:T(8,128)} custom-call(s32[4]{0:T(128)} %copy-done.4, bf16[256,256]{1,0:T(8,128)(2,1)} %copy-done, bf16[256,256]{1,0:T(8,128)(2,1)} %copy-done.1, f32[5120,128]{1,0:T(8,128)} %copy-done.8, f32[5120,128]{1,0:T(8,128)} %collective-permute-done.6.refs_1_, f32[5120,128]{1,0:T(8,128)} %get-tuple-element.25.refs_2_, ...), custom_call_target="tpu_custom_call" | custom-call | flops 1000 | bytes 1000 | tf_op jit(solution)/shard_map/pallas_call | solution.py:363
  342.4 7.4 %shard_map.38.refs_5_ = f32[2,12288,128]{2,1,0:T(8,128)} custom-call(s32[4]{0:T(128)} %copy-done.4, bf16[256,256]{1,0:T(8,128)(2,1)} %copy-done, bf16[256,256]{1,0:T(8,128)(2,1)} %copy-done.1, f32[4096,128]{1,0:T(8,128)} %copy-done.9, f32[4096,128]{1,0:T(8,128)} %collective-permute-done.8.refs_1_, ...), custom_call_target="tpu_custom_call", output_to_operand_aliasing={{}: (7, {})} | custom-call | flops 1000 | bytes 1000 | tf_op jit(solution)/shard_map/pallas_call | solution.py:363
  349.8 5.0 %shard_map.39.refs_5_ = f32[2,12288,128]{2,1,0:T(8,128)} custom-call(s32[4]{0:T(128)} %copy-done.4, bf16[256,256]{1,0:T(8,128)(2,1)} %copy-done, bf16[256,256]{1,0:T(8,128)(2,1)} %copy-done.1, f32[2048,128]{1,0:T(8,128)} %collective-permute-done.16.refs_0_, f32[2048,128]{1,0:T(8,128)} %collective-permute-done.17.refs_1_, ...), custom_call_target="tpu_custom_call", output_to_operand_aliasing={{}: (8, {})} | custom-call | flops 1000 | bytes 1000 | tf_op jit(solution)/shard_map/pallas_call | solution.py:363
  354.7 0.8 copy-done.11
  355.5 0.8 copy-done.12
  356.3 3.9 %shard_map.40 = f32[2,12288,128]{2,1,0:T(8,128)} custom-call(s32[4]{0:T(128)} %copy-done.4, bf16[256,256]{1,0:T(8,128)(2,1)} %copy-done, bf16[256,256]{1,0:T(8,128)(2,1)} %copy-done.1, f32[1024,128]{1,0:T(8,128)} %copy-done.11, f32[1024,128]{1,0:T(8,128)} %copy-done.12, ...), custom_call_target="tpu_custom_call", output_to_operand_aliasing={{}: (8, {})} | custom-call | flops 1000 | bytes 1000 | tf_op jit(solution)/shard_map/pallas_call | solution.py:363
  (33 shorter events, 0.2 us)
Async XLA Ops:
  0.0 14.9 %copy-start.6 = (s32[2,4]{1,0:T(2,128)S(1)}, s32[2,4]{1,0:T(2,128)}, u32[]{:S(2)}) copy-start(s32[2,4]{1,0:T(2,128)} %offsets_ref.3) | copy-start | bytes 100
  6.8 1.5 collective-permute-start
  9.1 5.8 %collective-permute-start.1 = (f32[128,128]{1,0:T(8,128)S(1)}, f32[128,128]{1,0:T(8,128)S(1)}, u32[]{:S(2)}, u32[]{:S(2)}) collective-permute-start(f32[128,128]{1,0:T(8,128)S(1)} %add.17.one_ref), channel_id=1, source_target_pairs={{0,64},{32,96},{64,0},{96,32},{1,65},{33,97},{65,1},{97,33},{2,66}... | collective-permute-start | bytes 196616 | tf_op jit(solution)/shard_map/ppermute | solution.py:380
  12.5 6.6 %copy-start.4 = (s32[4]{0:T(128)}, s32[4]{0:T(128)S(1)}, u32[]{:S(2)}) copy-start(s32[4]{0:T(128)S(1)} %pad_add_fusion.flags_ref) | copy-start | bytes 52
  17.8 0.7 copy-start.2
  18.4 0.7 copy-start.3
  25.5 60.7 %collective-permute-start.2 = (f32[3072,128]{1,0:T(8,128)}, f32[3072,128]{1,0:T(8,128)S(1)}, u32[]{:S(2)}, u32[]{:S(2)}) collective-permute-start(f32[3072,128]{1,0:T(8,128)} %get-tuple-element.20._), channel_id=1, source_target_pairs={{0,2},{2,4},{4,6},{6,8},{8,10},{10,12},{12,14},{14,16},{16,18},{18... | collective-permute-start | bytes 4718600 | tf_op jit(solution)/shard_map/ppermute | solution.py:455
  33.2 161.1 %collective-permute-start.5 = (f32[5120,128]{1,0:T(8,128)}, f32[5120,128]{1,0:T(8,128)S(1)}, u32[]{:S(2)}, u32[]{:S(2)}) collective-permute-start(f32[5120,128]{1,0:T(8,128)} %get-tuple-element.25.refs_2_), channel_id=1, source_target_pairs={{0,1},{1,2},{2,3},{3,4},{4,5},{5,6},{6,7},{7,8},{8,9},{9,10},{10,1... | collective-permute-start | bytes 7864328 | tf_op jit(solution)/shard_map/ppermute | solution.py:457
  35.8 207.2 %collective-permute-start.6 = (f32[5120,128]{1,0:T(8,128)}, f32[5120,128]{1,0:T(8,128)}, u32[]{:S(2)}, u32[]{:S(2)}) collective-permute-start(f32[5120,128]{1,0:T(8,128)} %get-tuple-element.26.refs_3_), channel_id=1, source_target_pairs={{1,0},{2,1},{3,2},{4,3},{5,4},{6,5},{7,6},{8,7},{9,8},{10,9},{11,1... | collective-permute-start | bytes 7864328 | tf_op jit(solution)/shard_map/ppermute | solution.py:458
  86.2 1.1 copy-start.7
  93.9 15.1 %copy-start.10 = (f32[2048,128]{1,0:T(8,128)S(1)}, f32[2048,128]{1,0:T(8,128)}, u32[]{:S(2)}) copy-start(f32[2048,128]{1,0:T(8,128)} %get-tuple-element.21.refs_1_.refs_2_) | copy-start | bytes 3145732
  93.9 167.9 %collective-permute-start.7 = (f32[4096,128]{1,0:T(8,128)}, f32[4096,128]{1,0:T(8,128)S(1)}, u32[]{:S(2)}, u32[]{:S(2)}) collective-permute-start(f32[4096,128]{1,0:T(8,128)} %get-tuple-element.27.refs_2_), channel_id=1, source_target_pairs={{0,1},{1,2},{2,3},{3,4},{4,5},{5,6},{6,7},{7,8},{8,9},{9,10},{10,1... | collective-permute-start | bytes 6291464 | tf_op jit(solution)/shard_map/ppermute | solution.py:460
  95.4 201.7 %collective-permute-start.8 = (f32[4096,128]{1,0:T(8,128)}, f32[4096,128]{1,0:T(8,128)}, u32[]{:S(2)}, u32[]{:S(2)}) collective-permute-start(f32[4096,128]{1,0:T(8,128)} %get-tuple-element.28.refs_3_), channel_id=1, source_target_pairs={{1,0},{2,1},{3,2},{4,3},{5,4},{6,5},{7,6},{8,7},{9,8},{10,9},{11,1... | collective-permute-start | bytes 6291464 | tf_op jit(solution)/shard_map/ppermute | solution.py:461
  102.1 6.9 %collective-permute-start.3 = (f32[128,128]{1,0:T(8,128)}, f32[128,128]{1,0:T(8,128)S(1)}, u32[]{:S(2)}, u32[]{:S(2)}) collective-permute-start(f32[128,128]{1,0:T(8,128)} %shard_map.31), channel_id=1, source_target_pairs={{0,65},{1,64},{2,67},{3,66},{4,69},{5,68},{6,71},{7,70},{8,73},{9,... | collective-permute-start | bytes 196616 | tf_op jit(solution)/shard_map/ppermute | solution.py:390
  109.0 240.7 %collective-permute-start.16 = (f32[2048,128]{1,0:T(8,128)S(1)}, f32[2048,128]{1,0:T(8,128)}, u32[]{:S(2)}, u32[]{:S(2)}) collective-permute-start(f32[2048,128]{1,0:T(8,128)S(1)} %copy-done.10), channel_id=1, source_target_pairs={{0,1},{1,2},{2,3},{3,4},{4,5},{5,6},{6,7},{7,8},{8,9},{9,10},{10,1... | collective-permute-start | bytes 3145736 | tf_op jit(solution)/shard_map/ppermute | solution.py:462
  194.3 48.6 %copy-start.8 = (f32[5120,128]{1,0:T(8,128)}, f32[5120,128]{1,0:T(8,128)S(1)}, u32[]{:S(2)}) copy-start(f32[5120,128]{1,0:T(8,128)S(1)} %collective-permute-done.5.refs_0_) | copy-start | bytes 7864324
  194.3 155.4 %collective-permute-start.17 = (f32[2048,128]{1,0:T(8,128)}, f32[2048,128]{1,0:T(8,128)}, u32[]{:S(2)}, u32[]{:S(2)}) collective-permute-start(f32[2048,128]{1,0:T(8,128)} %get-tuple-element.22.refs_2_.refs_3_), channel_id=1, source_target_pairs={{2,1},{3,2},{4,3},{5,4},{6,5},{7,6},{8,7},{9,8},{10,9},{11,10},{12... | collective-permute-start | bytes 3145736 | tf_op jit(solution)/shard_map/ppermute | solution.py:463
  242.9 61.3 %collective-permute-start.4 = (f32[128,128]{1,0:T(8,128)S(1)}, f32[128,128]{1,0:T(8,128)S(1)}, u32[]{:S(2)}, u32[]{:S(2)}) collective-permute-start(f32[128,128]{1,0:T(8,128)S(1)} %collective-permute-done.3), channel_id=1, source_target_pairs={{0,2},{1,64},{2,4},{3,1},{4,6},{5,3},{6,8},{7,5},{8,10},{9,7},{10,... | collective-permute-start | bytes 196616 | tf_op jit(solution)/shard_map/ppermute | solution.py:390
  249.4 54.8 %copy-start.13 = (f32[128,128]{1,0:T(8,128)S(1)}, f32[128,128]{1,0:T(8,128)}, u32[]{:S(2)}) copy-start(f32[128,128]{1,0:T(8,128)} %shard_map.33) | copy-start | bytes 196612
  249.4 81.6 %copy-start.5 = (s32[4]{0:T(128)S(1)}, s32[4]{0:T(128)}, u32[]{:S(2)}) copy-start(s32[4]{0:T(128)} %copy-done.4) | copy-start | bytes 52
  261.7 36.1 %copy-start.9 = (f32[4096,128]{1,0:T(8,128)}, f32[4096,128]{1,0:T(8,128)S(1)}, u32[]{:S(2)}) copy-start(f32[4096,128]{1,0:T(8,128)S(1)} %collective-permute-done.7.refs_0_) | copy-start | bytes 6291460
  261.7 93.0 %collective-permute-start.14 = (f32[1024,128]{1,0:T(8,128)}, f32[1024,128]{1,0:T(8,128)S(1)}, u32[]{:S(2)}, u32[]{:S(2)}) collective-permute-start(f32[1024,128]{1,0:T(8,128)} %get-tuple-element.23.refs_3_.refs_2_), channel_id=1, source_target_pairs={{0,1},{1,2},{2,3},{3,4},{4,5},{5,6},{6,7},{7,8},{8,9},{9,10},{10,1... | collective-permute-start | bytes 1572872 | tf_op jit(solution)/shard_map/ppermute | solution.py:464
  297.1 57.6 %collective-permute-start.15 = (f32[1024,128]{1,0:T(8,128)}, f32[1024,128]{1,0:T(8,128)S(1)}, u32[]{:S(2)}, u32[]{:S(2)}) collective-permute-start(f32[1024,128]{1,0:T(8,128)} %get-tuple-element.24.refs_4_.refs_3_), channel_id=1, source_target_pairs={{2,1},{3,2},{4,3},{5,4},{6,5},{7,6},{8,7},{9,8},{10,9},{11,10},{12... | collective-permute-start | bytes 1572872 | tf_op jit(solution)/shard_map/ppermute | solution.py:465
  305.1 1.3 collective-permute-start.9
  306.4 8.1 %collective-permute-start.10 = (f32[128,128]{1,0:T(8,128)S(1)}, f32[128,128]{1,0:T(8,128)S(1)}, u32[]{:S(2)}, u32[]{:S(2)}) collective-permute-start(f32[128,128]{1,0:T(8,128)S(1)} %add.20.one_ref), channel_id=1, source_target_pairs={{0,66},{1,71},{2,68},{3,65},{4,70},{5,67},{6,64},{7,69},{8,74},{9,... | collective-permute-start | bytes 196616 | tf_op jit(solution)/shard_map/ppermute | solution.py:390
  314.6 5.5 %collective-permute-start.11 = (f32[128,128]{1,0:T(8,128)S(1)}, f32[128,128]{1,0:T(8,128)S(1)}, u32[]{:S(2)}, u32[]{:S(2)}) collective-permute-start(f32[128,128]{1,0:T(8,128)S(1)} %collective-permute-done.10), channel_id=1, source_target_pairs={{0,2},{1,7},{2,4},{3,1},{4,6},{5,3},{6,0},{7,5},{8,10},{9,15},{10,... | collective-permute-start | bytes 196616 | tf_op jit(solution)/shard_map/ppermute | solution.py:390
  320.0 5.5 %collective-permute-start.12 = (f32[128,128]{1,0:T(8,128)S(1)}, f32[128,128]{1,0:T(8,128)S(1)}, u32[]{:S(2)}, u32[]{:S(2)}) collective-permute-start(f32[128,128]{1,0:T(8,128)S(1)} %collective-permute-done.11), channel_id=1, source_target_pairs={{0,2},{1,7},{2,4},{3,1},{4,6},{5,3},{6,0},{7,5},{8,10},{9,15},{10,... | collective-permute-start | bytes 196616 | tf_op jit(solution)/shard_map/ppermute | solution.py:390
  325.5 5.5 %collective-permute-start.13 = (f32[128,128]{1,0:T(8,128)S(1)}, f32[128,128]{1,0:T(8,128)S(1)}, u32[]{:S(2)}, u32[]{:S(2)}) collective-permute-start(f32[128,128]{1,0:T(8,128)S(1)} %collective-permute-done.12), channel_id=1, source_target_pairs={{0,2},{1,7},{2,4},{3,1},{4,6},{5,3},{6,0},{7,5},{8,10},{9,15},{10,... | collective-permute-start | bytes 196616 | tf_op jit(solution)/shard_map/ppermute | solution.py:390
  333.7 0.7 copy-start
  334.4 0.7 copy-start.1
  354.7 0.8 copy-start.11
  355.5 0.8 copy-start.12

commit v5 on v4

--- a/solution.py
+++ b/solution.py
@@ -405,24 +405,38 @@
 def far_partner(x, count):
     ring = min(4, count // 2)
 
-    def along(place):
+    def across(place):
         pair, odd = divmod(place, 2)
         group, at = divmod(pair, ring)
         at = (at - 1) % ring if odd else (at + 1) % ring
-        return 2 * (group * ring + at) + odd
-
-    x = everywhere(x, lambda row, place: (row ^ 2, along(place)))
-    for _ in range(ring - 1):
-        x = everywhere(x, lambda row, place: (row, along(place)))
-    return x
+        return 2 * (group * ring + at) + 1 - odd
+
+    x = everywhere(x, lambda row, place: (row, across(place)))
+    return everywhere(x, lambda row, place: (row ^ 2, across(place)))
+
+
+def held_kernel(*refs):
+    pass
+
+
+def held(arrays, earlier):
+    anywhere = pl.BlockSpec(memory_space=pl.ANY)
+    return pl.pallas_call(
+        held_kernel,
+        in_specs=[anywhere] * (len(arrays) + 1),
+        out_specs=[anywhere] * len(arrays),
+        out_shape=[jax.ShapeDtypeStruct(x.shape, x.dtype) for x in arrays],
+        input_output_aliases={k: k for k in range(len(arrays))},
+        cost_estimate=HINT,
+        compiler_params=params(),
+    )(*arrays, earlier)
 
 
 def body(x, offsets):
     rows, width = x.shape
     half_rows = rows // 2
-    small = half_rows // 12
-    large = 5 * small // 2
-    middle, late, final = 2 * large, 9 * small, 11 * small
+    large, small = half_rows // 6, half_rows // 12
+    late, final = 8 * small, 11 * small
     place = lax.axis_index("loop")
     count = lax.axis_size("loop")
     last = count - 1
@@ -442,40 +456,44 @@
     skips = (
         [(i, i + 2) for i in range(0, last - 1, 2)]
         + [(i, i - 2) for i in range(3, count, 2)]
-        + [(1, 0), (last - 1, last)]
-    )
+    )
+    by_down, by_up = (25, 6) if count == 32 else (1, last - 1)
 
     gram = local_gram(x, rows // 3)
     gram = gram + row_partner(gram, 1)
     a, b = rotations(0, flags, offsets, gram, row_partner(gram, 2))
 
-    u2, w2, u3, w3, sent = first_product(
-        flags, halves, a, b, halves, late, small, [(0, 2), (2, 1)], True
-    )
-    got = lax.ppermute(sent, "loop", skips)
-    u0, w0 = first_product(flags, halves, a, b, sent, 0, large, [(0, 2)], False)
+    u0, w0 = first_product(flags, halves, a, b, halves, 0, large, [(0, 4)], False)
     up0 = lax.ppermute(u0, "loop", ups)
     down0 = lax.ppermute(w0, "loop", downs)
-    u1, w1 = first_product(flags, halves, a, b, got, middle, small, [(0, 4)], False)
-    up1 = lax.ppermute(u1, "loop", ups)
-    down1 = lax.ppermute(w1, "loop", downs)
+    u1, w1, u2, w2, sent = first_product(
+        flags, halves, a, b, u0, late, small, [(0, 3), (3, 1)], True
+    )
+    got = lax.ppermute(sent, "loop", skips)
+    ends = lax.ppermute(sent, "loop", [(1, by_down), (last - 1, by_up)])
+    (ends,) = held([ends], got)
+    ends = lax.ppermute(ends, "loop", [(by_down, 0), (by_up, last)])
+    got = jnp.where((place == 0) | (place == last), ends, got)
+
+    gram = neighbour_gram(flags, got, u1, w1, u2, w2, small)
+    u1, w1 = held([u1, w1], gram)
+    up1 = lax.ppermute(u1, "loop", ups[:-1])
+    down1 = lax.ppermute(w1, "loop", downs[1:])
+    (gram,) = held([gram], up0)
+    (gram,) = held([gram], down0)
+    gram = home(gram, last)
+    gram = gram + arrived_gram(flags, up0, down0, u0, w0, large)
+    u2, w2 = held([u2, w2], gram)
     up2 = lax.ppermute(u2, "loop", ups[:-1])
     down2 = lax.ppermute(w2, "loop", downs[1:])
-    up3 = lax.ppermute(u3, "loop", ups[:-1])
-    down3 = lax.ppermute(w3, "loop", downs[1:])
-
-    gram = home(neighbour_gram(flags, got, u2, w2, u3, w3, small), last)
-    gram = gram + arrived_gram(flags, up0, down0, u0, w0, large)
-    gram = gram + arrived_gram(flags, up1, down1, u1, w1, small)
     gram = gram + row_partner(gram, 1)
     a, b = rotations(1, flags, offsets, gram, far_partner(gram, count))
 
     out = None
     for arrays, got_start, low, size in (
         ((up0, down0, u0, w0), None, 0, large),
-        ((up1, down1, u1, w1), None, middle, small),
-        ((up2, down2, u2, w2), 0, late, small),
-        ((up3, down3, u3, w3), final - late, final, small),
+        ((up1, down1, u1, w1), 0, late, small),
+        ((up2, down2, u2, w2), final - late, final, small),
     ):
         skipped = None if got_start is None else got
         out = second_product(

time: 364 us -> 333 us (0.915)
  waiting for transfers between devices: 249 us -> 211 us
  starting transfers between devices: 30.3 us -> 39.8 us
  Pallas kernels: 73.3 us -> 66.4 us
  local copies, waits for them, and re-layouts: 5.38 us -> 9.12 us
    ppermute x4, waiting for transfers between devices: 43.4 us -> 99 us  [the longest x1 99 us: body(): ends = lax.ppermute(ends, 'loop', [(by_down, 0), (by_up, last)])]
    ppermute x1, waiting for transfers between devices: 46.8 us -> 0.01 us  [body(): down0 = lax.ppermute(w0, 'loop', downs)]
    ppermute x1, waiting for transfers between devices: 49.2 us -> 30.4 us  [body(): got = lax.ppermute(sent, 'loop', skips)]
    ppermute x6 -> x4, waiting for transfers between devices: 22.7 us -> 8.31 us  [everywhere(): return lax.ppermute(x, ('rows', 'loop'), pairs)]
    ppermute x1, waiting for transfers between devices: 82.2 us -> 68.3 us  [body(): up0 = lax.ppermute(u0, 'loop', ups)]
    ppermute x1, starting transfers between devices: 2.51 us -> 11.7 us  [body(): up0 = lax.ppermute(u0, 'loop', ups)]
    ppermute x6 -> x4, starting transfers between devices: 8.83 us -> 13.6 us  [everywhere(): return lax.ppermute(x, ('rows', 'loop'), pairs)]
    unnamed x28 -> x26, local copies, waits for them, and re-layouts: 5.38 us -> 9.12 us
  transfers between devices with their start and end apart: 18 -> 16, of which waited for: 13 -> 9; matrix products, arithmetic and copies ran while one was open for 0% -> 1% of each run, Pallas kernels for 15% -> 11%
where the time goes in v5:
time: 333 us; the launch traced here: 332 us
  waiting for transfers between devices  211 us (63%)
  Pallas kernels  66.4 us (20%)
  starting transfers between devices  39.8 us (12%)
  local copies, waits for them, and re-layouts  9.12 us (3%)
  other arithmetic  4.85 us (1%)
    ppermute x1, waiting for transfers between devices, body(): ends = lax.ppermute(ends, 'loop', [(by_down, 0), (by_up, last)])  99 us
    ppermute x1, waiting for transfers between devices, body(): up0 = lax.ppermute(u0, 'loop', ups)  68.3 us
    ppermute x1, waiting for transfers between devices, body(): got = lax.ppermute(sent, 'loop', skips)  30.4 us
    pallas_call x3, Pallas kernels, second_product(): pl.pallas_call(functools.partial(second_product_kernel, halves, count), g...  22.1 us
    pallas_call x2, Pallas kernels, first_product(): pl.pallas_call(functools.partial(first_product_kernel, runs, skip), grid_...  16.7 us
    pallas_call x2, Pallas kernels, gram_call(): pl.pallas_call(functools.partial(packed_gram_kernel, halves), grid_spec=p...  15.2 us
    ppermute x4, starting transfers between devices, everywhere(): return lax.ppermute(x, ('rows', 'loop'), pairs)  13.6 us
    ppermute x1, starting transfers between devices, body(): up0 = lax.ppermute(u0, 'loop', ups)  11.7 us
  transfers between devices with their start and end apart: 16, of which 9 were waited for; matrix products, arithmetic and copies ran while one was open for 1% of the time, Pallas kernels for 11%

profile of v5, /device:TPU:0, one launch (start us, length us, event | category | flops | bytes accessed | tf_op | source)
XLA Modules:
  0.0 331.7 jit_solution(11073935390398347915)
XLA Ops:
  0.0 6.8 %shard_map.28 = f32[128,128]{1,0:T(8,128)} custom-call(f32[24576,128]{1,0:T(8,128)} %x_ref.1), custom_call_target="tpu_custom_call" | custom-call | flops 1000 | bytes 1000 | tf_op jit(solution)/shard_map/pallas_call | solution.py:80
  6.8 1.5 collective-permute-done
  8.2 0.9 add.14.one_ref
  9.1 3.3 collective-permute-start.1
  12.4 0.1 pad_add_fusion.flags_ref
  12.5 2.4 collective-permute-done.1.two_ref
  14.9 2.9 shard_map.29
  17.8 0.6 copy-done.2
  18.4 0.7 copy-done.3
  19.1 9.5 %shard_map.30 = (f32[8192,128]{1,0:T(8,128)}, f32[8192,128]{1,0:T(8,128)}) custom-call(s32[4]{0:T(128)} %copy-done.4, f32[2,12288,128]{2,1,0:T(8,128)} %bitcast.6, bf16[256,256]{1,0:T(8,128)(2,1)} %copy-done.2, bf16[256,256]{1,0:T(8,128)(2,1)} %copy-done.3, f32[2,12288,128]{2,1,0:T(8,128)} %bitcast.7), custom_call_target="tpu_custom_call" | custom-call | flops 1000 | bytes 1000 | tf_op jit(solution)/shard_map/pallas_call | solution.py:188
  28.6 7.2 %shard_map.31 = (f32[3072,128]{1,0:T(8,128)}, f32[3072,128]{1,0:T(8,128)}, f32[1024,128]{1,0:T(8,128)}, f32[1024,128]{1,0:T(8,128)}, f32[4096,128]{1,0:T(8,128)}) custom-call(s32[4]{0:T(128)} %copy-done.4, f32[2,12288,128]{2,1,0:T(8,128)} %bitcast.8, bf16[256,256]{1,0:T(8,128)(2,1)} %copy-done.2, bf16[256,256]{1,0:T(8,128)(2,1)} %copy-done.3, ...), custom_call_target="tpu_custom_call" | custom-call | flops 1000 | bytes 1000 | tf_op jit(solution)/shard_map/pallas_call | solution.py:188
  35.8 3.6 %collective-permute-start.3 = (f32[4096,128]{1,0:T(8,128)}, f32[4096,128]{1,0:T(8,128)S(1)}, u32[]{:S(2)}, u32[]{:S(2)}) collective-permute-start(f32[4096,128]{1,0:T(8,128)} %get-tuple-element.23), channel_id=1, source_target_pairs={{0,2},{2,4},{4,6},{6,8},{8,10},{10,12},{12,14},{14,16},{16,18},{18... | collective-permute-start | bytes 6291464 | tf_op jit(solution)/shard_map/ppermute | solution.py:472
  39.4 0.8 collective-permute-start.2
  40.2 11.7 %collective-permute-start.5 = (f32[8192,128]{1,0:T(8,128)}, f32[8192,128]{1,0:T(8,128)}, u32[]{:S(2)}, u32[]{:S(2)}) collective-permute-start(f32[8192,128]{1,0:T(8,128)} %get-tuple-element.22._.refs_2_), channel_id=1, source_target_pairs={{0,1},{1,2},{2,3},{3,4},{4,5},{5,6},{6,7},{7,8},{8,9},{9,10},{10,1... | collective-permute-start | bytes 12582920 | tf_op jit(solution)/shard_map/ppermute | solution.py:467
  51.9 1.3 collective-permute-start.6
  53.2 30.4 %collective-permute-done.3.refs_1_ = f32[4096,128]{1,0:T(8,128)S(1)} collective-permute-done((f32[4096,128]{1,0:T(8,128)}, f32[4096,128]{1,0:T(8,128)S(1)}, u32[]{:S(2)}, u32[]{:S(2)}) %collective-permute-start.3) | collective-permute-done | bytes 2097184 | tf_op jit(solution)/shard_map/ppermute | solution.py:472
  83.6 1.3 copy-done.7
  84.9 1.3 copy-done.8
  86.3 1.3 collective-permute-start.4
  87.6 99.0 %collective-permute-done.4 = f32[4096,128]{1,0:T(8,128)S(1)} collective-permute-done((f32[4096,128]{1,0:T(8,128)}, f32[4096,128]{1,0:T(8,128)S(1)}, u32[]{:S(2)}, u32[]{:S(2)}) %collective-permute-start.4) | collective-permute-done | bytes 2097184 | tf_op jit(solution)/shard_map/ppermute | solution.py:475
  186.6 1.6 broadcast_select_fusion.refs_0_.refs_4_
  188.2 6.2 %shard_map.33.refs_0_.refs_2_ = f32[128,128]{1,0:T(8,128)} custom-call(s32[4]{0:T(128)} %copy-done.4, f32[4096,128]{1,0:T(8,128)} %broadcast_select_fusion.refs_0_.refs_4_, f32[3072,128]{1,0:T(8,128)} %get-tuple-element.24.refs_1_.refs_0_, f32[3072,128]{1,0:T(8,128)} %get-tuple-element.25.refs_2_.refs_1_, f32[1024,128]{1,0:T(8,128)} %get-tuple-element.26.refs_3_.refs_0_, ...), custom_call_target="tpu_custom_call" | custom-call | flops 1000 | bytes 1000 | tf_op jit(solution)/shard_map/pallas_call | solution.py:283
  194.4 1.4 collective-permute-start.14
  195.8 0.8 collective-permute-start.15
  196.6 68.3 %collective-permute-done.5.refs_1_.refs_0_ = f32[8192,128]{1,0:T(8,128)} collective-permute-done((f32[8192,128]{1,0:T(8,128)}, f32[8192,128]{1,0:T(8,128)}, u32[]{:S(2)}, u32[]{:S(2)}) %collective-permute-start.5) | collective-permute-done | bytes 4194336 | tf_op jit(solution)/shard_map/ppermute | solution.py:467
  264.8 4.0 %collective-permute-start.7 = (f32[128,128]{1,0:T(8,128)}, f32[128,128]{1,0:T(8,128)S(1)}, u32[]{:S(2)}, u32[]{:S(2)}) collective-permute-start(f32[128,128]{1,0:T(8,128)} %shard_map.35), channel_id=1, source_target_pairs={{0,65},{1,64},{2,67},{3,66},{4,69},{5,68},{6,71},{7,70},{8,73},{9,... | collective-permute-start | bytes 196616 | tf_op jit(solution)/shard_map/ppermute | solution.py:390
  268.8 2.8 collective-permute-done.7
  271.7 9.0 %shard_map.36 = f32[128,128]{1,0:T(8,128)} custom-call(s32[4]{0:T(128)} %copy-done.4, f32[8192,128]{1,0:T(8,128)} %collective-permute-done.5.refs_1_.refs_0_, f32[8192,128]{1,0:T(8,128)} %collective-permute-done.6.refs_1_, f32[8192,128]{1,0:T(8,128)} %get-tuple-element.22._.refs_2_, f32[8192,128]{1,0:T(8,128)} %get-tuple-element.28.refs_3_), custom_call_target="tpu_custom_call" | custom-call | flops 1000 | bytes 1000 | tf_op jit(solution)/shard_map/pallas_call | solution.py:283
  280.6 1.5 add.15.refs_2_
  282.1 1.3 collective-permute-start.12
  283.4 0.7 collective-permute-start.13
  284.1 0.1 collective-permute-start.9
  284.2 1.5 collective-permute-done.9
  285.7 0.9 add.16.one_ref
  286.5 3.7 %collective-permute-start.10 = (f32[128,128]{1,0:T(8,128)S(1)}, f32[128,128]{1,0:T(8,128)S(1)}, u32[]{:S(2)}, u32[]{:S(2)}) collective-permute-start(f32[128,128]{1,0:T(8,128)S(1)} %add.16.one_ref), channel_id=1, source_target_pairs={{0,3},{1,6},{2,5},{3,0},{4,7},{5,2},{6,1},{7,4},{8,11},{9,14},{10,... | collective-permute-start | bytes 196616 | tf_op jit(solution)/shard_map/ppermute | solution.py:390
  290.2 3.3 collective-permute-done.10
  293.4 5.9 %collective-permute-start.11 = (f32[128,128]{1,0:T(8,128)S(1)}, f32[128,128]{1,0:T(8,128)S(1)}, u32[]{:S(2)}, u32[]{:S(2)}) collective-permute-start(f32[128,128]{1,0:T(8,128)S(1)} %collective-permute-done.10), channel_id=1, source_target_pairs={{0,67},{1,70},{2,69},{3,64},{4,71},{5,66},{6,65},{7,68},{8,75},{9,... | collective-permute-start | bytes 196616 | tf_op jit(solution)/shard_map/ppermute | solution.py:390
  299.4 2.2 collective-permute-done.11.two_ref
  301.6 2.7 shard_map.37
  304.4 0.6 copy-done
  305.0 0.6 copy-done.1
  305.6 11.1 %shard_map.40.refs_5_ = f32[2,12288,128]{2,1,0:T(8,128)} custom-call(s32[4]{0:T(128)} %copy-done.4, bf16[256,256]{1,0:T(8,128)(2,1)} %copy-done, bf16[256,256]{1,0:T(8,128)(2,1)} %copy-done.1, f32[8192,128]{1,0:T(8,128)} %collective-permute-done.5.refs_1_.refs_0_, f32[8192,128]{1,0:T(8,128)} %collective-permute-done.6.refs_1_, ...), custom_call_target="tpu_custom_call" | custom-call | flops 1000 | bytes 1000 | tf_op jit(solution)/shard_map/pallas_call | solution.py:363
  316.7 1.1 copy-done.9
  317.8 1.2 copy-done.10
  319.0 7.2 %shard_map.41.refs_5_ = f32[2,12288,128]{2,1,0:T(8,128)} custom-call(s32[4]{0:T(128)} %copy-done.4, bf16[256,256]{1,0:T(8,128)(2,1)} %copy-done, bf16[256,256]{1,0:T(8,128)(2,1)} %copy-done.1, f32[3072,128]{1,0:T(8,128)} %copy-done.9, f32[3072,128]{1,0:T(8,128)} %copy-done.10, ...), custom_call_target="tpu_custom_call", output_to_operand_aliasing={{}: (8, {})} | custom-call | flops 1000 | bytes 1000 | tf_op jit(solution)/shard_map/pallas_call | solution.py:363
  326.2 0.8 copy-done.11
  327.0 0.8 copy-done.12
  327.8 3.9 %shard_map.42 = f32[2,12288,128]{2,1,0:T(8,128)} custom-call(s32[4]{0:T(128)} %copy-done.4, bf16[256,256]{1,0:T(8,128)(2,1)} %copy-done, bf16[256,256]{1,0:T(8,128)(2,1)} %copy-done.1, f32[1024,128]{1,0:T(8,128)} %copy-done.11, f32[1024,128]{1,0:T(8,128)} %copy-done.12, f32[1024,128]{1,0:T(8,128)} %get-tuple-element.31.refs_2_, ...), custom_call_target="tpu_custom_call", output_to_operand_aliasing={{}: (8, {})} | custom-call | flops 1000 | bytes 1000 | tf_op jit(solution)/shard_map/pallas_call | solution.py:363
  (30 shorter events, 0.1 us)
Async XLA Ops:
  0.0 14.9 %copy-start.6 = (s32[2,4]{1,0:T(2,128)S(1)}, s32[2,4]{1,0:T(2,128)}, u32[]{:S(2)}) copy-start(s32[2,4]{1,0:T(2,128)} %offsets_ref.3) | copy-start | bytes 100
  6.8 1.5 collective-permute-start
  9.1 5.8 %collective-permute-start.1 = (f32[128,128]{1,0:T(8,128)S(1)}, f32[128,128]{1,0:T(8,128)S(1)}, u32[]{:S(2)}, u32[]{:S(2)}) collective-permute-start(f32[128,128]{1,0:T(8,128)S(1)} %add.14.one_ref), channel_id=1, source_target_pairs={{0,64},{32,96},{64,0},{96,32},{1,65},{33,97},{65,1},{97,33},{2,66}... | collective-permute-start | bytes 196616 | tf_op jit(solution)/shard_map/ppermute | solution.py:380
  12.5 6.6 %copy-start.4 = (s32[4]{0:T(128)}, s32[4]{0:T(128)S(1)}, u32[]{:S(2)}) copy-start(s32[4]{0:T(128)S(1)} %pad_add_fusion.flags_ref) | copy-start | bytes 52
  17.8 0.6 copy-start.2
  18.4 0.7 copy-start.3
  35.8 47.8 %collective-permute-start.3 = (f32[4096,128]{1,0:T(8,128)}, f32[4096,128]{1,0:T(8,128)S(1)}, u32[]{:S(2)}, u32[]{:S(2)}) collective-permute-start(f32[4096,128]{1,0:T(8,128)} %get-tuple-element.23), channel_id=1, source_target_pairs={{0,2},{2,4},{4,6},{6,8},{8,10},{10,12},{12,14},{14,16},{16,18},{18... | collective-permute-start | bytes 6291464 | tf_op jit(solution)/shard_map/ppermute | solution.py:472
  39.4 44.2 %collective-permute-start.2 = (f32[4096,128]{1,0:T(8,128)}, f32[4096,128]{1,0:T(8,128)S(1)}, u32[]{:S(2)}, u32[]{:S(2)}) collective-permute-start(f32[4096,128]{1,0:T(8,128)} %get-tuple-element.23), channel_id=1, source_target_pairs={{1,25},{30,6},{33,57},{62,38},{65,89},{94,70},{97,121},{126,102}} | collective-permute-start | bytes 6291464 | tf_op jit(solution)/shard_map/ppermute | solution.py:473
  40.2 224.7 %collective-permute-start.5 = (f32[8192,128]{1,0:T(8,128)}, f32[8192,128]{1,0:T(8,128)}, u32[]{:S(2)}, u32[]{:S(2)}) collective-permute-start(f32[8192,128]{1,0:T(8,128)} %get-tuple-element.22._.refs_2_), channel_id=1, source_target_pairs={{0,1},{1,2},{2,3},{3,4},{4,5},{5,6},{6,7},{7,8},{8,9},{9,10},{10,1... | collective-permute-start | bytes 12582920 | tf_op jit(solution)/shard_map/ppermute | solution.py:467
  51.9 212.9 %collective-permute-start.6 = (f32[8192,128]{1,0:T(8,128)}, f32[8192,128]{1,0:T(8,128)}, u32[]{:S(2)}, u32[]{:S(2)}) collective-permute-start(f32[8192,128]{1,0:T(8,128)} %get-tuple-element.28.refs_3_), channel_id=1, source_target_pairs={{1,0},{2,1},{3,2},{4,3},{5,4},{6,5},{7,6},{8,7},{9,8},{10,9},{11,1... | collective-permute-start | bytes 12582920 | tf_op jit(solution)/shard_map/ppermute | solution.py:468
  83.6 1.3 copy-start.7
  84.9 1.3 copy-start.8
  86.3 100.3 %collective-permute-start.4 = (f32[4096,128]{1,0:T(8,128)}, f32[4096,128]{1,0:T(8,128)S(1)}, u32[]{:S(2)}, u32[]{:S(2)}) collective-permute-start(f32[4096,128]{1,0:T(8,128)} %shard_map.32), channel_id=1, source_target_pairs={{25,0},{6,31},{57,32},{38,63},{89,64},{70,95},{121,96},{102,127}} | collective-permute-start | bytes 6291464 | tf_op jit(solution)/shard_map/ppermute | solution.py:475
  194.4 122.3 %collective-permute-start.14 = (f32[3072,128]{1,0:T(8,128)}, f32[3072,128]{1,0:T(8,128)S(1)}, u32[]{:S(2)}, u32[]{:S(2)}) collective-permute-start(f32[3072,128]{1,0:T(8,128)} %get-tuple-element.33.refs_2_), channel_id=1, source_target_pairs={{0,1},{1,2},{2,3},{3,4},{4,5},{5,6},{6,7},{7,8},{8,9},{9,10},{10,1... | collective-permute-start | bytes 4718600 | tf_op jit(solution)/shard_map/ppermute | solution.py:480
  195.8 120.9 %collective-permute-start.15 = (f32[3072,128]{1,0:T(8,128)}, f32[3072,128]{1,0:T(8,128)S(1)}, u32[]{:S(2)}, u32[]{:S(2)}) collective-permute-start(f32[3072,128]{1,0:T(8,128)} %get-tuple-element.34.refs_3_), channel_id=1, source_target_pairs={{2,1},{3,2},{4,3},{5,4},{6,5},{7,6},{8,7},{9,8},{10,9},{11,10},{12... | collective-permute-start | bytes 4718600 | tf_op jit(solution)/shard_map/ppermute | solution.py:481
  264.8 36.8 %copy-start.5 = (s32[4]{0:T(128)S(1)}, s32[4]{0:T(128)}, u32[]{:S(2)}) copy-start(s32[4]{0:T(128)} %copy-done.4) | copy-start | bytes 52
  264.8 6.8 %collective-permute-start.7 = (f32[128,128]{1,0:T(8,128)}, f32[128,128]{1,0:T(8,128)S(1)}, u32[]{:S(2)}, u32[]{:S(2)}) collective-permute-start(f32[128,128]{1,0:T(8,128)} %shard_map.35), channel_id=1, source_target_pairs={{0,65},{1,64},{2,67},{3,66},{4,69},{5,68},{6,71},{7,70},{8,73},{9,... | collective-permute-start | bytes 196616 | tf_op jit(solution)/shard_map/ppermute | solution.py:390
  271.7 9.0 %collective-permute-start.8 = (f32[128,128]{1,0:T(8,128)S(1)}, f32[128,128]{1,0:T(8,128)S(1)}, u32[]{:S(2)}, u32[]{:S(2)}) collective-permute-start(f32[128,128]{1,0:T(8,128)S(1)} %collective-permute-done.7), channel_id=1, source_target_pairs={{0,2},{1,64},{2,4},{3,1},{4,6},{5,3},{6,8},{7,5},{8,10},{9,7},{10,... | collective-permute-start | bytes 196616 | tf_op jit(solution)/shard_map/ppermute | solution.py:390
  282.1 44.1 %collective-permute-start.12 = (f32[1024,128]{1,0:T(8,128)}, f32[1024,128]{1,0:T(8,128)S(1)}, u32[]{:S(2)}, u32[]{:S(2)}) collective-permute-start(f32[1024,128]{1,0:T(8,128)} %get-tuple-element.31.refs_2_), channel_id=1, source_target_pairs={{0,1},{1,2},{2,3},{3,4},{4,5},{5,6},{6,7},{7,8},{8,9},{9,10},{10,1... | collective-permute-start | bytes 1572872 | tf_op jit(solution)/shard_map/ppermute | solution.py:487
  283.4 42.8 %collective-permute-start.13 = (f32[1024,128]{1,0:T(8,128)}, f32[1024,128]{1,0:T(8,128)S(1)}, u32[]{:S(2)}, u32[]{:S(2)}) collective-permute-start(f32[1024,128]{1,0:T(8,128)} %get-tuple-element.32.refs_3_), channel_id=1, source_target_pairs={{2,1},{3,2},{4,3},{5,4},{6,5},{7,6},{8,7},{9,8},{10,9},{11,10},{12... | collective-permute-start | bytes 1572872 | tf_op jit(solution)/shard_map/ppermute | solution.py:488
  284.1 1.5 collective-permute-start.9
  286.5 6.9 %collective-permute-start.10 = (f32[128,128]{1,0:T(8,128)S(1)}, f32[128,128]{1,0:T(8,128)S(1)}, u32[]{:S(2)}, u32[]{:S(2)}) collective-permute-start(f32[128,128]{1,0:T(8,128)S(1)} %add.16.one_ref), channel_id=1, source_target_pairs={{0,3},{1,6},{2,5},{3,0},{4,7},{5,2},{6,1},{7,4},{8,11},{9,14},{10,... | collective-permute-start | bytes 196616 | tf_op jit(solution)/shard_map/ppermute | solution.py:390
  293.4 8.2 %collective-permute-start.11 = (f32[128,128]{1,0:T(8,128)S(1)}, f32[128,128]{1,0:T(8,128)S(1)}, u32[]{:S(2)}, u32[]{:S(2)}) collective-permute-start(f32[128,128]{1,0:T(8,128)S(1)} %collective-permute-done.10), channel_id=1, source_target_pairs={{0,67},{1,70},{2,69},{3,64},{4,71},{5,66},{6,65},{7,68},{8,75},{9,... | collective-permute-start | bytes 196616 | tf_op jit(solution)/shard_map/ppermute | solution.py:390
  304.3 0.6 copy-start
  305.0 0.6 copy-start.1
  316.7 1.2 copy-start.9
  317.8 1.2 copy-start.10
  326.2 0.8 copy-start.11
  327.0 0.8 copy-start.12

commit v6 on v5

--- a/solution.py
+++ b/solution.py
@@ -226,22 +226,13 @@
         gram_ref[...] = gram_of_terms(a_ref[...]) + swapped(swapped(other, 0), 1)
 
 
-def neighbour_halves(early, step, flags_ref, add, got_ref, *own_refs):
-    def with_own(u_ref, w_ref):
-        own = jnp.where(flags_ref[2] == 1, u_ref[...], w_ref[...])
-        at_end = flags_ref[0] + flags_ref[1]
-        own = jnp.where(at_end == 1, swapped(own, 1), own)
-        got = got_ref[...]
-        own_first = flags_ref[3] == 1
-        add(jnp.where(own_first, own, got), jnp.where(own_first, got, own))
-
-    @pl.when(step < early)
-    def _():
-        with_own(*own_refs[:2])
-
-    @pl.when(step >= early)
-    def _():
-        with_own(*own_refs[2:])
+def neighbour_halves(step, flags_ref, add, got_ref, u_ref, w_ref):
+    own = jnp.where(flags_ref[2] == 1, u_ref[...], w_ref[...])
+    at_end = flags_ref[0] + flags_ref[1]
+    own = jnp.where(at_end == 1, swapped(own, 1), own)
+    got = got_ref[...]
+    own_first = flags_ref[3] == 1
+    add(jnp.where(own_first, own, got), jnp.where(own_first, got, own))
 
 
 def arrived_halves(step, flags_ref, add, up_ref, down_ref, u_ref, w_ref):
@@ -295,20 +286,11 @@
     )(flags, *operands)
 
 
-def neighbour_gram(flags, got, u2, w2, u3, w3, block):
+def neighbour_gram(flags, got, u, w, block):
     rows, width = got.shape
-    early = u2.shape[0] // block
-    late = u3.shape[0] // block
-    one = run_spec(0, early, block, width)
-    two = run_spec(early, late, block, width)
-    every = run_spec(0, early + late, block, width)
-    return gram_call(
-        functools.partial(neighbour_halves, early),
-        flags,
-        [got, u2, w2, u3, w3],
-        [every, one, one, two, two],
-        early + late,
-    )
+    steps = rows // block
+    every = run_spec(0, steps, block, width)
+    return gram_call(neighbour_halves, flags, [got, u, w], [every] * 3, steps)
 
 
 def kept_spec(block, width):
@@ -435,8 +417,8 @@
 def body(x, offsets):
     rows, width = x.shape
     half_rows = rows // 2
-    large, small = half_rows // 6, half_rows // 12
-    late, final = 8 * small, 11 * small
+    block = half_rows // 8
+    late = 5 * block
     place = lax.axis_index("loop")
     count = lax.axis_size("loop")
     last = count - 1
@@ -463,42 +445,33 @@
     gram = gram + row_partner(gram, 1)
     a, b = rotations(0, flags, offsets, gram, row_partner(gram, 2))
 
-    u0, w0 = first_product(flags, halves, a, b, halves, 0, large, [(0, 4)], False)
+    u0, w0 = first_product(flags, halves, a, b, halves, 0, block, [(0, 5)], False)
     up0 = lax.ppermute(u0, "loop", ups)
     down0 = lax.ppermute(w0, "loop", downs)
-    u1, w1, u2, w2, sent = first_product(
-        flags, halves, a, b, u0, late, small, [(0, 3), (3, 1)], True
-    )
+    u1, w1, sent = first_product(flags, halves, a, b, u0, late, block, [(0, 3)], True)
     got = lax.ppermute(sent, "loop", skips)
     ends = lax.ppermute(sent, "loop", [(1, by_down), (last - 1, by_up)])
     (ends,) = held([ends], got)
     ends = lax.ppermute(ends, "loop", [(by_down, 0), (by_up, last)])
-    got = jnp.where((place == 0) | (place == last), ends, got)
-
-    gram = neighbour_gram(flags, got, u1, w1, u2, w2, small)
-    u1, w1 = held([u1, w1], gram)
+    u1, w1 = held([u1, w1], got)
     up1 = lax.ppermute(u1, "loop", ups[:-1])
     down1 = lax.ppermute(w1, "loop", downs[1:])
+    got = jnp.where((place == 0) | (place == last), ends, got)
+
+    gram = neighbour_gram(flags, got, u1, w1, block)
     (gram,) = held([gram], up0)
     (gram,) = held([gram], down0)
     gram = home(gram, last)
-    gram = gram + arrived_gram(flags, up0, down0, u0, w0, large)
-    u2, w2 = held([u2, w2], gram)
-    up2 = lax.ppermute(u2, "loop", ups[:-1])
-    down2 = lax.ppermute(w2, "loop", downs[1:])
+    gram = gram + arrived_gram(flags, up0, down0, u0, w0, block)
     gram = gram + row_partner(gram, 1)
     a, b = rotations(1, flags, offsets, gram, far_partner(gram, count))
 
-    out = None
-    for arrays, got_start, low, size in (
-        ((up0, down0, u0, w0), None, 0, large),
-        ((up1, down1, u1, w1), 0, late, small),
-        ((up2, down2, u2, w2), final - late, final, small),
-    ):
-        skipped = None if got_start is None else got
-        out = second_product(
-            flags, a, b, arrays, skipped, got_start or 0, out, low, half_rows, size
-        )
+    out = second_product(
+        flags, a, b, (up0, down0, u0, w0), None, 0, None, 0, half_rows, block
+    )
+    out = second_product(
+        flags, a, b, (up1, down1, u1, w1), got, 0, out, late, half_rows, block
+    )
     return out.reshape(rows, width)
 
 

time: 333 us -> 331 us (level)
  local copies, waits for them, and re-layouts: 9.12 us -> 5.42 us
    ppermute x1, waiting for transfers between devices: 99 us -> 84.5 us  [body(): ends = lax.ppermute(ends, 'loop', [(by_down, 0), (by_up, last)])]
    ppermute x1, starting transfers between devices: 1.38 us -> 11.3 us  [body(): up1 = lax.ppermute(u1, 'loop', ups[:-1])]
    ppermute x4, starting transfers between devices: 13.6 us -> 6.68 us  [everywhere(): return lax.ppermute(x, ('rows', 'loop'), pairs)]
    ppermute x1, waiting for transfers between devices: 30.4 us -> 36.1 us  [body(): got = lax.ppermute(sent, 'loop', skips)]
    unnamed x26 -> x20, local copies, waits for them, and re-layouts: 9.12 us -> 5.42 us
    ppermute x4, waiting for transfers between devices: 8.31 us -> 11.8 us  [everywhere(): return lax.ppermute(x, ('rows', 'loop'), pairs)]
    pallas_call x3 -> x2, Pallas kernels: 22.1 us -> 21.1 us  [second_product(): pl.pallas_call(functools.partial(second_product_kernel, halves, count), g...]
  transfers between devices with their start and end apart: 16 -> 14, of which waited for: 9 -> 10; matrix products, arithmetic and copies ran while one was open for 1% -> 1% of each run, Pallas kernels for 11% -> 9%
where the time goes in v6:
time: 331 us; the launch traced here: 330 us
  waiting for transfers between devices  211 us (64%)
  Pallas kernels  66.9 us (20%)
  starting transfers between devices  41.9 us (13%)
  local copies, waits for them, and re-layouts  5.42 us (2%)
  other arithmetic  5.23 us (2%)
    ppermute x1, waiting for transfers between devices, body(): ends = lax.ppermute(ends, 'loop', [(by_down, 0), (by_up, last)])  84.5 us
    ppermute x1, waiting for transfers between devices, body(): up0 = lax.ppermute(u0, 'loop', ups)  69.8 us
    ppermute x1, waiting for transfers between devices, body(): got = lax.ppermute(sent, 'loop', skips)  36.1 us
    pallas_call x2, Pallas kernels, second_product(): pl.pallas_call(functools.partial(second_product_kernel, halves, count), g...  21.1 us
    pallas_call x2, Pallas kernels, first_product(): pl.pallas_call(functools.partial(first_product_kernel, runs, skip), grid_...  17.9 us
    pallas_call x2, Pallas kernels, gram_call(): pl.pallas_call(functools.partial(packed_gram_kernel, halves), grid_spec=p...  15.4 us
    ppermute x4, waiting for transfers between devices, everywhere(): return lax.ppermute(x, ('rows', 'loop'), pairs)  11.8 us
    ppermute x1, starting transfers between devices, body(): up0 = lax.ppermute(u0, 'loop', ups)  11.6 us
  transfers between devices with their start and end apart: 14, of which 10 were waited for; matrix products, arithmetic and copies ran while one was open for 1% of the time, Pallas kernels for 9%

profile of v6, /device:TPU:0, one launch (start us, length us, event | category | flops | bytes accessed | tf_op | source)
XLA Modules:
  0.0 330.1 jit_solution(5041190231937824662)
XLA Ops:
  0.0 6.8 %shard_map.28 = f32[128,128]{1,0:T(8,128)} custom-call(f32[24576,128]{1,0:T(8,128)} %x_ref.1), custom_call_target="tpu_custom_call" | custom-call | flops 1000 | bytes 1000 | tf_op jit(solution)/shard_map/pallas_call | solution.py:80
  6.8 0.0 collective-permute-start
  6.8 1.5 collective-permute-done
  8.2 0.9 add.14.one_ref
  9.1 3.3 collective-permute-start.1
  12.4 0.1 pad_add_fusion.flags_ref
  12.5 2.4 collective-permute-done.1.two_ref
  14.9 0.0 copy-done.6
  14.9 2.9 shard_map.29
  17.8 0.7 copy-done.2
  18.4 0.6 copy-done.3
  19.1 10.4 %shard_map.30 = (f32[7680,128]{1,0:T(8,128)}, f32[7680,128]{1,0:T(8,128)}) custom-call(s32[4]{0:T(128)} %copy-done.4, f32[2,12288,128]{2,1,0:T(8,128)} %bitcast.6, bf16[256,256]{1,0:T(8,128)(2,1)} %copy-done.2, bf16[256,256]{1,0:T(8,128)(2,1)} %copy-done.3, f32[2,12288,128]{2,1,0:T(8,128)} %bitcast.7), custom_call_target="tpu_custom_call" | custom-call | flops 1000 | bytes 1000 | tf_op jit(solution)/shard_map/pallas_call | solution.py:188
  29.5 7.5 %shard_map.31 = (f32[4608,128]{1,0:T(8,128)}, f32[4608,128]{1,0:T(8,128)}, f32[4608,128]{1,0:T(8,128)}) custom-call(s32[4]{0:T(128)} %copy-done.4, f32[2,12288,128]{2,1,0:T(8,128)} %bitcast.8, bf16[256,256]{1,0:T(8,128)(2,1)} %copy-done.2, bf16[256,256]{1,0:T(8,128)(2,1)} %copy-done.3, f32[7680,128]{1,0:T(8,128)} %get-tuple-element.18._.refs_2_), custom_call_target="tpu_custom_call" | custom-call | flops 1000 | bytes 1000 | tf_op jit(solution)/shard_map/pallas_call | solution.py:188
  37.0 3.6 %collective-permute-start.3 = (f32[4608,128]{1,0:T(8,128)}, f32[4608,128]{1,0:T(8,128)S(1)}, u32[]{:S(2)}, u32[]{:S(2)}) collective-permute-start(f32[4608,128]{1,0:T(8,128)} %get-tuple-element.19), channel_id=1, source_target_pairs={{0,2},{2,4},{4,6},{6,8},{8,10},{10,12},{12,14},{14,16},{16,18},{18... | collective-permute-start | bytes 7077896 | tf_op jit(solution)/shard_map/ppermute | solution.py:452
  40.7 0.8 collective-permute-start.2
  41.5 11.6 %collective-permute-start.5 = (f32[7680,128]{1,0:T(8,128)}, f32[7680,128]{1,0:T(8,128)}, u32[]{:S(2)}, u32[]{:S(2)}) collective-permute-start(f32[7680,128]{1,0:T(8,128)} %get-tuple-element.18._.refs_2_), channel_id=1, source_target_pairs={{0,1},{1,2},{2,3},{3,4},{4,5},{5,6},{6,7},{7,8},{8,9},{9,10},{10,1... | collective-permute-start | bytes 11796488 | tf_op jit(solution)/shard_map/ppermute | solution.py:449
  53.1 1.3 collective-permute-start.6
  54.4 36.1 %collective-permute-done.3.refs_1_.refs_2_ = f32[4608,128]{1,0:T(8,128)S(1)} collective-permute-done((f32[4608,128]{1,0:T(8,128)}, f32[4608,128]{1,0:T(8,128)S(1)}, u32[]{:S(2)}, u32[]{:S(2)}) %collective-permute-start.3) | collective-permute-done | bytes 2359328 | tf_op jit(solution)/shard_map/ppermute | solution.py:452
  90.5 0.0 collective-permute-done.2.refs_0_
  90.5 1.4 copy-done.7
  91.9 1.4 copy-done.9
  93.3 1.3 collective-permute-start.4
  94.6 11.3 %collective-permute-start.12 = (f32[4608,128]{1,0:T(8,128)}, f32[4608,128]{1,0:T(8,128)}, u32[]{:S(2)}, u32[]{:S(2)}) collective-permute-start(f32[4608,128]{1,0:T(8,128)} %get-tuple-element.22.refs_1_.refs_2_), channel_id=1, source_target_pairs={{0,1},{1,2},{2,3},{3,4},{4,5},{5,6},{6,7},{7,8},{8,9},{9,10},{10,1... | collective-permute-start | bytes 7077896 | tf_op jit(solution)/shard_map/ppermute | solution.py:457
  105.9 2.0 collective-permute-start.13
  107.9 84.5 %collective-permute-done.4 = f32[4608,128]{1,0:T(8,128)} collective-permute-done((f32[4608,128]{1,0:T(8,128)}, f32[4608,128]{1,0:T(8,128)}, u32[]{:S(2)}, u32[]{:S(2)}) %collective-permute-start.4) | collective-permute-done | bytes 2359328 | tf_op jit(solution)/shard_map/ppermute | solution.py:455
  192.4 3.4 %broadcast_select_fusion.refs_0_.refs_4_ = f32[4608,128]{1,0:T(8,128)} fusion(f32[4608,128]{1,0:T(8,128)} %collective-permute-done.4, f32[4608,128]{1,0:T(8,128)S(1)} %copy-done.8, pred[]{:T(512)S(6)} %or.7), kind=kLoop, calls=%fused_computation | loop fusion | flops 589824 | bytes 7077889 | tf_op jit(solution)/shard_map/jit(_where)/select_n | solution.py:459
  195.8 6.1 %shard_map.34.refs_0_ = f32[128,128]{1,0:T(8,128)} custom-call(s32[4]{0:T(128)} %copy-done.4, f32[4608,128]{1,0:T(8,128)} %broadcast_select_fusion.refs_0_.refs_4_, f32[4608,128]{1,0:T(8,128)} %get-tuple-element.22.refs_1_.refs_2_, f32[4608,128]{1,0:T(8,128)} %get-tuple-element.23.refs_2_.refs_3_), custom_call_target="tpu_custom_call" | custom-call | flops 1000 | bytes 1000 | tf_op jit(solution)/shard_map/pallas_call | solution.py:274
  201.9 69.8 %collective-permute-done.5.refs_1_.refs_0_ = f32[7680,128]{1,0:T(8,128)} collective-permute-done((f32[7680,128]{1,0:T(8,128)}, f32[7680,128]{1,0:T(8,128)}, u32[]{:S(2)}, u32[]{:S(2)}) %collective-permute-start.5) | collective-permute-done | bytes 3932192 | tf_op jit(solution)/shard_map/ppermute | solution.py:449
  271.7 0.0 collective-permute-done.6.refs_1_
  271.7 4.0 %collective-permute-start.7 = (f32[128,128]{1,0:T(8,128)}, f32[128,128]{1,0:T(8,128)S(1)}, u32[]{:S(2)}, u32[]{:S(2)}) collective-permute-start(f32[128,128]{1,0:T(8,128)} %shard_map.36), channel_id=1, source_target_pairs={{0,65},{1,64},{2,67},{3,66},{4,69},{5,68},{6,71},{7,70},{8,73},{9,... | collective-permute-start | bytes 196616 | tf_op jit(solution)/shard_map/ppermute | solution.py:372
  275.7 2.8 collective-permute-done.7
  278.6 0.0 collective-permute-start.8
  278.6 9.3 %shard_map.37 = f32[128,128]{1,0:T(8,128)} custom-call(s32[4]{0:T(128)} %copy-done.4, f32[7680,128]{1,0:T(8,128)} %collective-permute-done.5.refs_1_.refs_0_, f32[7680,128]{1,0:T(8,128)} %collective-permute-done.6.refs_1_, f32[7680,128]{1,0:T(8,128)} %get-tuple-element.18._.refs_2_, f32[7680,128]{1,0:T(8,128)} %get-tuple-element.24.refs_3_), custom_call_target="tpu_custom_call" | custom-call | flops 1000 | bytes 1000 | tf_op jit(solution)/shard_map/pallas_call | solution.py:274
  287.9 0.0 collective-permute-done.8
  287.9 0.9 add.15
  288.7 0.0 collective-permute-start.9
  288.7 1.2 collective-permute-done.9
  290.0 0.1 collective-permute-start.10
  290.1 5.2 %collective-permute-done.10 = f32[128,128]{1,0:T(8,128)S(1)} collective-permute-done((f32[128,128]{1,0:T(8,128)S(1)}, f32[128,128]{1,0:T(8,128)S(1)}, u32[]{:S(2)}, u32[]{:S(2)}) %collective-permute-start.10) | collective-permute-done | bytes 65568 | tf_op jit(solution)/shard_map/ppermute | solution.py:372
  295.2 2.6 collective-permute-start.11
  297.8 3.8 %collective-permute-done.11.two_ref = f32[128,128]{1,0:T(8,128)S(1)} collective-permute-done((f32[128,128]{1,0:T(8,128)S(1)}, f32[128,128]{1,0:T(8,128)S(1)}, u32[]{:S(2)}, u32[]{:S(2)}) %collective-permute-start.11) | collective-permute-done | bytes 65568 | tf_op jit(solution)/shard_map/ppermute | solution.py:372
  301.6 2.7 shard_map.38
  304.4 0.6 copy-done
  305.0 0.7 copy-done.1
  305.6 12.2 %shard_map.39.refs_5_ = f32[2,12288,128]{2,1,0:T(8,128)} custom-call(s32[4]{0:T(128)} %copy-done.4, bf16[256,256]{1,0:T(8,128)(2,1)} %copy-done, bf16[256,256]{1,0:T(8,128)(2,1)} %copy-done.1, f32[7680,128]{1,0:T(8,128)} %collective-permute-done.5.refs_1_.refs_0_, f32[7680,128]{1,0:T(8,128)} %collective-permute-done.6.refs_1_, ...), custom_call_target="tpu_custom_call" | custom-call | flops 1000 | bytes 1000 | tf_op jit(solution)/shard_map/pallas_call | solution.py:345
  317.8 3.3 %collective-permute-done.12.refs_0_ = f32[4608,128]{1,0:T(8,128)} collective-permute-done((f32[4608,128]{1,0:T(8,128)}, f32[4608,128]{1,0:T(8,128)}, u32[]{:S(2)}, u32[]{:S(2)}) %collective-permute-start.12) | collective-permute-done | bytes 2359328 | tf_op jit(solution)/shard_map/ppermute | solution.py:457
  321.1 0.0 collective-permute-done.13.refs_1_
  321.1 8.9 %shard_map.40 = f32[2,12288,128]{2,1,0:T(8,128)} custom-call(s32[4]{0:T(128)} %copy-done.4, bf16[256,256]{1,0:T(8,128)(2,1)} %copy-done, bf16[256,256]{1,0:T(8,128)(2,1)} %copy-done.1, f32[4608,128]{1,0:T(8,128)} %collective-permute-done.12.refs_0_, f32[4608,128]{1,0:T(8,128)} %collective-permute-done.13.refs_1_, ...), custom_call_target="tpu_custom_call", output_to_operand_aliasing={{}: (8, {})} | custom-call | flops 1000 | bytes 1000 | tf_op jit(solution)/shard_map/pallas_call | solution.py:345
  (18 shorter events, 0.0 us)
Async XLA Ops:
  0.0 14.9 %copy-start.6 = (s32[2,4]{1,0:T(2,128)S(1)}, s32[2,4]{1,0:T(2,128)}, u32[]{:S(2)}) copy-start(s32[2,4]{1,0:T(2,128)} %offsets_ref.3) | copy-start | bytes 100
  6.8 1.5 collective-permute-start
  9.1 5.8 %collective-permute-start.1 = (f32[128,128]{1,0:T(8,128)S(1)}, f32[128,128]{1,0:T(8,128)S(1)}, u32[]{:S(2)}, u32[]{:S(2)}) collective-permute-start(f32[128,128]{1,0:T(8,128)S(1)} %add.14.one_ref), channel_id=1, source_target_pairs={{0,64},{32,96},{64,0},{96,32},{1,65},{33,97},{65,1},{97,33},{2,66}... | collective-permute-start | bytes 196616 | tf_op jit(solution)/shard_map/ppermute | solution.py:362
  12.5 6.6 %copy-start.4 = (s32[4]{0:T(128)}, s32[4]{0:T(128)S(1)}, u32[]{:S(2)}) copy-start(s32[4]{0:T(128)S(1)} %pad_add_fusion.flags_ref) | copy-start | bytes 52
  17.8 0.7 copy-start.2
  18.4 0.6 copy-start.3
  37.0 53.5 %collective-permute-start.3 = (f32[4608,128]{1,0:T(8,128)}, f32[4608,128]{1,0:T(8,128)S(1)}, u32[]{:S(2)}, u32[]{:S(2)}) collective-permute-start(f32[4608,128]{1,0:T(8,128)} %get-tuple-element.19), channel_id=1, source_target_pairs={{0,2},{2,4},{4,6},{6,8},{8,10},{10,12},{12,14},{14,16},{16,18},{18... | collective-permute-start | bytes 7077896 | tf_op jit(solution)/shard_map/ppermute | solution.py:452
  40.7 49.8 %collective-permute-start.2 = (f32[4608,128]{1,0:T(8,128)}, f32[4608,128]{1,0:T(8,128)S(1)}, u32[]{:S(2)}, u32[]{:S(2)}) collective-permute-start(f32[4608,128]{1,0:T(8,128)} %get-tuple-element.19), channel_id=1, source_target_pairs={{1,25},{30,6},{33,57},{62,38},{65,89},{94,70},{97,121},{126,102}} | collective-permute-start | bytes 7077896 | tf_op jit(solution)/shard_map/ppermute | solution.py:453
  41.5 230.2 %collective-permute-start.5 = (f32[7680,128]{1,0:T(8,128)}, f32[7680,128]{1,0:T(8,128)}, u32[]{:S(2)}, u32[]{:S(2)}) collective-permute-start(f32[7680,128]{1,0:T(8,128)} %get-tuple-element.18._.refs_2_), channel_id=1, source_target_pairs={{0,1},{1,2},{2,3},{3,4},{4,5},{5,6},{6,7},{7,8},{8,9},{9,10},{10,1... | collective-permute-start | bytes 11796488 | tf_op jit(solution)/shard_map/ppermute | solution.py:449
  53.1 218.6 %collective-permute-start.6 = (f32[7680,128]{1,0:T(8,128)}, f32[7680,128]{1,0:T(8,128)}, u32[]{:S(2)}, u32[]{:S(2)}) collective-permute-start(f32[7680,128]{1,0:T(8,128)} %get-tuple-element.24.refs_3_), channel_id=1, source_target_pairs={{1,0},{2,1},{3,2},{4,3},{5,4},{6,5},{7,6},{8,7},{9,8},{10,9},{11,1... | collective-permute-start | bytes 11796488 | tf_op jit(solution)/shard_map/ppermute | solution.py:450
  90.5 1.4 copy-start.7
  91.9 1.4 copy-start.9
  93.3 99.1 %collective-permute-start.4 = (f32[4608,128]{1,0:T(8,128)}, f32[4608,128]{1,0:T(8,128)}, u32[]{:S(2)}, u32[]{:S(2)}) collective-permute-start(f32[4608,128]{1,0:T(8,128)} %shard_map.32), channel_id=1, source_target_pairs={{25,0},{6,31},{57,32},{38,63},{89,64},{70,95},{121,96},{102,127}} | collective-permute-start | bytes 7077896 | tf_op jit(solution)/shard_map/ppermute | solution.py:455
  94.6 97.8 %copy-start.8 = (f32[4608,128]{1,0:T(8,128)S(1)}, f32[4608,128]{1,0:T(8,128)}, u32[]{:S(2)}) copy-start(f32[4608,128]{1,0:T(8,128)} %copy-done.7) | copy-start | bytes 7077892
  94.6 226.5 %collective-permute-start.12 = (f32[4608,128]{1,0:T(8,128)}, f32[4608,128]{1,0:T(8,128)}, u32[]{:S(2)}, u32[]{:S(2)}) collective-permute-start(f32[4608,128]{1,0:T(8,128)} %get-tuple-element.22.refs_1_.refs_2_), channel_id=1, source_target_pairs={{0,1},{1,2},{2,3},{3,4},{4,5},{5,6},{6,7},{7,8},{8,9},{9,10},{10,1... | collective-permute-start | bytes 7077896 | tf_op jit(solution)/shard_map/ppermute | solution.py:457
  105.9 215.3 %collective-permute-start.13 = (f32[4608,128]{1,0:T(8,128)}, f32[4608,128]{1,0:T(8,128)}, u32[]{:S(2)}, u32[]{:S(2)}) collective-permute-start(f32[4608,128]{1,0:T(8,128)} %get-tuple-element.23.refs_2_.refs_3_), channel_id=1, source_target_pairs={{2,1},{3,2},{4,3},{5,4},{6,5},{7,6},{8,7},{9,8},{10,9},{11,10},{12... | collective-permute-start | bytes 7077896 | tf_op jit(solution)/shard_map/ppermute | solution.py:458
  271.7 29.9 %copy-start.5 = (s32[4]{0:T(128)S(1)}, s32[4]{0:T(128)}, u32[]{:S(2)}) copy-start(s32[4]{0:T(128)} %copy-done.4) | copy-start | bytes 52
  271.7 6.8 %collective-permute-start.7 = (f32[128,128]{1,0:T(8,128)}, f32[128,128]{1,0:T(8,128)S(1)}, u32[]{:S(2)}, u32[]{:S(2)}) collective-permute-start(f32[128,128]{1,0:T(8,128)} %shard_map.36), channel_id=1, source_target_pairs={{0,65},{1,64},{2,67},{3,66},{4,69},{5,68},{6,71},{7,70},{8,73},{9,... | collective-permute-start | bytes 196616 | tf_op jit(solution)/shard_map/ppermute | solution.py:372
  278.6 9.3 %collective-permute-start.8 = (f32[128,128]{1,0:T(8,128)S(1)}, f32[128,128]{1,0:T(8,128)S(1)}, u32[]{:S(2)}, u32[]{:S(2)}) collective-permute-start(f32[128,128]{1,0:T(8,128)S(1)} %collective-permute-done.7), channel_id=1, source_target_pairs={{0,2},{1,64},{2,4},{3,1},{4,6},{5,3},{6,8},{7,5},{8,10},{9,7},{10,... | collective-permute-start | bytes 196616 | tf_op jit(solution)/shard_map/ppermute | solution.py:372
  288.7 1.3 collective-permute-start.9
  290.0 5.2 %collective-permute-start.10 = (f32[128,128]{1,0:T(8,128)S(1)}, f32[128,128]{1,0:T(8,128)S(1)}, u32[]{:S(2)}, u32[]{:S(2)}) collective-permute-start(f32[128,128]{1,0:T(8,128)S(1)} %add.16.one_ref), channel_id=1, source_target_pairs={{0,3},{1,6},{2,5},{3,0},{4,7},{5,2},{6,1},{7,4},{8,11},{9,14},{10,... | collective-permute-start | bytes 196616 | tf_op jit(solution)/shard_map/ppermute | solution.py:372
  295.2 6.4 %collective-permute-start.11 = (f32[128,128]{1,0:T(8,128)S(1)}, f32[128,128]{1,0:T(8,128)S(1)}, u32[]{:S(2)}, u32[]{:S(2)}) collective-permute-start(f32[128,128]{1,0:T(8,128)S(1)} %collective-permute-done.10), channel_id=1, source_target_pairs={{0,67},{1,70},{2,69},{3,64},{4,71},{5,66},{6,65},{7,68},{8,75},{9,... | collective-permute-start | bytes 196616 | tf_op jit(solution)/shard_map/ppermute | solution.py:372
  304.3 0.6 copy-start
  305.0 0.7 copy-start.1

commit v7 on v6

--- a/solution.py
+++ b/solution.py
@@ -158,7 +158,7 @@
     )
 
 
-def first_product_kernel(runs, skip, flags_ref, x_ref, a_ref, b_ref, _, *out_refs):
+def first_product_kernel(runs, flags_ref, x_ref, a_ref, b_ref, *out_refs):
     ya = times(x_ref[0], a_ref[...])
     yb = times(x_ref[1], b_ref[...])
     left = left_lanes(ya.shape)
@@ -172,36 +172,35 @@
             out_refs[2 * which][...] = up
             out_refs[2 * which + 1][...] = down
 
-    if skip:
-        out_refs[2 * len(runs)][...] = jnp.where(flags_ref[2] == 1, down, up)
-
-
-def first_product(flags, x, a, b, earlier, start, block, runs, skip):
+    @pl.when(step >= runs[-1][0])
+    def _():
+        out_refs[-1][...] = jnp.where(flags_ref[2] == 1, down, up)
+
+
+def first_product(flags, x, a, b, block, runs):
     width = x.shape[2]
     steps = sum(count for _, count in runs)
-    first = start // block
     whole = pl.BlockSpec(a.shape, lambda i, f: (0, 0))
     out_specs, out_shape = [], []
-    for low, count in [run for run in runs for _ in range(2)] + [(0, steps)] * skip:
+    for low, count in [run for run in runs for _ in range(2)] + runs[-1:]:
         out_specs.append(run_spec(low, count, block, width))
         out_shape.append(jax.ShapeDtypeStruct((count * block, width), F32))
     return pl.pallas_call(
-        functools.partial(first_product_kernel, runs, skip),
+        functools.partial(first_product_kernel, runs),
         grid_spec=pltpu.PrefetchScalarGridSpec(
             num_scalar_prefetch=1,
             grid=(steps,),
             in_specs=[
-                pl.BlockSpec((2, block, width), lambda i, f: (0, i + first, 0)),
+                pl.BlockSpec((2, block, width), lambda i, f: (0, i, 0)),
                 whole,
                 whole,
-                pl.BlockSpec(memory_space=pl.ANY),
             ],
             out_specs=out_specs,
         ),
         out_shape=out_shape,
         cost_estimate=HINT,
-        compiler_params=params(),
-    )(flags, x, a, b, earlier)
+        compiler_params=params(48),
+    )(flags, x, a, b)
 
 
 def packed_gram_kernel(halves, flags_ref, *refs):
@@ -353,7 +352,7 @@
         out_shape=jax.ShapeDtypeStruct((2, total, width), F32),
         input_output_aliases=aliases,
         cost_estimate=HINT,
-        compiler_params=params(),
+        compiler_params=params(48),
     )(flags, a, b, *operands)
 
 
@@ -445,10 +444,11 @@
     gram = gram + row_partner(gram, 1)
     a, b = rotations(0, flags, offsets, gram, row_partner(gram, 2))
 
-    u0, w0 = first_product(flags, halves, a, b, halves, 0, block, [(0, 5)], False)
+    u0, w0, u1, w1, sent = first_product(
+        flags, halves, a, b, block, [(0, 5), (5, 3)]
+    )
     up0 = lax.ppermute(u0, "loop", ups)
     down0 = lax.ppermute(w0, "loop", downs)
-    u1, w1, sent = first_product(flags, halves, a, b, u0, late, block, [(0, 3)], True)
     got = lax.ppermute(sent, "loop", skips)
     ends = lax.ppermute(sent, "loop", [(1, by_down), (last - 1, by_up)])
     (ends,) = held([ends], got)

time: 331 us -> 327 us (0.988)
  Pallas kernels: 66.9 us -> 61.2 us
    pallas_call x2 -> x1, Pallas kernels: 17.9 us -> 13.9 us  [first_product(): pl.pallas_call(functools.partial(first_product_kernel, runs), grid_spec=p...]
where the time goes in v7:
time: 327 us
  waiting for transfers between devices  214 us (65%)
  Pallas kernels  61.2 us (19%)
  starting transfers between devices  40.5 us (12%)
  local copies, waits for them, and re-layouts  5.81 us (2%)
  other arithmetic  5.1 us (2%)
    ppermute x1, waiting for transfers between devices, body(): ends = lax.ppermute(ends, 'loop', [(by_down, 0), (by_up, last)])  85.9 us
    ppermute x1, waiting for transfers between devices, body(): up0 = lax.ppermute(u0, 'loop', ups)  69.9 us
    ppermute x1, waiting for transfers between devices, body(): got = lax.ppermute(sent, 'loop', skips)  36.1 us
    pallas_call x2, Pallas kernels, second_product(): pl.pallas_call(functools.partial(second_product_kernel, halves, count), g...  19.5 us
    pallas_call x2, Pallas kernels, gram_call(): pl.pallas_call(functools.partial(packed_gram_kernel, halves), grid_spec=p...  15.4 us
    pallas_call x1, Pallas kernels, first_product(): pl.pallas_call(functools.partial(first_product_kernel, runs), grid_spec=p...  13.9 us
    ppermute x4, waiting for transfers between devices, everywhere(): return lax.ppermute(x, ('rows', 'loop'), pairs)  11.8 us
    ppermute x1, starting transfers between devices, body(): up0 = lax.ppermute(u0, 'loop', ups)  11.7 us
  transfers between devices with their start and end apart: 14, of which 10 were waited for; matrix products, arithmetic and copies ran while one was open for 1% of the time, Pallas kernels for 9%

profile of v7, /device:TPU:0, one launch (start us, length us, event | category | flops | bytes accessed | tf_op | source)
XLA Modules:
  0.0 326.6 jit_solution(1790733743965148369)
XLA Ops:
  0.0 0.0 copy-start.4
  0.0 6.8 %shard_map.28 = f32[128,128]{1,0:T(8,128)} custom-call(f32[24576,128]{1,0:T(8,128)} %x_ref.1), custom_call_target="tpu_custom_call" | custom-call | flops 1000 | bytes 1000 | tf_op jit(solution)/shard_map/pallas_call | solution.py:80
  6.8 0.0 collective-permute-start
  6.8 1.5 collective-permute-done
  8.2 0.9 add.14.one_ref
  9.1 3.3 %collective-permute-start.1 = (f32[128,128]{1,0:T(8,128)S(1)}, f32[128,128]{1,0:T(8,128)S(1)}, u32[]{:S(2)}, u32[]{:S(2)}) collective-permute-start(f32[128,128]{1,0:T(8,128)S(1)} %add.14.one_ref), channel_id=1, source_target_pairs={{0,64},{32,96},{64,0},{96,32},{1,65},{33,97},{65,1},{97,33},{2,66}... | collective-permute-start | bytes 196616 | tf_op jit(solution)/shard_map/ppermute | solution.py:361
  12.4 0.1 pad_add_fusion.flags_ref
  12.5 2.4 collective-permute-done.1.two_ref
  14.9 0.0 copy-done.4
  14.9 2.9 shard_map.29
  17.8 13.9 %shard_map.30 = (f32[7680,128]{1,0:T(8,128)}, f32[7680,128]{1,0:T(8,128)}, f32[4608,128]{1,0:T(8,128)S(1)}, f32[4608,128]{1,0:T(8,128)S(1)}, f32[4608,128]{1,0:T(8,128)}) custom-call(s32[4]{0:T(128)S(1)} %pad_add_fusion.flags_ref, f32[2,12288,128]{2,1,0:T(8,128)} %bitcast.6, bf16[256,256]{1,0:T(8,128)(2,1)S(1)} %get-tuple-element.16.a_ref, ...), custom_call_target="tpu_custom_call" | custom-call | flops 1000 | bytes 1000 | tf_op jit(solution)/shard_map/pallas_call | solution.py:188
  31.7 0.0 copy-done.2
  31.7 1.5 copy-done
  33.2 1.5 copy-done.1
  34.7 3.6 %collective-permute-start.3 = (f32[4608,128]{1,0:T(8,128)}, f32[4608,128]{1,0:T(8,128)S(1)}, u32[]{:S(2)}, u32[]{:S(2)}) collective-permute-start(f32[4608,128]{1,0:T(8,128)} %get-tuple-element.18), channel_id=1, source_target_pairs={{0,2},{2,4},{4,6},{6,8},{8,10},{10,12},{12,14},{14,16},{16,18},{18... | collective-permute-start | bytes 7077896 | tf_op jit(solution)/shard_map/ppermute | solution.py:452
  38.3 0.8 collective-permute-start.2
  39.1 11.7 %collective-permute-start.5 = (f32[7680,128]{1,0:T(8,128)}, f32[7680,128]{1,0:T(8,128)}, u32[]{:S(2)}, u32[]{:S(2)}) collective-permute-start(f32[7680,128]{1,0:T(8,128)} %get-tuple-element.23.refs_2_), channel_id=1, source_target_pairs={{0,1},{1,2},{2,3},{3,4},{4,5},{5,6},{6,7},{7,8},{8,9},{9,10},{10,1... | collective-permute-start | bytes 11796488 | tf_op jit(solution)/shard_map/ppermute | solution.py:450
  50.8 1.3 collective-permute-start.6
  52.1 36.1 %collective-permute-done.3.refs_1_.refs_2_ = f32[4608,128]{1,0:T(8,128)S(1)} collective-permute-done((f32[4608,128]{1,0:T(8,128)}, f32[4608,128]{1,0:T(8,128)S(1)}, u32[]{:S(2)}, u32[]{:S(2)}) %collective-permute-start.3) | collective-permute-done | bytes 2359328 | tf_op jit(solution)/shard_map/ppermute | solution.py:452
  88.1 0.0 collective-permute-done.2.refs_0_
  88.1 1.4 copy-done.5
  89.5 1.4 copy-done.6
  90.9 1.3 collective-permute-start.4
  92.2 9.8 %collective-permute-start.12 = (f32[4608,128]{1,0:T(8,128)}, f32[4608,128]{1,0:T(8,128)S(1)}, u32[]{:S(2)}, u32[]{:S(2)}) collective-permute-start(f32[4608,128]{1,0:T(8,128)} %get-tuple-element.21.refs_1_.refs_2_), channel_id=1, source_target_pairs={{0,1},{1,2},{2,3},{3,4},{4,5},{5,6},{6,7},{7,8},{8,9},{9,10},{10,1... | collective-permute-start | bytes 7077896 | tf_op jit(solution)/shard_map/ppermute | solution.py:457
  102.0 2.1 collective-permute-start.13
  104.1 85.9 %collective-permute-done.4 = f32[4608,128]{1,0:T(8,128)} collective-permute-done((f32[4608,128]{1,0:T(8,128)}, f32[4608,128]{1,0:T(8,128)}, u32[]{:S(2)}, u32[]{:S(2)}) %collective-permute-start.4) | collective-permute-done | bytes 2359328 | tf_op jit(solution)/shard_map/ppermute | solution.py:455
  190.0 3.3 %broadcast_select_fusion.refs_0_.refs_4_ = f32[4608,128]{1,0:T(8,128)} fusion(f32[4608,128]{1,0:T(8,128)} %collective-permute-done.4, f32[4608,128]{1,0:T(8,128)} %copy-done.5, pred[]{:T(512)S(6)} %or.7), kind=kLoop, calls=%fused_computation | loop fusion | flops 589824 | bytes 7077889 | tf_op jit(solution)/shard_map/jit(_where)/select_n | solution.py:459
  193.3 6.1 %shard_map.33.refs_0_ = f32[128,128]{1,0:T(8,128)} custom-call(s32[4]{0:T(128)} %copy-done.2, f32[4608,128]{1,0:T(8,128)} %broadcast_select_fusion.refs_0_.refs_4_, f32[4608,128]{1,0:T(8,128)} %get-tuple-element.21.refs_1_.refs_2_, f32[4608,128]{1,0:T(8,128)} %get-tuple-element.22.refs_2_.refs_3_), custom_call_target="tpu_custom_call" | custom-call | flops 1000 | bytes 1000 | tf_op jit(solution)/shard_map/pallas_call | solution.py:273
  199.5 69.9 %collective-permute-done.5.refs_1_.refs_0_ = f32[7680,128]{1,0:T(8,128)} collective-permute-done((f32[7680,128]{1,0:T(8,128)}, f32[7680,128]{1,0:T(8,128)}, u32[]{:S(2)}, u32[]{:S(2)}) %collective-permute-start.5) | collective-permute-done | bytes 3932192 | tf_op jit(solution)/shard_map/ppermute | solution.py:450
  269.4 0.0 collective-permute-done.6.refs_1_
  269.4 4.0 %collective-permute-start.7 = (f32[128,128]{1,0:T(8,128)}, f32[128,128]{1,0:T(8,128)S(1)}, u32[]{:S(2)}, u32[]{:S(2)}) collective-permute-start(f32[128,128]{1,0:T(8,128)} %shard_map.35), channel_id=1, source_target_pairs={{0,65},{1,64},{2,67},{3,66},{4,69},{5,68},{6,71},{7,70},{8,73},{9,... | collective-permute-start | bytes 196616 | tf_op jit(solution)/shard_map/ppermute | solution.py:371
  273.4 2.9 collective-permute-done.7
  276.2 0.0 collective-permute-start.8
  276.2 9.3 %shard_map.36 = f32[128,128]{1,0:T(8,128)} custom-call(s32[4]{0:T(128)} %copy-done.2, f32[7680,128]{1,0:T(8,128)} %collective-permute-done.5.refs_1_.refs_0_, f32[7680,128]{1,0:T(8,128)} %collective-permute-done.6.refs_1_, f32[7680,128]{1,0:T(8,128)} %get-tuple-element.23.refs_2_, f32[7680,128]{1,0:T(8,128)} %get-tuple-element.24.refs_3_), custom_call_target="tpu_custom_call" | custom-call | flops 1000 | bytes 1000 | tf_op jit(solution)/shard_map/pallas_call | solution.py:273
  285.5 0.0 collective-permute-done.8
  285.5 0.9 add.15
  286.4 0.0 collective-permute-start.9
  286.4 1.2 collective-permute-done.9
  287.6 0.1 collective-permute-start.10
  287.7 5.2 %collective-permute-done.10 = f32[128,128]{1,0:T(8,128)S(1)} collective-permute-done((f32[128,128]{1,0:T(8,128)S(1)}, f32[128,128]{1,0:T(8,128)S(1)}, u32[]{:S(2)}, u32[]{:S(2)}) %collective-permute-start.10) | collective-permute-done | bytes 65568 | tf_op jit(solution)/shard_map/ppermute | solution.py:371
  292.9 2.6 collective-permute-start.11
  295.5 3.8 %collective-permute-done.11.two_ref = f32[128,128]{1,0:T(8,128)S(1)} collective-permute-done((f32[128,128]{1,0:T(8,128)S(1)}, f32[128,128]{1,0:T(8,128)S(1)}, u32[]{:S(2)}, u32[]{:S(2)}) %collective-permute-start.11) | collective-permute-done | bytes 65568 | tf_op jit(solution)/shard_map/ppermute | solution.py:371
  299.3 0.0 copy-done.3
  299.3 2.7 shard_map.37
  302.0 11.6 %shard_map.38.refs_5_ = f32[2,12288,128]{2,1,0:T(8,128)} custom-call(s32[4]{0:T(128)S(1)} %copy-done.3, bf16[256,256]{1,0:T(8,128)(2,1)S(1)} %get-tuple-element.25.a_ref, bf16[256,256]{1,0:T(8,128)(2,1)S(1)} %get-tuple-element.26.b_ref, f32[7680,128]{1,0:T(8,128)} %collective-permute-done.5.refs_1_.refs_0_, f32[7680,128]{1,0:T(8,128)} %collective-permute-done.6.refs_1_, ...), custom_call_target="tpu_custom_call" | custom-call | flops 1000 | bytes 1000 | tf_op jit(solution)/shard_map/pallas_call | solution.py:344
  313.6 5.1 %collective-permute-done.12.refs_0_ = f32[4608,128]{1,0:T(8,128)S(1)} collective-permute-done((f32[4608,128]{1,0:T(8,128)}, f32[4608,128]{1,0:T(8,128)S(1)}, u32[]{:S(2)}, u32[]{:S(2)}) %collective-permute-start.12) | collective-permute-done | bytes 2359328 | tf_op jit(solution)/shard_map/ppermute | solution.py:457
  318.8 0.0 collective-permute-done.13.refs_1_
  318.8 7.9 %shard_map.39 = f32[2,12288,128]{2,1,0:T(8,128)} custom-call(s32[4]{0:T(128)S(1)} %copy-done.3, bf16[256,256]{1,0:T(8,128)(2,1)S(1)} %get-tuple-element.25.a_ref, bf16[256,256]{1,0:T(8,128)(2,1)S(1)} %get-tuple-element.26.b_ref, f32[4608,128]{1,0:T(8,128)S(1)} %collective-permute-done.12.refs_0_, ...), custom_call_target="tpu_custom_call", output_to_operand_aliasing={{}: (8, {})} | custom-call | flops 1000 | bytes 1000 | tf_op jit(solution)/shard_map/pallas_call | solution.py:344
  (11 shorter events, 0.0 us)
Async XLA Ops:
  0.0 14.9 %copy-start.4 = (s32[2,4]{1,0:T(2,128)S(1)}, s32[2,4]{1,0:T(2,128)}, u32[]{:S(2)}) copy-start(s32[2,4]{1,0:T(2,128)} %offsets_ref.3) | copy-start | bytes 100
  6.8 1.5 collective-permute-start
  9.1 5.8 %collective-permute-start.1 = (f32[128,128]{1,0:T(8,128)S(1)}, f32[128,128]{1,0:T(8,128)S(1)}, u32[]{:S(2)}, u32[]{:S(2)}) collective-permute-start(f32[128,128]{1,0:T(8,128)S(1)} %add.14.one_ref), channel_id=1, source_target_pairs={{0,64},{32,96},{64,0},{96,32},{1,65},{33,97},{65,1},{97,33},{2,66}... | collective-permute-start | bytes 196616 | tf_op jit(solution)/shard_map/ppermute | solution.py:361
  12.5 19.2 %copy-start.2 = (s32[4]{0:T(128)}, s32[4]{0:T(128)S(1)}, u32[]{:S(2)}) copy-start(s32[4]{0:T(128)S(1)} %pad_add_fusion.flags_ref) | copy-start | bytes 52
  31.7 1.5 copy-start
  33.2 1.5 copy-start.1
  34.7 53.4 %collective-permute-start.3 = (f32[4608,128]{1,0:T(8,128)}, f32[4608,128]{1,0:T(8,128)S(1)}, u32[]{:S(2)}, u32[]{:S(2)}) collective-permute-start(f32[4608,128]{1,0:T(8,128)} %get-tuple-element.18), channel_id=1, source_target_pairs={{0,2},{2,4},{4,6},{6,8},{8,10},{10,12},{12,14},{14,16},{16,18},{18... | collective-permute-start | bytes 7077896 | tf_op jit(solution)/shard_map/ppermute | solution.py:452
  38.3 49.8 %collective-permute-start.2 = (f32[4608,128]{1,0:T(8,128)}, f32[4608,128]{1,0:T(8,128)S(1)}, u32[]{:S(2)}, u32[]{:S(2)}) collective-permute-start(f32[4608,128]{1,0:T(8,128)} %get-tuple-element.18), channel_id=1, source_target_pairs={{1,25},{30,6},{33,57},{62,38},{65,89},{94,70},{97,121},{126,102}} | collective-permute-start | bytes 7077896 | tf_op jit(solution)/shard_map/ppermute | solution.py:453
  39.1 230.3 %collective-permute-start.5 = (f32[7680,128]{1,0:T(8,128)}, f32[7680,128]{1,0:T(8,128)}, u32[]{:S(2)}, u32[]{:S(2)}) collective-permute-start(f32[7680,128]{1,0:T(8,128)} %get-tuple-element.23.refs_2_), channel_id=1, source_target_pairs={{0,1},{1,2},{2,3},{3,4},{4,5},{5,6},{6,7},{7,8},{8,9},{9,10},{10,1... | collective-permute-start | bytes 11796488 | tf_op jit(solution)/shard_map/ppermute | solution.py:450
  50.8 218.6 %collective-permute-start.6 = (f32[7680,128]{1,0:T(8,128)}, f32[7680,128]{1,0:T(8,128)}, u32[]{:S(2)}, u32[]{:S(2)}) collective-permute-start(f32[7680,128]{1,0:T(8,128)} %get-tuple-element.24.refs_3_), channel_id=1, source_target_pairs={{1,0},{2,1},{3,2},{4,3},{5,4},{6,5},{7,6},{8,7},{9,8},{10,9},{11,1... | collective-permute-start | bytes 11796488 | tf_op jit(solution)/shard_map/ppermute | solution.py:451
  88.1 1.4 copy-start.5
  89.5 1.4 copy-start.6
  90.9 99.1 %collective-permute-start.4 = (f32[4608,128]{1,0:T(8,128)}, f32[4608,128]{1,0:T(8,128)}, u32[]{:S(2)}, u32[]{:S(2)}) collective-permute-start(f32[4608,128]{1,0:T(8,128)} %shard_map.31), channel_id=1, source_target_pairs={{25,0},{6,31},{57,32},{38,63},{89,64},{70,95},{121,96},{102,127}} | collective-permute-start | bytes 7077896 | tf_op jit(solution)/shard_map/ppermute | solution.py:455
  92.2 226.5 %collective-permute-start.12 = (f32[4608,128]{1,0:T(8,128)}, f32[4608,128]{1,0:T(8,128)S(1)}, u32[]{:S(2)}, u32[]{:S(2)}) collective-permute-start(f32[4608,128]{1,0:T(8,128)} %get-tuple-element.21.refs_1_.refs_2_), channel_id=1, source_target_pairs={{0,1},{1,2},{2,3},{3,4},{4,5},{5,6},{6,7},{7,8},{8,9},{9,10},{10,1... | collective-permute-start | bytes 7077896 | tf_op jit(solution)/shard_map/ppermute | solution.py:457
  102.0 216.7 %collective-permute-start.13 = (f32[4608,128]{1,0:T(8,128)}, f32[4608,128]{1,0:T(8,128)}, u32[]{:S(2)}, u32[]{:S(2)}) collective-permute-start(f32[4608,128]{1,0:T(8,128)} %get-tuple-element.22.refs_2_.refs_3_), channel_id=1, source_target_pairs={{2,1},{3,2},{4,3},{5,4},{6,5},{7,6},{8,7},{9,8},{10,9},{11,10},{12... | collective-permute-start | bytes 7077896 | tf_op jit(solution)/shard_map/ppermute | solution.py:458
  269.4 29.9 %copy-start.3 = (s32[4]{0:T(128)S(1)}, s32[4]{0:T(128)}, u32[]{:S(2)}) copy-start(s32[4]{0:T(128)} %copy-done.2) | copy-start | bytes 52
  269.4 6.8 %collective-permute-start.7 = (f32[128,128]{1,0:T(8,128)}, f32[128,128]{1,0:T(8,128)S(1)}, u32[]{:S(2)}, u32[]{:S(2)}) collective-permute-start(f32[128,128]{1,0:T(8,128)} %shard_map.35), channel_id=1, source_target_pairs={{0,65},{1,64},{2,67},{3,66},{4,69},{5,68},{6,71},{7,70},{8,73},{9,... | collective-permute-start | bytes 196616 | tf_op jit(solution)/shard_map/ppermute | solution.py:371
  276.2 9.3 %collective-permute-start.8 = (f32[128,128]{1,0:T(8,128)S(1)}, f32[128,128]{1,0:T(8,128)S(1)}, u32[]{:S(2)}, u32[]{:S(2)}) collective-permute-start(f32[128,128]{1,0:T(8,128)S(1)} %collective-permute-done.7), channel_id=1, source_target_pairs={{0,2},{1,64},{2,4},{3,1},{4,6},{5,3},{6,8},{7,5},{8,10},{9,7},{10,... | collective-permute-start | bytes 196616 | tf_op jit(solution)/shard_map/ppermute | solution.py:371
  286.4 1.3 collective-permute-start.9
  287.6 5.2 %collective-permute-start.10 = (f32[128,128]{1,0:T(8,128)S(1)}, f32[128,128]{1,0:T(8,128)S(1)}, u32[]{:S(2)}, u32[]{:S(2)}) collective-permute-start(f32[128,128]{1,0:T(8,128)S(1)} %add.16.one_ref), channel_id=1, source_target_pairs={{0,3},{1,6},{2,5},{3,0},{4,7},{5,2},{6,1},{7,4},{8,11},{9,14},{10,... | collective-permute-start | bytes 196616 | tf_op jit(solution)/shard_map/ppermute | solution.py:371
  292.9 6.4 %collective-permute-start.11 = (f32[128,128]{1,0:T(8,128)S(1)}, f32[128,128]{1,0:T(8,128)S(1)}, u32[]{:S(2)}, u32[]{:S(2)}) collective-permute-start(f32[128,128]{1,0:T(8,128)S(1)} %collective-permute-done.10), channel_id=1, source_target_pairs={{0,67},{1,70},{2,69},{3,64},{4,71},{5,66},{6,65},{7,68},{8,75},{9,... | collective-permute-start | bytes 196616 | tf_op jit(solution)/shard_map/ppermute | solution.py:371

commit v8 on v7

--- a/solution.py
+++ b/solution.py
@@ -199,7 +199,7 @@
         ),
         out_shape=out_shape,
         cost_estimate=HINT,
-        compiler_params=params(48),
+        compiler_params=params(52),
     )(flags, x, a, b)
 
 
@@ -352,7 +352,7 @@
         out_shape=jax.ShapeDtypeStruct((2, total, width), F32),
         input_output_aliases=aliases,
         cost_estimate=HINT,
-        compiler_params=params(48),
+        compiler_params=params(52),
     )(flags, a, b, *operands)
 
 

time: 327 us -> 326 us (level)
  no operation moved by 1% of the time
where the time goes in v8:
time: 326 us; the launch traced here: 325 us
  waiting for transfers between devices  212 us (65%)
  Pallas kernels  62.9 us (19%)
  starting transfers between devices  41.9 us (13%)
  other arithmetic  5.24 us (2%)
    ppermute x1, waiting for transfers between devices, body(): ends = lax.ppermute(ends, 'loop', [(by_down, 0), (by_up, last)])  84.5 us
    ppermute x1, waiting for transfers between devices, body(): up0 = lax.ppermute(u0, 'loop', ups)  69.8 us
    ppermute x1, waiting for transfers between devices, body(): got = lax.ppermute(sent, 'loop', skips)  36.1 us
    pallas_call x2, Pallas kernels, second_product(): pl.pallas_call(functools.partial(second_product_kernel, halves, count), g...  20 us
    pallas_call x2, Pallas kernels, gram_call(): pl.pallas_call(functools.partial(packed_gram_kernel, halves), grid_spec=p...  15.4 us
    pallas_call x1, Pallas kernels, first_product(): pl.pallas_call(functools.partial(first_product_kernel, runs), grid_spec=p...  15 us
    ppermute x4, waiting for transfers between devices, everywhere(): return lax.ppermute(x, ('rows', 'loop'), pairs)  11.8 us
    ppermute x1, starting transfers between devices, body(): up0 = lax.ppermute(u0, 'loop', ups)  11.6 us
  transfers between devices with their start and end apart: 14, of which 10 were waited for; matrix products, arithmetic and copies ran while one was open for 1% of the time, Pallas kernels for 9%

profile of v8, /device:TPU:0, one launch (start us, length us, event | category | flops | bytes accessed | tf_op | source)
XLA Modules:
  0.0 325.3 jit_solution(3954174912645241307)
XLA Ops:
  0.0 0.0 copy-start.2
  0.0 6.8 %shard_map.28 = f32[128,128]{1,0:T(8,128)} custom-call(f32[24576,128]{1,0:T(8,128)} %x_ref.1), custom_call_target="tpu_custom_call" | custom-call | flops 1000 | bytes 1000 | tf_op jit(solution)/shard_map/pallas_call | solution.py:80
  6.8 0.0 collective-permute-start
  6.8 1.5 collective-permute-done
  8.2 0.9 add.14.one_ref
  9.1 3.3 %collective-permute-start.1 = (f32[128,128]{1,0:T(8,128)S(1)}, f32[128,128]{1,0:T(8,128)S(1)}, u32[]{:S(2)}, u32[]{:S(2)}) collective-permute-start(f32[128,128]{1,0:T(8,128)S(1)} %add.14.one_ref), channel_id=1, source_target_pairs={{0,64},{32,96},{64,0},{96,32},{1,65},{33,97},{65,1},{97,33},{2,66}... | collective-permute-start | bytes 196616 | tf_op jit(solution)/shard_map/ppermute | solution.py:361
  12.4 0.1 pad_add_fusion.flags_ref
  12.5 2.4 collective-permute-done.1.two_ref
  14.9 0.0 copy-done.2
  14.9 2.9 shard_map.29
  17.8 15.0 %shard_map.30 = (f32[7680,128]{1,0:T(8,128)}, f32[7680,128]{1,0:T(8,128)}, f32[4608,128]{1,0:T(8,128)}, f32[4608,128]{1,0:T(8,128)}, f32[4608,128]{1,0:T(8,128)}) custom-call(s32[4]{0:T(128)S(1)} %pad_add_fusion.flags_ref, f32[2,12288,128]{2,1,0:T(8,128)} %bitcast.6, bf16[256,256]{1,0:T(8,128)(2,1)S(1)} %get-tuple-element.16.a_ref, ...), custom_call_target="tpu_custom_call" | custom-call | flops 1000 | bytes 1000 | tf_op jit(solution)/shard_map/pallas_call | solution.py:188
  32.8 0.0 copy-done
  32.8 3.6 %collective-permute-start.3 = (f32[4608,128]{1,0:T(8,128)}, f32[4608,128]{1,0:T(8,128)S(1)}, u32[]{:S(2)}, u32[]{:S(2)}) collective-permute-start(f32[4608,128]{1,0:T(8,128)} %get-tuple-element.18), channel_id=1, source_target_pairs={{0,2},{2,4},{4,6},{6,8},{8,10},{10,12},{12,14},{14,16},{16,18},{18... | collective-permute-start | bytes 7077896 | tf_op jit(solution)/shard_map/ppermute | solution.py:452
  36.4 0.8 collective-permute-start.2
  37.3 11.6 %collective-permute-start.5 = (f32[7680,128]{1,0:T(8,128)}, f32[7680,128]{1,0:T(8,128)}, u32[]{:S(2)}, u32[]{:S(2)}) collective-permute-start(f32[7680,128]{1,0:T(8,128)} %get-tuple-element.23.refs_2_), channel_id=1, source_target_pairs={{0,1},{1,2},{2,3},{3,4},{4,5},{5,6},{6,7},{7,8},{8,9},{9,10},{10,1... | collective-permute-start | bytes 11796488 | tf_op jit(solution)/shard_map/ppermute | solution.py:450
  48.9 1.3 collective-permute-start.6
  50.2 36.1 %collective-permute-done.3.refs_1_.refs_2_ = f32[4608,128]{1,0:T(8,128)S(1)} collective-permute-done((f32[4608,128]{1,0:T(8,128)}, f32[4608,128]{1,0:T(8,128)S(1)}, u32[]{:S(2)}, u32[]{:S(2)}) %collective-permute-start.3) | collective-permute-done | bytes 2359328 | tf_op jit(solution)/shard_map/ppermute | solution.py:452
  86.3 0.0 collective-permute-done.2.refs_0_
  86.3 1.4 copy-done.3
  87.7 1.4 copy-done.5
  89.1 1.3 collective-permute-start.4
  90.4 0.0 copy-start.4
  90.4 11.2 %collective-permute-start.12 = (f32[4608,128]{1,0:T(8,128)}, f32[4608,128]{1,0:T(8,128)}, u32[]{:S(2)}, u32[]{:S(2)}) collective-permute-start(f32[4608,128]{1,0:T(8,128)} %get-tuple-element.21.refs_1_.refs_2_), channel_id=1, source_target_pairs={{0,1},{1,2},{2,3},{3,4},{4,5},{5,6},{6,7},{7,8},{8,9},{9,10},{10,1... | collective-permute-start | bytes 7077896 | tf_op jit(solution)/shard_map/ppermute | solution.py:457
  101.6 2.0 collective-permute-start.13
  103.6 84.5 %collective-permute-done.4 = f32[4608,128]{1,0:T(8,128)} collective-permute-done((f32[4608,128]{1,0:T(8,128)}, f32[4608,128]{1,0:T(8,128)}, u32[]{:S(2)}, u32[]{:S(2)}) %collective-permute-start.4) | collective-permute-done | bytes 2359328 | tf_op jit(solution)/shard_map/ppermute | solution.py:455
  188.1 0.0 copy-done.4
  188.1 3.5 %broadcast_select_fusion.refs_0_.refs_4_ = f32[4608,128]{1,0:T(8,128)} fusion(f32[4608,128]{1,0:T(8,128)} %collective-permute-done.4, f32[4608,128]{1,0:T(8,128)S(1)} %copy-done.4, pred[]{:T(512)S(6)} %or.7), kind=kLoop, calls=%fused_computation | loop fusion | flops 589824 | bytes 7077889 | tf_op jit(solution)/shard_map/jit(_where)/select_n | solution.py:459
  191.6 6.1 %shard_map.33.refs_0_ = f32[128,128]{1,0:T(8,128)} custom-call(s32[4]{0:T(128)} %copy-done, f32[4608,128]{1,0:T(8,128)} %broadcast_select_fusion.refs_0_.refs_4_, f32[4608,128]{1,0:T(8,128)} %get-tuple-element.21.refs_1_.refs_2_, f32[4608,128]{1,0:T(8,128)} %get-tuple-element.22.refs_2_.refs_3_), custom_call_target="tpu_custom_call" | custom-call | flops 1000 | bytes 1000 | tf_op jit(solution)/shard_map/pallas_call | solution.py:273
  197.7 69.8 %collective-permute-done.5.refs_1_.refs_0_ = f32[7680,128]{1,0:T(8,128)} collective-permute-done((f32[7680,128]{1,0:T(8,128)}, f32[7680,128]{1,0:T(8,128)}, u32[]{:S(2)}, u32[]{:S(2)}) %collective-permute-start.5) | collective-permute-done | bytes 3932192 | tf_op jit(solution)/shard_map/ppermute | solution.py:450
  267.5 0.0 collective-permute-done.6.refs_1_
  267.5 4.0 %collective-permute-start.7 = (f32[128,128]{1,0:T(8,128)}, f32[128,128]{1,0:T(8,128)S(1)}, u32[]{:S(2)}, u32[]{:S(2)}) collective-permute-start(f32[128,128]{1,0:T(8,128)} %shard_map.35), channel_id=1, source_target_pairs={{0,65},{1,64},{2,67},{3,66},{4,69},{5,68},{6,71},{7,70},{8,73},{9,... | collective-permute-start | bytes 196616 | tf_op jit(solution)/shard_map/ppermute | solution.py:371
  271.5 2.8 collective-permute-done.7
  274.3 0.0 collective-permute-start.8
  274.3 9.3 %shard_map.36 = f32[128,128]{1,0:T(8,128)} custom-call(s32[4]{0:T(128)} %copy-done, f32[7680,128]{1,0:T(8,128)} %collective-permute-done.5.refs_1_.refs_0_, f32[7680,128]{1,0:T(8,128)} %collective-permute-done.6.refs_1_, f32[7680,128]{1,0:T(8,128)} %get-tuple-element.23.refs_2_, f32[7680,128]{1,0:T(8,128)} %get-tuple-element.24.refs_3_), custom_call_target="tpu_custom_call" | custom-call | flops 1000 | bytes 1000 | tf_op jit(solution)/shard_map/pallas_call | solution.py:273
  283.6 0.0 collective-permute-done.8
  283.6 0.9 add.15
  284.5 0.0 collective-permute-start.9
  284.5 1.2 collective-permute-done.9
  285.7 0.1 collective-permute-start.10
  285.8 5.2 %collective-permute-done.10 = f32[128,128]{1,0:T(8,128)S(1)} collective-permute-done((f32[128,128]{1,0:T(8,128)S(1)}, f32[128,128]{1,0:T(8,128)S(1)}, u32[]{:S(2)}, u32[]{:S(2)}) %collective-permute-start.10) | collective-permute-done | bytes 65568 | tf_op jit(solution)/shard_map/ppermute | solution.py:371
  291.0 2.6 collective-permute-start.11
  293.6 3.8 %collective-permute-done.11.two_ref = f32[128,128]{1,0:T(8,128)S(1)} collective-permute-done((f32[128,128]{1,0:T(8,128)S(1)}, f32[128,128]{1,0:T(8,128)S(1)}, u32[]{:S(2)}, u32[]{:S(2)}) %collective-permute-start.11) | collective-permute-done | bytes 65568 | tf_op jit(solution)/shard_map/ppermute | solution.py:371
  297.4 0.0 copy-done.1
  297.4 2.7 shard_map.37
  300.1 11.6 %shard_map.38.refs_5_ = f32[2,12288,128]{2,1,0:T(8,128)} custom-call(s32[4]{0:T(128)S(1)} %copy-done.1, bf16[256,256]{1,0:T(8,128)(2,1)S(1)} %get-tuple-element.25.a_ref, bf16[256,256]{1,0:T(8,128)(2,1)S(1)} %get-tuple-element.26.b_ref, f32[7680,128]{1,0:T(8,128)} %collective-permute-done.5.refs_1_.refs_0_, f32[7680,128]{1,0:T(8,128)} %collective-permute-done.6.refs_1_, ...), custom_call_target="tpu_custom_call" | custom-call | flops 1000 | bytes 1000 | tf_op jit(solution)/shard_map/pallas_call | solution.py:344
  311.7 5.2 %collective-permute-done.12.refs_0_ = f32[4608,128]{1,0:T(8,128)} collective-permute-done((f32[4608,128]{1,0:T(8,128)}, f32[4608,128]{1,0:T(8,128)}, u32[]{:S(2)}, u32[]{:S(2)}) %collective-permute-start.12) | collective-permute-done | bytes 2359328 | tf_op jit(solution)/shard_map/ppermute | solution.py:457
  316.9 0.0 collective-permute-done.13.refs_1_
  316.9 8.4 %shard_map.39 = f32[2,12288,128]{2,1,0:T(8,128)} custom-call(s32[4]{0:T(128)S(1)} %copy-done.1, bf16[256,256]{1,0:T(8,128)(2,1)S(1)} %get-tuple-element.25.a_ref, bf16[256,256]{1,0:T(8,128)(2,1)S(1)} %get-tuple-element.26.b_ref, f32[4608,128]{1,0:T(8,128)} %collective-permute-done.12.refs_0_, ...), custom_call_target="tpu_custom_call", output_to_operand_aliasing={{}: (8, {})} | custom-call | flops 1000 | bytes 1000 | tf_op jit(solution)/shard_map/pallas_call | solution.py:344
  (9 shorter events, 0.0 us)
Async XLA Ops:
  0.0 14.9 %copy-start.2 = (s32[2,4]{1,0:T(2,128)S(1)}, s32[2,4]{1,0:T(2,128)}, u32[]{:S(2)}) copy-start(s32[2,4]{1,0:T(2,128)} %offsets_ref.3) | copy-start | bytes 100
  6.8 1.5 collective-permute-start
  9.1 5.8 %collective-permute-start.1 = (f32[128,128]{1,0:T(8,128)S(1)}, f32[128,128]{1,0:T(8,128)S(1)}, u32[]{:S(2)}, u32[]{:S(2)}) collective-permute-start(f32[128,128]{1,0:T(8,128)S(1)} %add.14.one_ref), channel_id=1, source_target_pairs={{0,64},{32,96},{64,0},{96,32},{1,65},{33,97},{65,1},{97,33},{2,66}... | collective-permute-start | bytes 196616 | tf_op jit(solution)/shard_map/ppermute | solution.py:361
  12.5 20.3 %copy-start = (s32[4]{0:T(128)}, s32[4]{0:T(128)S(1)}, u32[]{:S(2)}) copy-start(s32[4]{0:T(128)S(1)} %pad_add_fusion.flags_ref) | copy-start | bytes 52
  32.8 53.5 %collective-permute-start.3 = (f32[4608,128]{1,0:T(8,128)}, f32[4608,128]{1,0:T(8,128)S(1)}, u32[]{:S(2)}, u32[]{:S(2)}) collective-permute-start(f32[4608,128]{1,0:T(8,128)} %get-tuple-element.18), channel_id=1, source_target_pairs={{0,2},{2,4},{4,6},{6,8},{8,10},{10,12},{12,14},{14,16},{16,18},{18... | collective-permute-start | bytes 7077896 | tf_op jit(solution)/shard_map/ppermute | solution.py:452
  36.4 49.8 %collective-permute-start.2 = (f32[4608,128]{1,0:T(8,128)}, f32[4608,128]{1,0:T(8,128)S(1)}, u32[]{:S(2)}, u32[]{:S(2)}) collective-permute-start(f32[4608,128]{1,0:T(8,128)} %get-tuple-element.18), channel_id=1, source_target_pairs={{1,25},{30,6},{33,57},{62,38},{65,89},{94,70},{97,121},{126,102}} | collective-permute-start | bytes 7077896 | tf_op jit(solution)/shard_map/ppermute | solution.py:453
  37.3 230.2 %collective-permute-start.5 = (f32[7680,128]{1,0:T(8,128)}, f32[7680,128]{1,0:T(8,128)}, u32[]{:S(2)}, u32[]{:S(2)}) collective-permute-start(f32[7680,128]{1,0:T(8,128)} %get-tuple-element.23.refs_2_), channel_id=1, source_target_pairs={{0,1},{1,2},{2,3},{3,4},{4,5},{5,6},{6,7},{7,8},{8,9},{9,10},{10,1... | collective-permute-start | bytes 11796488 | tf_op jit(solution)/shard_map/ppermute | solution.py:450
  48.9 218.6 %collective-permute-start.6 = (f32[7680,128]{1,0:T(8,128)}, f32[7680,128]{1,0:T(8,128)}, u32[]{:S(2)}, u32[]{:S(2)}) collective-permute-start(f32[7680,128]{1,0:T(8,128)} %get-tuple-element.24.refs_3_), channel_id=1, source_target_pairs={{1,0},{2,1},{3,2},{4,3},{5,4},{6,5},{7,6},{8,7},{9,8},{10,9},{11,1... | collective-permute-start | bytes 11796488 | tf_op jit(solution)/shard_map/ppermute | solution.py:451
  86.3 1.4 copy-start.3
  87.7 1.4 copy-start.5
  89.1 99.1 %collective-permute-start.4 = (f32[4608,128]{1,0:T(8,128)}, f32[4608,128]{1,0:T(8,128)}, u32[]{:S(2)}, u32[]{:S(2)}) collective-permute-start(f32[4608,128]{1,0:T(8,128)} %shard_map.31), channel_id=1, source_target_pairs={{25,0},{6,31},{57,32},{38,63},{89,64},{70,95},{121,96},{102,127}} | collective-permute-start | bytes 7077896 | tf_op jit(solution)/shard_map/ppermute | solution.py:455
  90.4 97.8 %copy-start.4 = (f32[4608,128]{1,0:T(8,128)S(1)}, f32[4608,128]{1,0:T(8,128)}, u32[]{:S(2)}) copy-start(f32[4608,128]{1,0:T(8,128)} %copy-done.3) | copy-start | bytes 7077892
  90.4 226.5 %collective-permute-start.12 = (f32[4608,128]{1,0:T(8,128)}, f32[4608,128]{1,0:T(8,128)}, u32[]{:S(2)}, u32[]{:S(2)}) collective-permute-start(f32[4608,128]{1,0:T(8,128)} %get-tuple-element.21.refs_1_.refs_2_), channel_id=1, source_target_pairs={{0,1},{1,2},{2,3},{3,4},{4,5},{5,6},{6,7},{7,8},{8,9},{9,10},{10,1... | collective-permute-start | bytes 7077896 | tf_op jit(solution)/shard_map/ppermute | solution.py:457
  101.6 215.3 %collective-permute-start.13 = (f32[4608,128]{1,0:T(8,128)}, f32[4608,128]{1,0:T(8,128)}, u32[]{:S(2)}, u32[]{:S(2)}) collective-permute-start(f32[4608,128]{1,0:T(8,128)} %get-tuple-element.22.refs_2_.refs_3_), channel_id=1, source_target_pairs={{2,1},{3,2},{4,3},{5,4},{6,5},{7,6},{8,7},{9,8},{10,9},{11,10},{12... | collective-permute-start | bytes 7077896 | tf_op jit(solution)/shard_map/ppermute | solution.py:458
  267.5 29.9 %copy-start.1 = (s32[4]{0:T(128)S(1)}, s32[4]{0:T(128)}, u32[]{:S(2)}) copy-start(s32[4]{0:T(128)} %copy-done) | copy-start | bytes 52
  267.5 6.8 %collective-permute-start.7 = (f32[128,128]{1,0:T(8,128)}, f32[128,128]{1,0:T(8,128)S(1)}, u32[]{:S(2)}, u32[]{:S(2)}) collective-permute-start(f32[128,128]{1,0:T(8,128)} %shard_map.35), channel_id=1, source_target_pairs={{0,65},{1,64},{2,67},{3,66},{4,69},{5,68},{6,71},{7,70},{8,73},{9,... | collective-permute-start | bytes 196616 | tf_op jit(solution)/shard_map/ppermute | solution.py:371
  274.3 9.3 %collective-permute-start.8 = (f32[128,128]{1,0:T(8,128)S(1)}, f32[128,128]{1,0:T(8,128)S(1)}, u32[]{:S(2)}, u32[]{:S(2)}) collective-permute-start(f32[128,128]{1,0:T(8,128)S(1)} %collective-permute-done.7), channel_id=1, source_target_pairs={{0,2},{1,64},{2,4},{3,1},{4,6},{5,3},{6,8},{7,5},{8,10},{9,7},{10,... | collective-permute-start | bytes 196616 | tf_op jit(solution)/shard_map/ppermute | solution.py:371
  284.5 1.3 collective-permute-start.9
  285.7 5.2 %collective-permute-start.10 = (f32[128,128]{1,0:T(8,128)S(1)}, f32[128,128]{1,0:T(8,128)S(1)}, u32[]{:S(2)}, u32[]{:S(2)}) collective-permute-start(f32[128,128]{1,0:T(8,128)S(1)} %add.16.one_ref), channel_id=1, source_target_pairs={{0,3},{1,6},{2,5},{3,0},{4,7},{5,2},{6,1},{7,4},{8,11},{9,14},{10,... | collective-permute-start | bytes 196616 | tf_op jit(solution)/shard_map/ppermute | solution.py:371
  291.0 6.4 %collective-permute-start.11 = (f32[128,128]{1,0:T(8,128)S(1)}, f32[128,128]{1,0:T(8,128)S(1)}, u32[]{:S(2)}, u32[]{:S(2)}) collective-permute-start(f32[128,128]{1,0:T(8,128)S(1)} %collective-permute-done.10), channel_id=1, source_target_pairs={{0,67},{1,70},{2,69},{3,64},{4,71},{5,66},{6,65},{7,68},{8,75},{9,... | collective-permute-start | bytes 196616 | tf_op jit(solution)/shard_map/ppermute | solution.py:371

commit v9 on v8

--- a/solution.py
+++ b/solution.py
@@ -416,8 +416,8 @@
 def body(x, offsets):
     rows, width = x.shape
     half_rows = rows // 2
-    block = half_rows // 8
-    late = 5 * block
+    block = half_rows // 6
+    late = 4 * block
     place = lax.axis_index("loop")
     count = lax.axis_size("loop")
     last = count - 1
@@ -445,7 +445,7 @@
     a, b = rotations(0, flags, offsets, gram, row_partner(gram, 2))
 
     u0, w0, u1, w1, sent = first_product(
-        flags, halves, a, b, block, [(0, 5), (5, 3)]
+        flags, halves, a, b, block, [(0, 4), (4, 2)]
     )
     up0 = lax.ppermute(u0, "loop", ups)
     down0 = lax.ppermute(w0, "loop", downs)

time: 326 us -> 323 us (level)
  Pallas kernels: 62.9 us -> 57.4 us
    ppermute x1, waiting for transfers between devices: 69.8 us -> 78.4 us  [body(): up0 = lax.ppermute(u0, 'loop', ups)]
    ppermute x1, waiting for transfers between devices: 36.1 us -> 30.4 us  [body(): got = lax.ppermute(sent, 'loop', skips)]
    ppermute x1, waiting for transfers between devices: 5.17 us -> 0.87 us  [body(): up1 = lax.ppermute(u1, 'loop', ups[:-1])]
    ppermute x1, waiting for transfers between devices: 84.5 us -> 88.7 us  [body(): ends = lax.ppermute(ends, 'loop', [(by_down, 0), (by_up, last)])]
where the time goes in v9:
time: 323 us; the launch traced here: 322 us
  waiting for transfers between devices  215 us (67%)
  Pallas kernels  57.4 us (18%)
  starting transfers between devices  41.6 us (13%)
  other arithmetic  5.06 us (2%)
    ppermute x1, waiting for transfers between devices, body(): ends = lax.ppermute(ends, 'loop', [(by_down, 0), (by_up, last)])  88.7 us
    ppermute x1, waiting for transfers between devices, body(): up0 = lax.ppermute(u0, 'loop', ups)  78.4 us
    ppermute x1, waiting for transfers between devices, body(): got = lax.ppermute(sent, 'loop', skips)  30.4 us
    pallas_call x2, Pallas kernels, second_product(): pl.pallas_call(functools.partial(second_product_kernel, halves, count), g...  17.3 us
    pallas_call x2, Pallas kernels, gram_call(): pl.pallas_call(functools.partial(packed_gram_kernel, halves), grid_spec=p...  14.1 us
    pallas_call x1, Pallas kernels, first_product(): pl.pallas_call(functools.partial(first_product_kernel, runs), grid_spec=p...  13.6 us
    ppermute x4, waiting for transfers between devices, everywhere(): return lax.ppermute(x, ('rows', 'loop'), pairs)  11.8 us
    ppermute x1, starting transfers between devices, body(): up0 = lax.ppermute(u0, 'loop', ups)  11.7 us
  transfers between devices with their start and end apart: 14, of which 10 were waited for; matrix products, arithmetic and copies ran while one was open for 1% of the time, Pallas kernels for 9%

profile of v9, /device:TPU:0, one launch (start us, length us, event | category | flops | bytes accessed | tf_op | source)
XLA Modules:
  0.0 322.1 jit_solution(17755896110953176884)
XLA Ops:
  0.0 0.0 copy-start.2
  0.0 6.8 %shard_map.28 = f32[128,128]{1,0:T(8,128)} custom-call(f32[24576,128]{1,0:T(8,128)} %x_ref.1), custom_call_target="tpu_custom_call" | custom-call | flops 1000 | bytes 1000 | tf_op jit(solution)/shard_map/pallas_call | solution.py:80
  6.8 0.0 collective-permute-start
  6.8 1.5 collective-permute-done
  8.2 0.9 add.14.one_ref
  9.1 3.3 %collective-permute-start.1 = (f32[128,128]{1,0:T(8,128)S(1)}, f32[128,128]{1,0:T(8,128)S(1)}, u32[]{:S(2)}, u32[]{:S(2)}) collective-permute-start(f32[128,128]{1,0:T(8,128)S(1)} %add.14.one_ref), channel_id=1, source_target_pairs={{0,64},{32,96},{64,0},{96,32},{1,65},{33,97},{65,1},{97,33},{2,66}... | collective-permute-start | bytes 196616 | tf_op jit(solution)/shard_map/ppermute | solution.py:361
  12.4 0.1 pad_add_fusion.flags_ref
  12.5 2.4 collective-permute-done.1.two_ref
  14.9 0.0 copy-done.2
  14.9 2.9 shard_map.29
  17.8 13.6 %shard_map.30 = (f32[8192,128]{1,0:T(8,128)}, f32[8192,128]{1,0:T(8,128)}, f32[4096,128]{1,0:T(8,128)}, f32[4096,128]{1,0:T(8,128)}, f32[4096,128]{1,0:T(8,128)}) custom-call(s32[4]{0:T(128)S(1)} %pad_add_fusion.flags_ref, f32[2,12288,128]{2,1,0:T(8,128)} %bitcast.6, bf16[256,256]{1,0:T(8,128)(2,1)S(1)} %get-tuple-element.16.a_ref, ...), custom_call_target="tpu_custom_call" | custom-call | flops 1000 | bytes 1000 | tf_op jit(solution)/shard_map/pallas_call | solution.py:188
  31.4 0.0 copy-done
  31.4 3.6 %collective-permute-start.3 = (f32[4096,128]{1,0:T(8,128)}, f32[4096,128]{1,0:T(8,128)S(1)}, u32[]{:S(2)}, u32[]{:S(2)}) collective-permute-start(f32[4096,128]{1,0:T(8,128)} %get-tuple-element.18), channel_id=1, source_target_pairs={{0,2},{2,4},{4,6},{6,8},{8,10},{10,12},{12,14},{14,16},{16,18},{18... | collective-permute-start | bytes 6291464 | tf_op jit(solution)/shard_map/ppermute | solution.py:452
  35.0 0.8 collective-permute-start.2
  35.8 11.7 %collective-permute-start.5 = (f32[8192,128]{1,0:T(8,128)}, f32[8192,128]{1,0:T(8,128)}, u32[]{:S(2)}, u32[]{:S(2)}) collective-permute-start(f32[8192,128]{1,0:T(8,128)} %get-tuple-element.23.refs_2_), channel_id=1, source_target_pairs={{0,1},{1,2},{2,3},{3,4},{4,5},{5,6},{6,7},{7,8},{8,9},{9,10},{10,1... | collective-permute-start | bytes 12582920 | tf_op jit(solution)/shard_map/ppermute | solution.py:450
  47.5 1.3 collective-permute-start.6
  48.8 30.4 %collective-permute-done.3.refs_1_.refs_2_ = f32[4096,128]{1,0:T(8,128)S(1)} collective-permute-done((f32[4096,128]{1,0:T(8,128)}, f32[4096,128]{1,0:T(8,128)S(1)}, u32[]{:S(2)}, u32[]{:S(2)}) %collective-permute-start.3) | collective-permute-done | bytes 2097184 | tf_op jit(solution)/shard_map/ppermute | solution.py:452
  79.2 0.0 collective-permute-done.2.refs_0_
  79.2 1.3 copy-done.3
  80.5 1.3 copy-done.5
  81.9 1.3 collective-permute-start.4
  83.2 0.0 copy-start.4
  83.2 11.1 %collective-permute-start.12 = (f32[4096,128]{1,0:T(8,128)}, f32[4096,128]{1,0:T(8,128)}, u32[]{:S(2)}, u32[]{:S(2)}) collective-permute-start(f32[4096,128]{1,0:T(8,128)} %get-tuple-element.21.refs_1_.refs_2_), channel_id=1, source_target_pairs={{0,1},{1,2},{2,3},{3,4},{4,5},{5,6},{6,7},{7,8},{8,9},{9,10},{10,1... | collective-permute-start | bytes 6291464 | tf_op jit(solution)/shard_map/ppermute | solution.py:457
  94.2 2.0 collective-permute-start.13
  96.2 88.7 %collective-permute-done.4 = f32[4096,128]{1,0:T(8,128)} collective-permute-done((f32[4096,128]{1,0:T(8,128)}, f32[4096,128]{1,0:T(8,128)}, u32[]{:S(2)}, u32[]{:S(2)}) %collective-permute-start.4) | collective-permute-done | bytes 2097184 | tf_op jit(solution)/shard_map/ppermute | solution.py:455
  184.9 0.0 copy-done.4
  184.9 3.3 %broadcast_select_fusion.refs_0_.refs_4_ = f32[4096,128]{1,0:T(8,128)} fusion(f32[4096,128]{1,0:T(8,128)} %collective-permute-done.4, f32[4096,128]{1,0:T(8,128)S(1)} %copy-done.4, pred[]{:T(512)S(6)} %or.7), kind=kLoop, calls=%fused_computation | loop fusion | flops 524288 | bytes 6291457 | tf_op jit(solution)/shard_map/jit(_where)/select_n | solution.py:459
  188.2 5.2 %shard_map.33.refs_0_ = f32[128,128]{1,0:T(8,128)} custom-call(s32[4]{0:T(128)} %copy-done, f32[4096,128]{1,0:T(8,128)} %broadcast_select_fusion.refs_0_.refs_4_, f32[4096,128]{1,0:T(8,128)} %get-tuple-element.21.refs_1_.refs_2_, f32[4096,128]{1,0:T(8,128)} %get-tuple-element.22.refs_2_.refs_3_), custom_call_target="tpu_custom_call" | custom-call | flops 1000 | bytes 1000 | tf_op jit(solution)/shard_map/pallas_call | solution.py:273
  193.3 78.4 %collective-permute-done.5.refs_1_.refs_0_ = f32[8192,128]{1,0:T(8,128)} collective-permute-done((f32[8192,128]{1,0:T(8,128)}, f32[8192,128]{1,0:T(8,128)}, u32[]{:S(2)}, u32[]{:S(2)}) %collective-permute-start.5) | collective-permute-done | bytes 4194336 | tf_op jit(solution)/shard_map/ppermute | solution.py:450
  271.7 0.0 collective-permute-done.6.refs_1_
  271.7 4.0 %collective-permute-start.7 = (f32[128,128]{1,0:T(8,128)}, f32[128,128]{1,0:T(8,128)S(1)}, u32[]{:S(2)}, u32[]{:S(2)}) collective-permute-start(f32[128,128]{1,0:T(8,128)} %shard_map.35), channel_id=1, source_target_pairs={{0,65},{1,64},{2,67},{3,66},{4,69},{5,68},{6,71},{7,70},{8,73},{9,... | collective-permute-start | bytes 196616 | tf_op jit(solution)/shard_map/ppermute | solution.py:371
  275.7 2.8 collective-permute-done.7
  278.5 0.0 collective-permute-start.8
  278.5 9.0 %shard_map.36 = f32[128,128]{1,0:T(8,128)} custom-call(s32[4]{0:T(128)} %copy-done, f32[8192,128]{1,0:T(8,128)} %collective-permute-done.5.refs_1_.refs_0_, f32[8192,128]{1,0:T(8,128)} %collective-permute-done.6.refs_1_, f32[8192,128]{1,0:T(8,128)} %get-tuple-element.23.refs_2_, f32[8192,128]{1,0:T(8,128)} %get-tuple-element.24.refs_3_), custom_call_target="tpu_custom_call" | custom-call | flops 1000 | bytes 1000 | tf_op jit(solution)/shard_map/pallas_call | solution.py:273
  287.5 0.0 collective-permute-done.8
  287.5 0.9 add.15
  288.3 0.0 collective-permute-start.9
  288.3 1.2 collective-permute-done.9
  289.6 0.1 collective-permute-start.10
  289.7 5.2 %collective-permute-done.10 = f32[128,128]{1,0:T(8,128)S(1)} collective-permute-done((f32[128,128]{1,0:T(8,128)S(1)}, f32[128,128]{1,0:T(8,128)S(1)}, u32[]{:S(2)}, u32[]{:S(2)}) %collective-permute-start.10) | collective-permute-done | bytes 65568 | tf_op jit(solution)/shard_map/ppermute | solution.py:371
  294.8 2.5 collective-permute-start.11
  297.4 3.8 %collective-permute-done.11.two_ref = f32[128,128]{1,0:T(8,128)S(1)} collective-permute-done((f32[128,128]{1,0:T(8,128)S(1)}, f32[128,128]{1,0:T(8,128)S(1)}, u32[]{:S(2)}, u32[]{:S(2)}) %collective-permute-start.11) | collective-permute-done | bytes 65568 | tf_op jit(solution)/shard_map/ppermute | solution.py:371
  301.2 0.0 copy-done.1
  301.2 2.7 shard_map.37
  304.0 10.6 %shard_map.38.refs_5_ = f32[2,12288,128]{2,1,0:T(8,128)} custom-call(s32[4]{0:T(128)S(1)} %copy-done.1, bf16[256,256]{1,0:T(8,128)(2,1)S(1)} %get-tuple-element.25.a_ref, bf16[256,256]{1,0:T(8,128)(2,1)S(1)} %get-tuple-element.26.b_ref, f32[8192,128]{1,0:T(8,128)} %collective-permute-done.5.refs_1_.refs_0_, f32[8192,128]{1,0:T(8,128)} %collective-permute-done.6.refs_1_, ...), custom_call_target="tpu_custom_call" | custom-call | flops 1000 | bytes 1000 | tf_op jit(solution)/shard_map/pallas_call | solution.py:344
  314.6 0.9 collective-permute-done.12.refs_0_
  315.4 0.0 collective-permute-done.13.refs_1_
  315.4 6.7 %shard_map.39 = f32[2,12288,128]{2,1,0:T(8,128)} custom-call(s32[4]{0:T(128)S(1)} %copy-done.1, bf16[256,256]{1,0:T(8,128)(2,1)S(1)} %get-tuple-element.25.a_ref, bf16[256,256]{1,0:T(8,128)(2,1)S(1)} %get-tuple-element.26.b_ref, f32[4096,128]{1,0:T(8,128)} %collective-permute-done.12.refs_0_, ...), custom_call_target="tpu_custom_call", output_to_operand_aliasing={{}: (8, {})} | custom-call | flops 1000 | bytes 1000 | tf_op jit(solution)/shard_map/pallas_call | solution.py:344
  (9 shorter events, 0.0 us)
Async XLA Ops:
  0.0 14.9 %copy-start.2 = (s32[2,4]{1,0:T(2,128)S(1)}, s32[2,4]{1,0:T(2,128)}, u32[]{:S(2)}) copy-start(s32[2,4]{1,0:T(2,128)} %offsets_ref.3) | copy-start | bytes 100
  6.8 1.5 collective-permute-start
  9.1 5.8 %collective-permute-start.1 = (f32[128,128]{1,0:T(8,128)S(1)}, f32[128,128]{1,0:T(8,128)S(1)}, u32[]{:S(2)}, u32[]{:S(2)}) collective-permute-start(f32[128,128]{1,0:T(8,128)S(1)} %add.14.one_ref), channel_id=1, source_target_pairs={{0,64},{32,96},{64,0},{96,32},{1,65},{33,97},{65,1},{97,33},{2,66}... | collective-permute-start | bytes 196616 | tf_op jit(solution)/shard_map/ppermute | solution.py:361
  12.5 18.9 %copy-start = (s32[4]{0:T(128)}, s32[4]{0:T(128)S(1)}, u32[]{:S(2)}) copy-start(s32[4]{0:T(128)S(1)} %pad_add_fusion.flags_ref) | copy-start | bytes 52
  31.4 47.8 %collective-permute-start.3 = (f32[4096,128]{1,0:T(8,128)}, f32[4096,128]{1,0:T(8,128)S(1)}, u32[]{:S(2)}, u32[]{:S(2)}) collective-permute-start(f32[4096,128]{1,0:T(8,128)} %get-tuple-element.18), channel_id=1, source_target_pairs={{0,2},{2,4},{4,6},{6,8},{8,10},{10,12},{12,14},{14,16},{16,18},{18... | collective-permute-start | bytes 6291464 | tf_op jit(solution)/shard_map/ppermute | solution.py:452
  35.0 44.2 %collective-permute-start.2 = (f32[4096,128]{1,0:T(8,128)}, f32[4096,128]{1,0:T(8,128)S(1)}, u32[]{:S(2)}, u32[]{:S(2)}) collective-permute-start(f32[4096,128]{1,0:T(8,128)} %get-tuple-element.18), channel_id=1, source_target_pairs={{1,25},{30,6},{33,57},{62,38},{65,89},{94,70},{97,121},{126,102}} | collective-permute-start | bytes 6291464 | tf_op jit(solution)/shard_map/ppermute | solution.py:453
  35.8 235.9 %collective-permute-start.5 = (f32[8192,128]{1,0:T(8,128)}, f32[8192,128]{1,0:T(8,128)}, u32[]{:S(2)}, u32[]{:S(2)}) collective-permute-start(f32[8192,128]{1,0:T(8,128)} %get-tuple-element.23.refs_2_), channel_id=1, source_target_pairs={{0,1},{1,2},{2,3},{3,4},{4,5},{5,6},{6,7},{7,8},{8,9},{9,10},{10,1... | collective-permute-start | bytes 12582920 | tf_op jit(solution)/shard_map/ppermute | solution.py:450
  47.5 224.2 %collective-permute-start.6 = (f32[8192,128]{1,0:T(8,128)}, f32[8192,128]{1,0:T(8,128)}, u32[]{:S(2)}, u32[]{:S(2)}) collective-permute-start(f32[8192,128]{1,0:T(8,128)} %get-tuple-element.24.refs_3_), channel_id=1, source_target_pairs={{1,0},{2,1},{3,2},{4,3},{5,4},{6,5},{7,6},{8,7},{9,8},{10,9},{11,1... | collective-permute-start | bytes 12582920 | tf_op jit(solution)/shard_map/ppermute | solution.py:451
  79.2 1.3 copy-start.3
  80.5 1.3 copy-start.5
  81.9 103.0 %collective-permute-start.4 = (f32[4096,128]{1,0:T(8,128)}, f32[4096,128]{1,0:T(8,128)}, u32[]{:S(2)}, u32[]{:S(2)}) collective-permute-start(f32[4096,128]{1,0:T(8,128)} %shard_map.31), channel_id=1, source_target_pairs={{25,0},{6,31},{57,32},{38,63},{89,64},{70,95},{121,96},{102,127}} | collective-permute-start | bytes 6291464 | tf_op jit(solution)/shard_map/ppermute | solution.py:455
  83.2 101.7 %copy-start.4 = (f32[4096,128]{1,0:T(8,128)S(1)}, f32[4096,128]{1,0:T(8,128)}, u32[]{:S(2)}) copy-start(f32[4096,128]{1,0:T(8,128)} %copy-done.3) | copy-start | bytes 6291460
  83.2 232.3 %collective-permute-start.12 = (f32[4096,128]{1,0:T(8,128)}, f32[4096,128]{1,0:T(8,128)}, u32[]{:S(2)}, u32[]{:S(2)}) collective-permute-start(f32[4096,128]{1,0:T(8,128)} %get-tuple-element.21.refs_1_.refs_2_), channel_id=1, source_target_pairs={{0,1},{1,2},{2,3},{3,4},{4,5},{5,6},{6,7},{7,8},{8,9},{9,10},{10,1... | collective-permute-start | bytes 6291464 | tf_op jit(solution)/shard_map/ppermute | solution.py:457
  94.2 221.2 %collective-permute-start.13 = (f32[4096,128]{1,0:T(8,128)}, f32[4096,128]{1,0:T(8,128)}, u32[]{:S(2)}, u32[]{:S(2)}) collective-permute-start(f32[4096,128]{1,0:T(8,128)} %get-tuple-element.22.refs_2_.refs_3_), channel_id=1, source_target_pairs={{2,1},{3,2},{4,3},{5,4},{6,5},{7,6},{8,7},{9,8},{10,9},{11,10},{12... | collective-permute-start | bytes 6291464 | tf_op jit(solution)/shard_map/ppermute | solution.py:458
  271.7 29.5 %copy-start.1 = (s32[4]{0:T(128)S(1)}, s32[4]{0:T(128)}, u32[]{:S(2)}) copy-start(s32[4]{0:T(128)} %copy-done) | copy-start | bytes 52
  271.7 6.8 %collective-permute-start.7 = (f32[128,128]{1,0:T(8,128)}, f32[128,128]{1,0:T(8,128)S(1)}, u32[]{:S(2)}, u32[]{:S(2)}) collective-permute-start(f32[128,128]{1,0:T(8,128)} %shard_map.35), channel_id=1, source_target_pairs={{0,65},{1,64},{2,67},{3,66},{4,69},{5,68},{6,71},{7,70},{8,73},{9,... | collective-permute-start | bytes 196616 | tf_op jit(solution)/shard_map/ppermute | solution.py:371
  278.5 9.0 %collective-permute-start.8 = (f32[128,128]{1,0:T(8,128)S(1)}, f32[128,128]{1,0:T(8,128)S(1)}, u32[]{:S(2)}, u32[]{:S(2)}) collective-permute-start(f32[128,128]{1,0:T(8,128)S(1)} %collective-permute-done.7), channel_id=1, source_target_pairs={{0,2},{1,64},{2,4},{3,1},{4,6},{5,3},{6,8},{7,5},{8,10},{9,7},{10,... | collective-permute-start | bytes 196616 | tf_op jit(solution)/shard_map/ppermute | solution.py:371
  288.3 1.3 collective-permute-start.9
  289.6 5.2 %collective-permute-start.10 = (f32[128,128]{1,0:T(8,128)S(1)}, f32[128,128]{1,0:T(8,128)S(1)}, u32[]{:S(2)}, u32[]{:S(2)}) collective-permute-start(f32[128,128]{1,0:T(8,128)S(1)} %add.16.one_ref), channel_id=1, source_target_pairs={{0,3},{1,6},{2,5},{3,0},{4,7},{5,2},{6,1},{7,4},{8,11},{9,14},{10,... | collective-permute-start | bytes 196616 | tf_op jit(solution)/shard_map/ppermute | solution.py:371
  294.8 6.4 %collective-permute-start.11 = (f32[128,128]{1,0:T(8,128)S(1)}, f32[128,128]{1,0:T(8,128)S(1)}, u32[]{:S(2)}, u32[]{:S(2)}) collective-permute-start(f32[128,128]{1,0:T(8,128)S(1)} %collective-permute-done.10), channel_id=1, source_target_pairs={{0,67},{1,70},{2,69},{3,64},{4,71},{5,66},{6,65},{7,68},{8,75},{9,... | collective-permute-start | bytes 196616 | tf_op jit(solution)/shard_map/ppermute | solution.py:371
